TPU v7x, 32 devices: a whole 2x2x4 slice. The times are simulated.
32 devices in a mesh: clip: 2 (over x), tm: 16 (over z, y, core).
Axes of the slice: x: 2, y: 2, z: 4, core: 2. Of those that a mesh axis runs over, the one named last changes fastest.
Arguments:
- tokens: bfloat16 [32768, 512], P(('clip', 'tm')), parts along dimension 0, may hold values from -6 to 6
- qkv_weight: bfloat16 [512, 1536], replicated, may hold values from -0.25 to 0.25
- out_weight: bfloat16 [512, 1024], replicated, may hold values from -0.25 to 0.25
- conv_weight: bfloat16 [3, 3, 256, 256], replicated, may hold values from -0.125 to 0.125
- norm_gain: float32 [256], replicated, may hold values from 0.25 to 1.75
- norm_bias: float32 [256], replicated, may hold values from -3 to 3
- group_map: int32 [32], P('clip'), parts along dimension 0, may hold values from 0 to 7, as said below
- token_order: int32 [2048], P('clip'), parts along dimension 0, may hold values from 0 to 1023, each once
- valid_frames: int32 [32], P('clip'), parts along dimension 0, may hold values from 1 to 16
Outputs:
- decoded: bfloat16 [32, 32, 128, 256], P('clip', 'tm'), parts along dimension 0
There are 2 independent parts, one for each index of `clip`. A program takes and returns all parts, laid end to end along the dimension named above; an argument that names none is the same for every part. Nothing has to cross between parts.
Inputs may be any that keep to these rules, and one draw needn't show every extreme that they name: `group_map`: never falls from one run to the next, and every group from 0 to 7 holds at least one run.
All inputs are finite; a program needn't handle non-finite values.
Results may differ from a plain program's by a relative error of at most 0.0055.
The roundings to bfloat16 on the way count: a program that leaves them out, or rounds other values in their place, can miss the bound.
Values may be sent and summed in bfloat16 or wider, within the bound.
No kernel may reach another device: no remote copies, remote signals or barrier semaphores. Data moves between devices by JAX's collectives and lax.ppermute only.
A program may use at most 64 MiB of HBM per device.

v0:
```python
import jax
import jax.numpy as jnp
from jax import lax
from jax.sharding import PartitionSpec as P

HEADS = 16
NORM_GROUPS = 32


def padded_2(cells, sides, width):
    for axis, dim in sides:
        count = lax.axis_size(axis)
        ends = count - 1
        head = lax.slice_in_dim(cells, 0, width, axis=dim)
        tail = lax.slice_in_dim(cells, cells.shape[dim] - width, cells.shape[dim], axis=dim)
        cells = jnp.concatenate(
            [
                lax.ppermute(tail, axis, [(i, (i + 1) % count) for i in range(ends)]),
                cells,
                lax.ppermute(head, axis, [((i + 1) % count, i) for i in range(ends)]),
            ],
            axis=dim,
        )
    return cells


def group_total(field, group_size):
    return jnp.sum(field, axis=(0, 1, 2)).reshape(NORM_GROUPS, group_size).sum(axis=1)


def local(
    tokens,
    qkv_weight,
    out_weight,
    conv_weight,
    norm_gain,
    norm_bias,
    group_map,
    token_order,
    valid_frames,
):
    tile_count = lax.axis_size("tm")
    device_rank = lax.axis_index("tm")
    token_count, model_width = tokens.shape
    channels = conv_weight.shape[3]
    head_dim = model_width // HEADS
    highest = lax.Precision.HIGHEST
    mixed = jnp.dot(tokens, qkv_weight, preferred_element_type=jnp.float32).astype(jnp.bfloat16)
    query_feats = jax.nn.relu(mixed[:, :model_width]).reshape(token_count, HEADS, head_dim)
    key_feats = jax.nn.relu(mixed[:, model_width : 2 * model_width]).reshape(
        token_count, HEADS, head_dim
    )
    value_rows = mixed[:, 2 * model_width :].reshape(token_count, HEADS, head_dim)
    local_state = jnp.einsum(
        "thk,thv->khv", key_feats, value_rows, preferred_element_type=jnp.float32
    ).reshape(head_dim, model_width)
    local_sum = jnp.sum(key_feats, axis=0, dtype=jnp.float32).reshape(model_width)
    own_group = lax.dynamic_slice_in_dim(group_map, device_rank, 1)
    piece_states = lax.all_gather(local_state[None], "tm", axis=0, tiled=True)
    piece_sums = lax.all_gather(local_sum[None], "tm", axis=0, tiled=True)
    weights = (group_map < own_group).astype(jnp.float32)
    prefix_state = jnp.einsum("c,ckd->kd", weights, piece_states, precision=highest)
    prefix_sum = jnp.dot(weights, piece_sums, precision=highest)
    total_state = (local_state + prefix_state).reshape(head_dim, HEADS, head_dim)
    total_sum = (local_sum + prefix_sum).reshape(HEADS, head_dim)
    query_float = query_feats.astype(jnp.float32)
    numer = jnp.einsum("thk,khv->thv", query_float, total_state, precision=highest)
    denom = jnp.einsum("thk,hk->th", query_float, total_sum, precision=highest) + 1.0
    attended = (numer / denom[:, :, None]).reshape(token_count, model_width).astype(jnp.bfloat16)
    raster = jnp.take(attended, jnp.argsort(token_order), axis=0)
    row_tokens = token_count // tile_count
    mapped = jnp.dot(raster, out_weight, preferred_element_type=jnp.float32).astype(jnp.bfloat16)
    regrouped = mapped.reshape(1, tile_count, row_tokens * 4 * channels)
    tiled = lax.all_to_all(regrouped, "tm", split_axis=1, concat_axis=0, tiled=True)
    shuffled = tiled.reshape(tile_count, 1, row_tokens, 2, 2, channels).transpose(0, 1, 3, 2, 4, 5)
    shuffled = shuffled.reshape(tile_count, 2, 2 * row_tokens, channels)
    own_valid = lax.dynamic_slice_in_dim(valid_frames, device_rank, 1)
    frame_mask = (jnp.arange(tile_count, dtype=jnp.int32) < own_valid)[:, None, None, None]
    shuffled = jnp.where(frame_mask, shuffled, jnp.zeros((), jnp.bfloat16))
    padded = padded_2(shuffled, (("tm", 1),), 1)
    convolved = lax.conv_general_dilated(
        padded,
        conv_weight,
        (1, 1),
        ((0, 0), (1, 1)),
        dimension_numbers=("NHWC", "HWIO", "NHWC"),
        preferred_element_type=jnp.float32,
    )
    convolved = jnp.where(frame_mask, convolved, jnp.zeros((), jnp.float32))
    group_size = channels // NORM_GROUPS
    total_count = jnp.sum(valid_frames).astype(jnp.float32) * (group_size * 4 * row_tokens)
    group_mean = lax.psum(group_total(convolved, group_size), "tm") / total_count
    centred = jnp.where(
        frame_mask, convolved - jnp.repeat(group_mean, group_size), jnp.zeros((), jnp.float32)
    )
    group_var = lax.psum(group_total(centred * centred, group_size), "tm") / total_count
    norm_scale = norm_gain * lax.rsqrt(jnp.repeat(group_var, group_size) + 1e-05)
    normed = centred * norm_scale + norm_bias
    decoded = jnp.where(frame_mask, jax.nn.silu(normed), jnp.zeros((), jnp.float32)).astype(
        jnp.bfloat16
    )
    return decoded


def solution(mesh):
    in_specs = (P(("clip", "tm"), None), P(), P(), P(), P(), P(), P("clip"), P("clip"), P("clip"))
    out_specs = P("clip", "tm", None, None)
    return jax.shard_map(local, mesh=mesh, in_specs=in_specs, out_specs=out_specs, check_vma=False)
```

profile of v0, /device:TPU:0, one launch (start us, length us, event | category | flops | bytes accessed | tf_op | source)
XLA Modules:
  0.0 304.6 jit_solution(946376919256069075)
XLA Ops:
  7.9 3.0 convolution_convert_fusion
  15.9 2.3 copy.31
  22.7 23.2 %all-gather.1 = f32[16,1,512]{2,1,0:T(1,128)S(1)} all-gather(f32[1,1,512]{2,1,0:T(1,128)S(1)} %bitcast.63), channel_id=2, replica_groups=mesh['clip'=2,'tm'=16] {'tm'}, dimensions={0}, use_global_device_ids=true | all-gather | bytes 34816 | tf_op jit(solution)/shard_map/all_gather | solution.py:60
  48.1 4.4 %sort.17 = (s32[1024]{0:T(1024)}, s32[1024]{0:T(1024)S(1)}) sort(s32[1024]{0:T(1024)S(1)} %copy-done.3, s32[1024]{0:T(1024)S(1)} %iota.10), dimensions={0}, to_apply=%region_0.1 | sort | flops 10240 | bytes 16384 | tf_op jit(solution)/shard_map/jit(argsort)/sort | solution.py:70
  53.1 10.3 %all-gather.4.cloned.1.call-done = f32[16,32,512]{2,1,0:T(8,128)} async-done(((f32[1,32,512]{2,1,0:T(8,128)}), f32[16,32,512]{2,1,0:T(8,128)}) %all-gather.4.cloned.1.call-update) | async-done | bytes 1048592 | tf_op jit(solution)/shard_map/all_gather | solution.py:59
  63.4 2.8 fusion.7
  69.8 5.1 %gather_fusion = bf16[1024,512]{1,0:T(8,128)(2,1)} fusion(bf16[1024,512]{1,0:T(8,128)(2,1)S(1)} %copy.34, s32[1024]{0:T(1024)S(1)} %fusion.16), kind=kCustom, calls=%fused_computation | custom fusion | bytes 2101248 | tf_op jit(solution)/shard_map/jit(_take)/gather | solution.py:70
  74.9 4.2 %convolution_convert_fusion.1 = bf16[1024,1024]{1,0:T(8,128)(2,1)} fusion(bf16[512,1024]{1,0:T(8,128)(2,1)} %param.11, bf16[1024,512]{1,0:T(8,128)(2,1)} %gather_fusion, pred[1024]{0:T(1024)(128)(4,1)S(1)} %compare_and_fusion), kind=kOutput, calls=%fused_computation.16 | convolution fusion | flops 1075314688 | bytes 4195328 | tf_op jit(solution)/shard_map/dot_general | solution.py:72
  79.1 10.3 %reshape.91 = bf16[1,16,65536]{2,0,1:T(2,128)(2,1)} reshape(bf16[1024,1024]{1,0:T(8,128)(2,1)} %convolution_convert_fusion.1) | data formatting | bytes 4194304 | tf_op jit(solution)/shard_map/reshape | solution.py:73
  89.9 14.3 %reduce.3 = bf16[16,65536]{1,0:T(8,128)(2,1)} reduce(bf16[16,1,65536]{2,1,0:T(2,128)(2,1)} %bitcast.52, bf16[]{:T(256)} %broadcast.24), dimensions={1}, to_apply=%bitcast.39.reduce_sub_computation | reduce | bytes 4194306
  104.2 4.1 %reshape.93 = bf16[16,2,32768]{2,1,0:T(2,128)(2,1)} reshape(bf16[16,65536]{1,0:T(8,128)(2,1)} %reduce.3) | data formatting | bytes 4194304
  108.2 4.6 %all-to-all-start = ((bf16[16,2,32768]{2,1,0:T(2,128)(2,1)}), bf16[16,2,32768]{2,1,0:T(2,128)(2,1)}, u32[]{:S(2)}, u32[]{:S(2)}) async-start(bf16[16,2,32768]{2,1,0:T(2,128)(2,1)} %reshape.93), calls=%async_computation | async-start | bytes 4194304 | tf_op jit(solution)/shard_map/all_to_all | solution.py:74
  114.1 39.6 %all-to-all-done = bf16[16,2,32768]{2,1,0:T(2,128)(2,1)} async-done(((bf16[16,2,32768]{2,1,0:T(2,128)(2,1)}), bf16[16,2,32768]{2,1,0:T(2,128)(2,1)}, u32[]{:S(2)}, u32[]{:S(2)}) %all-to-all-start) | async-done | bytes 2097184 | tf_op jit(solution)/shard_map/all_to_all | solution.py:74
  153.8 10.4 %reshape.94 = bf16[16,1,65536]{2,1,0:T(2,128)(2,1)} reshape(bf16[16,2,32768]{2,1,0:T(2,128)(2,1)} %all-to-all-done) | data formatting | bytes 4194304
  164.2 14.5 %bitcast_reduce_fusion = bf16[16,65536]{1,0:T(8,128)(2,1)} fusion(bf16[16,1,65536]{2,1,0:T(2,128)(2,1)} %reshape.94), kind=kLoop, calls=%fused_computation.45 | loop fusion | bytes 4194304 | tf_op jit(solution)/shard_map/all_to_all | solution.py:74
  178.7 4.0 %reshape.67 = bf16[16,1,64,2,2,256]{5,4,3,2,0,1:T(2,128)(2,1)} reshape(bf16[16,65536]{1,0:T(8,128)(2,1)} %bitcast_reduce_fusion) | data formatting | bytes 4194304 | tf_op jit(solution)/shard_map/reshape | solution.py:75
  182.7 3.8 %copy.36 = bf16[16,1,2,64,2,256]{5,0,4,3,2,1:T(8,128)(2,1)S(1)} copy(bf16[16,1,2,64,2,256]{5,4,2,3,0,1:T(2,128)(2,1)} %bitcast.53) | data formatting | bytes 4194304 | tf_op jit(solution)/shard_map/transpose | solution.py:75
  189.2 3.7 %collective-permute-start = (bf16[16,1,128,256]{3,0,2,1:T(8,128)(2,1)}, bf16[16,1,128,256]{3,0,2,1:T(8,128)(2,1)}, u32[]{:S(2)}, u32[]{:S(2)}) collective-permute-start(bf16[16,1,128,256]{3,0,2,1:T(8,128)(2,1)} %get-tuple-element.10), channel_id=1, source_target_pairs={{0,1},{1,2},{2,3},{3,4},{4,5},{5,6},{6,7},{7,8},{8,9},{9,10},{10,1... | collective-permute-start | bytes 3145736 | tf_op jit(solution)/shard_map/ppermute | solution.py:18
  195.6 3.2 %collective-permute-done.1 = bf16[16,1,128,256]{3,0,2,1:T(8,128)(2,1)} collective-permute-done((bf16[16,1,128,256]{3,0,2,1:T(8,128)(2,1)S(1)}, bf16[16,1,128,256]{3,0,2,1:T(8,128)(2,1)}, u32[]{:S(2)}, u32[]{:S(2)}) %collective-permute-start.1) | collective-permute-done | bytes 1048608 | tf_op jit(solution)/shard_map/ppermute | solution.py:20
  198.8 8.6 %select_reduce_fusion = (f32[256]{0:T(256)S(1)}, f32[16,2,128,256]{3,0,2,1:T(8,128)}) fusion(pred[16]{0:T(512)(128)(4,1)S(1)} %iota_compare_fusion, bf16[3,3,256,256]{3,2,1,0:T(8,128)(2,1)} %param.12, bf16[16,1,128,256]{3,0,2,1:T(8,128)(2,1)} %collective-permute-done.1, bf16[16,2,128,256]{3,0,2,1:T(8,128)(2,1)} %copy-done.1, ...), kind=kOutput, calls=%fused_computation.10 | convolution fusion | flops 4821352448 | bytes 9569296 | tf_op jit(solution)/shard_map/conv_general_dilated | solution.py:81
  207.6 50.9 %psum.14 = f32[32]{0:T(128)S(1)} all-reduce(f32[32]{0:T(128)S(1)} %reduce_sum.56), channel_id=1, replica_groups=mesh['clip'=2,'tm'=16] {'tm'}, use_global_device_ids=true, to_apply=%region_4.5 | all-reduce | flops 32 | bytes 256 | tf_op jit(solution)/shard_map/psum | solution.py:92
  258.7 3.1 %multiply_reduce_fusion = f32[256]{0:T(256)S(1)} fusion(f32[16,2,128,256]{3,0,2,1:T(8,128)} %get-tuple-element.13, f32[256]{0:T(256)S(1)} %sub.10, pred[16]{0:T(512)(128)(4,1)S(1)} %iota_compare_fusion), kind=kLoop, calls=%fused_computation.8 | loop fusion | flops 5242624 | bytes 4196368 | tf_op jit(solution)/shard_map/reduce_sum | solution.py:28
  262.0 29.7 %psum.15 = f32[32]{0:T(128)S(1)} all-reduce(f32[32]{0:T(128)S(1)} %reduce_sum.59), channel_id=1, replica_groups=mesh['clip'=2,'tm'=16] {'tm'}, use_global_device_ids=true, to_apply=%region_8.9 | all-reduce | flops 32 | bytes 256 | tf_op jit(solution)/shard_map/psum | solution.py:96
  291.9 3.8 %select_convert_fusion = bf16[16,2,128,256]{3,0,2,1:T(8,128)(2,1)S(1)} fusion(f32[16,2,128,256]{3,0,2,1:T(8,128)} %get-tuple-element.13, f32[256]{0:T(256)S(1)} %copy-done.5, f32[256]{0:T(256)S(1)} %mul.23, f32[256]{0:T(256)S(1)} %sub.10, pred[16]{0:T(512)(128)(4,1)S(1)} %iota_compare_fusion), kind=kLoop, calls=%fused_computation.7 | loop fusion | flops 11534336 | bytes 6294544 | tf_op jit(solution)/shard_map/convert_element_type | solution.py:99
  (57 shorter events, 26.4 us)
Async XLA Ops:
  6.5 1.4 copy-start
  6.5 56.9 %all-gather.4.cloned.1.call-start = ((), (), s32[]{:S(2)}) async-start(), calls=%async_computation.1 | async-start | bytes 1114112 | tf_op jit(solution)/shard_map/all_gather | solution.py:59
  11.0 1.7 copy-start.2
  14.4 6.2 %copy-start.4 = (s32[16]{0:T(128)S(1)}, s32[16]{0:T(128)}, u32[]{:S(2)}) copy-start(s32[16]{0:T(128)} %param.15) | copy-start | bytes 196
  15.9 32.2 %copy-start.3 = (s32[1024]{0:T(1024)S(1)}, s32[1024]{0:T(1024)}, u32[]{:S(2)}) copy-start(s32[1024]{0:T(1024)} %param.16) | copy-start | bytes 12292
  104.2 8.7 %copy-start.7 = (s32[16]{0:T(128)S(1)}, s32[16]{0:T(128)}, u32[]{:S(2)}) copy-start(s32[16]{0:T(128)} %param.17) | copy-start | bytes 196
  108.2 45.5 %all-to-all-start = ((bf16[16,2,32768]{2,1,0:T(2,128)(2,1)}), bf16[16,2,32768]{2,1,0:T(2,128)(2,1)}, u32[]{:S(2)}, u32[]{:S(2)}) async-start(bf16[16,2,32768]{2,1,0:T(2,128)(2,1)} %reshape.93), calls=%async_computation | async-start | bytes 4194304 | tf_op jit(solution)/shard_map/all_to_all | solution.py:74
  186.7 1.3 copy-start.1
  189.2 6.4 %collective-permute-start = (bf16[16,1,128,256]{3,0,2,1:T(8,128)(2,1)}, bf16[16,1,128,256]{3,0,2,1:T(8,128)(2,1)}, u32[]{:S(2)}, u32[]{:S(2)}) collective-permute-start(bf16[16,1,128,256]{3,0,2,1:T(8,128)(2,1)} %get-tuple-element.10), channel_id=1, source_target_pairs={{0,1},{1,2},{2,3},{3,4},{4,5},{5,6},{6,7},{7,8},{8,9},{9,10},{10,1... | collective-permute-start | bytes 3145736 | tf_op jit(solution)/shard_map/ppermute | solution.py:18
  192.9 5.9 %collective-permute-start.1 = (bf16[16,1,128,256]{3,0,2,1:T(8,128)(2,1)S(1)}, bf16[16,1,128,256]{3,0,2,1:T(8,128)(2,1)}, u32[]{:S(2)}, u32[]{:S(2)}) collective-permute-start(bf16[16,1,128,256]{3,0,2,1:T(8,128)(2,1)S(1)} %get-tuple-element.11), channel_id=1, source_target_pairs={{1,0},{2,1},{3,2},{4,3},{5,4},{6,5},{7,6},{8,7},{9,8},{10,9},{11,1... | collective-permute-start | bytes 3145736 | tf_op jit(solution)/shard_map/ppermute | solution.py:20
  207.4 84.5 %copy-start.6 = (f32[256]{0:T(256)S(1)}, f32[256]{0:T(256)}, u32[]{:S(2)}) copy-start(f32[256]{0:T(256)} %param.13) | copy-start | bytes 3076
  207.4 84.5 %copy-start.5 = (f32[256]{0:T(256)S(1)}, f32[256]{0:T(256)}, u32[]{:S(2)}) copy-start(f32[256]{0:T(256)} %param.14) | copy-start | bytes 3076
Sparse Core Ops, SparseCore 0:
  20.7 42.6 all-gather.3
where the time goes:
time: 306 us; the launch traced here: 305 us
  blocking collectives  104 us (34%)
  local copies, waits for them, and re-layouts  69.7 us (23%)
  waiting for transfers between devices  53.2 us (17%)
  other arithmetic  30.7 us (10%)
  matrix products  23.4 us (8%)
  between operations  14.3 us (5%)
  starting transfers between devices  9.58 us (3%)
    psum x1, blocking collectives, local(): lax.psum(group_total(convolved, group_size), 'tm') / total_count  50.9 us
    all_to_all x1, waiting for transfers between devices, local(): lax.all_to_all(regrouped, 'tm', split_axis=1, concat_axis=0, tiled=True)  39.6 us
    psum x1, blocking collectives, local(): lax.psum(group_total(centred * centred, group_size), 'tm') / total_count  29.7 us
    all_gather x1, blocking collectives, local(): piece_sums = lax.all_gather(local_sum[None], 'tm', axis=0, tiled=True)  23.2 us
    unnamed x19, local copies, waits for them, and re-layouts  19.4 us
    all_to_all x1, local copies, waits for them, and re-layouts, local(): lax.all_to_all(regrouped, 'tm', split_axis=1, concat_axis=0, tiled=True)  14.5 us
    unnamed x1, other arithmetic  14.3 us
    all_gather x1, waiting for transfers between devices, local(): piece_states = lax.all_gather(local_state[None], 'tm', axis=0, tiled=True)  10.3 us
  transfers between devices with their start and end apart: 4, of which 3 were waited for; matrix products, arithmetic and copies ran while one was open for 4% of the time, Pallas kernels for 0%

commit v1 on v0

v1 whole, which is shorter than its diff:
```python
import functools

import jax
import jax.numpy as jnp
from jax import lax
from jax.experimental import pallas as pl
from jax.experimental.pallas import tpu as pltpu
from jax.sharding import PartitionSpec as P

HEADS = 16
NORM_GROUPS = 32
BF = jnp.bfloat16
F32 = jnp.float32
MIB = 1024 * 1024


def dot(a, b, **kw):
    return jnp.dot(a, b, preferred_element_type=F32, **kw)


def params(mib, dims=1):
    return pltpu.CompilerParams(
        vmem_limit_bytes=mib * MIB, dimension_semantics=("arbitrary",) * dims
    )


def cost(flops, nbytes, trans=0):
    return pl.CostEstimate(flops=int(flops), bytes_accessed=int(nbytes), transcendentals=int(trans))


def same_block(shape, size):
    rows = lax.broadcasted_iota(jnp.int32, shape, 0) // size
    cols = lax.broadcasted_iota(jnp.int32, shape, 1) // size
    return rows == cols


def permute_kernel(order_ref, tok_ref, out_ref):
    rows, count = out_ref.shape[0], tok_ref.shape[0]
    place = lax.broadcasted_iota(jnp.int32, (rows, count), 0) + pl.program_id(0) * rows
    pick = jnp.where(place == order_ref[...], 1.0, 0.0).astype(BF)
    out_ref[...] = dot(pick, tok_ref[...]).astype(BF)


def permute(order, tokens):
    count, width = tokens.shape
    steps = 2
    return pl.pallas_call(
        permute_kernel,
        grid=(steps,),
        in_specs=[
            pl.BlockSpec((1, count), lambda i: (0, 0)),
            pl.BlockSpec((count, width), lambda i: (0, 0)),
        ],
        out_specs=pl.BlockSpec((count // steps, width), lambda i: (i, 0)),
        out_shape=jax.ShapeDtypeStruct((count, width), BF),
        compiler_params=params(32),
        cost_estimate=cost(2 * count * count * width, 4 * count * width),
    )(order.reshape(1, count), tokens)


def state_kernel(head, tok_ref, wk_ref, wv_ref, out_ref, acc_ref, sum_ref):
    step = pl.program_id(0)
    width = tok_ref.shape[1]
    block = acc_ref.shape[1]

    @pl.when(step == 0)
    def _():
        acc_ref[...] = jnp.zeros_like(acc_ref)
        sum_ref[...] = jnp.zeros_like(sum_ref)

    tok = tok_ref[...]
    keys = jnp.maximum(dot(tok, wk_ref[...]), 0.0)
    keys_b = keys.astype(BF)
    vals_b = dot(tok, wv_ref[...]).astype(BF)
    sum_ref[0:1, :] += jnp.sum(keys_b.astype(F32), axis=0, keepdims=True)
    for i in range(width // block):
        cut = slice(i * block, (i + 1) * block)
        acc_ref[i] += lax.dot_general(
            keys_b[:, cut], vals_b[:, cut], (((0,), (0,)), ((), ())), preferred_element_type=F32
        )

    @pl.when(step == pl.num_programs(0) - 1)
    def _():
        own = same_block((block, block), head)
        parts = []
        for i in range(width // block):
            full = jnp.where(own, acc_ref[i], 0.0)
            small = full[:head]
            for h in range(1, block // head):
                small = small + full[h * head : (h + 1) * head]
            parts.append(small)
        total = sum_ref[0:1, :]
        high = total.astype(BF).astype(F32)
        low = total - high
        out_ref[0] = jnp.concatenate(
            [
                jnp.concatenate(parts, axis=1),
                high,
                low,
                jnp.zeros((out_ref.shape[1] - head - 2, width), F32),
            ],
            axis=0,
        ).astype(BF)


def run_state(tokens, qkv_weight, head):
    count, width = tokens.shape
    steps, block = 4, 256
    rows = head + 16
    return pl.pallas_call(
        functools.partial(state_kernel, head),
        grid=(steps,),
        in_specs=[
            pl.BlockSpec((count // steps, width), lambda i: (i, 0)),
            pl.BlockSpec((width, width), lambda i: (0, 1)),
            pl.BlockSpec((width, width), lambda i: (0, 2)),
        ],
        out_specs=pl.BlockSpec((1, rows, width), lambda i: (0, 0, 0)),
        out_shape=jax.ShapeDtypeStruct((1, rows, width), BF),
        scratch_shapes=[
            pltpu.VMEM((width // block, block, block), F32),
            pltpu.VMEM((8, width), F32),
        ],
        compiler_params=params(32),
        cost_estimate=cost(4 * count * width * width, 8 * count * width),
    )(tokens, qkv_weight, qkv_weight)


def queries(tok, wq):
    return jnp.maximum(dot(tok, wq).astype(BF).astype(F32), 0.0)


def attend(qf, state, total, own, ones):
    block = own.shape[0]
    head, width = state.shape
    qb = qf.astype(BF)
    den_in = (qf * total).astype(BF)
    outs = []
    for i in range(width // block):
        cut = slice(i * block, (i + 1) * block)
        wide = jnp.concatenate([state[:, cut]] * (block // head), axis=0)
        wide = jnp.where(own, wide, jnp.zeros_like(wide))
        numer = dot(qb[:, cut], wide)
        denom = dot(den_in[:, cut], ones) + 1.0
        outs.append(numer / denom)
    return jnp.concatenate(outs, axis=1)


def valid_rows(first, limit, frames, rows):
    frame = lax.broadcasted_iota(jnp.int32, (frames * rows, 1), 0) // rows + first
    return frame < limit


def near_kernel(
    order, rows, pos_ref, group_ref, valid_ref,
    buf_ref, own_ref, inner_ref, wq_ref, wo_ref,
    pown_ref, pinner_ref, state_ref, total_ref,
    acc_ref, pend_ref, att_ref,
):
    step = pl.program_id(0)
    width = own_ref.shape[1]
    frames = own_ref.shape[0] // rows
    me = pos_ref[0]
    head = state_ref.shape[1]

    @pl.when(step == 0)
    def _():
        acc_ref[...] = jnp.zeros_like(acc_ref)
        pend_ref[...] = jnp.zeros_like(pend_ref)

    block = 256
    own = same_block((block, block), head)
    ones = jnp.where(own, 1.0, 0.0).astype(BF)
    wq = wq_ref[...]
    q_own = queries(own_ref[...], wq)
    q_inner = queries(inner_ref[...], wq)
    for i in range(frames):
        frame = step * frames + i
        rel = jnp.bitwise_xor(frame, me)
        slot = jnp.int32(0)
        for bit, k in enumerate(order):
            slot = slot + (jnp.bitwise_and(rel, k) // k) * (1 << bit)
        piece = buf_ref[slot].astype(F32)
        before = group_ref[jnp.maximum(frame - 1, 0)]
        fresh = jnp.where(group_ref[frame] != before, 1.0, 0.0)
        pend = pend_ref[...]
        acc = acc_ref[...] + fresh * pend
        acc_ref[...] = acc
        pend_ref[...] = (1.0 - fresh) * pend + piece
        summed = acc + piece
        state = summed[:head].astype(BF)
        total = summed[head : head + 1] + summed[head + 1 : head + 2]
        state_ref[i] = state
        total_ref[i] = jnp.broadcast_to(total, (8, width))
        cut = slice(i * rows, (i + 1) * rows)
        both = jnp.concatenate([q_own[cut], q_inner[cut]], axis=0)
        res = attend(both, state, total, own, ones)
        att_ref[0, cut] = res[:rows]
        att_ref[1, cut] = res[rows:]
    first = step * frames
    keep_own = valid_rows(first, valid_ref[me], frames, rows)
    keep_inner = valid_rows(first, valid_ref[jnp.bitwise_xor(me, 1)], frames, rows)
    half = wo_ref.shape[1] // 2
    wo = wo_ref[...]
    odd = (me % 2) == 1
    p_own = dot(att_ref[0].astype(BF), wo)
    pown_ref[...] = jnp.where(keep_own, p_own, 0.0).astype(BF)
    w_in = jnp.where(odd, wo[:, half:], wo[:, :half])
    p_in = dot(att_ref[1].astype(BF), w_in)
    pinner_ref[...] = jnp.where(keep_inner, p_in, 0.0).astype(BF)


def near(order, rows, me, group_map, valid, buf, own, inner, qkv_weight, out_weight, head):
    count, width = own.shape
    frames = 4
    steps = count // rows // frames
    wide = out_weight.shape[1]
    m = frames * rows
    n, deep, _ = buf.shape
    whole = lambda *shape: pl.BlockSpec(shape, lambda i, *_: (0,) * len(shape))
    return pl.pallas_call(
        functools.partial(near_kernel, order, rows),
        grid_spec=pltpu.PrefetchScalarGridSpec(
            num_scalar_prefetch=3,
            grid=(steps,),
            in_specs=[
                whole(n, deep, width),
                pl.BlockSpec((m, width), lambda i, *_: (i, 0)),
                pl.BlockSpec((m, width), lambda i, *_: (i, 0)),
                pl.BlockSpec((width, width), lambda i, *_: (0, 0)),
                whole(width, wide),
            ],
            out_specs=[
                pl.BlockSpec((m, wide), lambda i, *_: (i, 0)),
                pl.BlockSpec((m, wide // 2), lambda i, *_: (i, 0)),
                pl.BlockSpec((frames, head, width), lambda i, *_: (i, 0, 0)),
                pl.BlockSpec((frames, 8, width), lambda i, *_: (i, 0, 0)),
            ],
            scratch_shapes=[
                pltpu.VMEM((deep, width), F32),
                pltpu.VMEM((deep, width), F32),
                pltpu.VMEM((2, m, width), F32),
            ],
        ),
        out_shape=[
            jax.ShapeDtypeStruct((count, wide), BF),
            jax.ShapeDtypeStruct((count, wide // 2), BF),
            jax.ShapeDtypeStruct((n, head, width), BF),
            jax.ShapeDtypeStruct((n, 8, width), F32),
        ],
        compiler_params=params(40),
        cost_estimate=cost(12 * count * width * width, 16 * count * width),
    )(me, group_map, valid, buf, own, inner, qkv_weight, out_weight)


def conv_kernel(
    rows, pos_ref, valid_ref,
    outer_ref, state_ref, total_ref, pown_ref, pinner_ref, wq_ref, wo_ref, wc_ref,
    conv_ref, stat_ref,
    x_ref, att_ref, run_ref,
):
    step = pl.program_id(0)
    m = outer_ref.shape[0]
    frames = m // rows
    me = pos_ref[0]
    odd = (me % 2) == 1
    channels = conv_ref.shape[3]
    head = state_ref.shape[1]
    block = 256
    own = same_block((block, block), head)
    ones = jnp.where(own, 1.0, 0.0).astype(BF)
    qf = queries(outer_ref[...], wq_ref[...])
    for i in range(frames):
        cut = slice(i * rows, (i + 1) * rows)
        att_ref[cut] = attend(qf[cut], state_ref[i], total_ref[i][0:1], own, ones)
    first = step * frames
    outer_at = jnp.clip(me + jnp.where(odd, 1, -1), 0, valid_ref.shape[0] - 1)
    keep = valid_rows(first, valid_ref[outer_at], frames, rows)
    half = wo_ref.shape[1] // 2
    wo = wo_ref[...]
    w_out = jnp.where(odd, wo[:, :half], wo[:, half:])
    far = jnp.where(keep, dot(att_ref[...].astype(BF), w_out), 0.0)
    close = pinner_ref[...].astype(F32)
    mine = pown_ref[...].astype(F32)
    lines = [
        jnp.where(odd, close, far),
        mine[:, :half],
        mine[:, half:],
        jnp.where(odd, far, close),
    ]
    column = lax.broadcasted_iota(jnp.int32, (m, 1), 0) % rows
    for r, line in enumerate(lines):
        even_px, odd_px = line[:, :channels], line[:, channels:]
        left = jnp.where(column == 0, 0.0, pltpu.roll(odd_px, 1, 0))
        right = jnp.where(column == rows - 1, 0.0, pltpu.roll(even_px, m - 1, 0))
        at = 3 * r * channels
        for b, taps in enumerate(((left, even_px, odd_px), (even_px, odd_px, right))):
            for d, tap in enumerate(taps):
                x_ref[b * m : (b + 1) * m, at + d * channels : at + (d + 1) * channels] = tap.astype(BF)
    deep = wc_ref.shape[0]
    limit = valid_ref[me]
    live = valid_rows(first, limit, frames, rows)
    live2 = jnp.concatenate([live, live], axis=0)
    outs = []
    for y in range(2):
        at = 3 * y * channels
        res = jnp.where(live2, dot(x_ref[:, at : at + deep], wc_ref[...]), 0.0)
        conv_ref[y, 0] = res[:m]
        conv_ref[y, 1] = res[m:]
        outs.append(res)
    part = jnp.sum(outs[0] + outs[1], axis=0, keepdims=True)
    count = (jnp.clip(limit - first, 0, frames) * (4 * rows)).astype(F32)
    mean = part / jnp.maximum(count, 1.0)
    dev = [jnp.where(live2, o - mean, 0.0) for o in outs]
    spread = jnp.sum(dev[0] * dev[0] + dev[1] * dev[1], axis=0, keepdims=True)

    @pl.when(step == 0)
    def _():
        run_ref[...] = jnp.zeros_like(run_ref)

    had = (jnp.clip(limit, 0, first) * (4 * rows)).astype(F32)
    run_sum = run_ref[0:1, :]
    gap = mean - run_sum / jnp.maximum(had, 1.0)
    weight = had * count / jnp.maximum(had + count, 1.0)
    run_ref[1:2, :] += spread + gap * gap * weight
    run_ref[0:1, :] = run_sum + part

    @pl.when(step == pl.num_programs(0) - 1)
    def _():
        stat_ref[...] = jnp.broadcast_to(run_ref[...][None], stat_ref.shape)


def conv(rows, me, valid, outer, state, total, pown, pinner, qkv_weight, out_weight, taps):
    count, width = outer.shape
    channels = taps.shape[1]
    frames = 4
    n = count // rows
    steps = n // frames
    m = frames * rows
    wide = out_weight.shape[1]
    head = state.shape[1]
    whole = lambda *shape: pl.BlockSpec(shape, lambda i, *_: (0,) * len(shape))
    return pl.pallas_call(
        functools.partial(conv_kernel, rows),
        grid_spec=pltpu.PrefetchScalarGridSpec(
            num_scalar_prefetch=2,
            grid=(steps,),
            in_specs=[
                pl.BlockSpec((m, width), lambda i, *_: (i, 0)),
                pl.BlockSpec((frames, head, width), lambda i, *_: (i, 0, 0)),
                pl.BlockSpec((frames, 8, width), lambda i, *_: (i, 0, 0)),
                pl.BlockSpec((m, wide), lambda i, *_: (i, 0)),
                pl.BlockSpec((m, wide // 2), lambda i, *_: (i, 0)),
                pl.BlockSpec((width, width), lambda i, *_: (0, 0)),
                whole(width, wide),
                whole(*taps.shape),
            ],
            out_specs=[
                pl.BlockSpec((2, 2, m, channels), lambda i, *_: (0, 0, i, 0)),
                whole(n, 8, channels),
            ],
            scratch_shapes=[
                pltpu.VMEM((2 * m, 12 * channels), BF),
                pltpu.VMEM((m, width), F32),
                pltpu.VMEM((8, channels), F32),
            ],
        ),
        out_shape=[
            jax.ShapeDtypeStruct((2, 2, count, channels), F32),
            jax.ShapeDtypeStruct((n, 8, channels), F32),
        ],
        compiler_params=params(40),
        cost_estimate=cost(80 * count * channels * channels, 30 * count * channels),
    )(me, valid, outer, state, total, pown, pinner, qkv_weight, out_weight, taps)


def norm_kernel(
    rows, size, pos_ref, valid_ref, stat_ref, count_ref, gain_ref, bias_ref, conv_ref,
    out_ref, mean_ref, scale_ref, mix_ref,
):
    step = pl.program_id(0)
    channels = conv_ref.shape[3]
    m = conv_ref.shape[2]
    frames = m // rows

    @pl.when(step == 0)
    def _():
        stat = stat_ref[...]
        counts = count_ref[...]
        sums, spreads = stat[:, 0, :], stat[:, 1, :]
        mix = jnp.where(same_block((channels, channels), size), 1.0, 0.0)
        all_count = jnp.sum(counts, axis=0, keepdims=True) * size

        def grouped(row):
            wide = jnp.broadcast_to(row, (8, channels))
            return dot(wide, mix, precision=lax.Precision.HIGHEST)[0:1]

        mean = grouped(jnp.sum(sums, axis=0, keepdims=True)) / all_count
        gap = sums / counts - mean
        var = grouped(jnp.sum(spreads + gap * gap * counts, axis=0, keepdims=True)) / all_count
        mean_ref[...] = mean
        scale_ref[...] = gain_ref[...] * lax.rsqrt(var + 1e-5)

    live = valid_rows(step * frames, valid_ref[pos_ref[0]], frames, rows)
    mean, scale, bias = mean_ref[...], scale_ref[...], bias_ref[...]
    for y in range(2):
        for b in range(2):
            z = (conv_ref[y, b] - mean) * scale + bias
            half = 0.5 * z
            z = half + half * jnp.tanh(half)
            z = jnp.where(live, z, 0.0)
            for c in range(channels // 128):
                mix_ref[y, c, pl.ds(b, m, 2), :] = z[:, 128 * c : 128 * (c + 1)]
    for y in range(2):
        for f in range(frames):
            for c in range(channels // 128):
                out_ref[f, y, :, 128 * c : 128 * (c + 1)] = mix_ref[
                    y, c, 2 * rows * f : 2 * rows * (f + 1), :
                ].astype(BF)


def norm(rows, me, valid, stat, counts, gain, bias, planes):
    channels = planes.shape[3]
    n = valid.shape[0]
    frames = 4
    m = frames * rows
    whole = lambda *shape: pl.BlockSpec(shape, lambda i, *_: (0,) * len(shape))
    return pl.pallas_call(
        functools.partial(norm_kernel, rows, channels // NORM_GROUPS),
        grid_spec=pltpu.PrefetchScalarGridSpec(
            num_scalar_prefetch=2,
            grid=(n // frames,),
            in_specs=[
                whole(*stat.shape),
                whole(n, channels),
                whole(1, channels),
                whole(1, channels),
                pl.BlockSpec((2, 2, m, channels), lambda i, *_: (0, 0, i, 0)),
            ],
            out_specs=pl.BlockSpec((frames, 2, 2 * rows, channels), lambda i, *_: (i, 0, 0, 0)),
            scratch_shapes=[
                pltpu.VMEM((1, channels), F32),
                pltpu.VMEM((1, channels), F32),
                pltpu.VMEM((2, channels // 128, 2 * m, 128), F32),
            ],
        ),
        out_shape=jax.ShapeDtypeStruct((n, 2, 2 * rows, channels), BF),
        compiler_params=params(32),
        cost_estimate=cost(8 * planes.size, 6 * planes.size, planes.size),
    )(me, valid, stat, counts, gain.reshape(1, channels), bias.reshape(1, channels), planes)


def local(
    tokens,
    qkv_weight,
    out_weight,
    conv_weight,
    norm_gain,
    norm_bias,
    group_map,
    token_order,
    valid_frames,
):
    tiles = lax.axis_size("tm")
    rank = lax.axis_index("tm")
    count, width = tokens.shape
    rows = count // tiles
    channels = conv_weight.shape[3]
    head = width // HEADS
    me = rank.reshape(1).astype(jnp.int32)

    def swap(x, pairs):
        return lax.ppermute(x, "tm", pairs)

    raster = permute(token_order, tokens)
    tile = lax.all_to_all(
        raster.reshape(tiles, rows, width), "tm", split_axis=0, concat_axis=0, tiled=True
    ).reshape(count, width)
    buf = run_state(tokens, qkv_weight, head)
    order = []
    k = tiles // 2
    while k >= 1:
        order.append(k)
        k //= 2
    for k in order:
        buf = jnp.concatenate([buf, swap(buf, [(i, i ^ k) for i in range(tiles)])], axis=0)
    inner = swap(tile, [(i, i ^ 1) for i in range(tiles)])
    ends = [(i, i + 1) for i in range(1, tiles - 1, 2)]
    outer = swap(tile, ends + [(j, i) for i, j in ends])
    pown, pinner, state, total = near(
        order, rows, me, group_map, valid_frames, buf, tile, inner, qkv_weight, out_weight, head
    )
    planes, stat = conv(
        rows, me, valid_frames, outer, state, total, pown, pinner, qkv_weight, out_weight,
        conv_weight.reshape(-1, channels),
    )
    stat = lax.all_to_all(stat, "tm", split_axis=0, concat_axis=0, tiled=True)
    counts = jnp.broadcast_to(
        (valid_frames * (4 * rows)).astype(F32)[:, None], (tiles, channels)
    )
    return norm(rows, me, valid_frames, stat, counts, norm_gain, norm_bias, planes)


def solution(mesh):
    in_specs = (P(("clip", "tm"), None), P(), P(), P(), P(), P(), P("clip"), P("clip"), P("clip"))
    out_specs = P("clip", "tm", None, None)
    return jax.shard_map(local, mesh=mesh, in_specs=in_specs, out_specs=out_specs, check_vma=False)
```

time: 306 us -> 108 us (0.35)
  blocking collectives: 104 us -> 0 us
  local copies, waits for them, and re-layouts: 69.7 us -> 12.4 us
  other arithmetic: 30.7 us -> 0.84 us
  Pallas kernels: 0 us -> 28.5 us
  matrix products: 23.4 us -> 0 us
  between operations: 14.3 us -> 0.24 us
  starting transfers between devices: 9.58 us -> 17.5 us
  waiting for transfers between devices: 53.2 us -> 47.8 us
    psum x2 -> x0, blocking collectives: 80.6 us -> none  [the longest x1 50.9 us: local(): lax.psum(group_total(convolved, group_size), 'tm') / total_count]
    ppermute x2 -> x6, waiting for transfers between devices: 3.19 us -> 39.8 us  [swap(): return lax.ppermute(x, 'tm', pairs)]
    all_to_all x1 -> x2, waiting for transfers between devices: 39.6 us -> 7.93 us  [the longest x1 7.92 us: local(): stat = lax.all_to_all(stat, 'tm', split_axis=0, concat_axis=0, tiled=True)]
    pallas_call x0 -> x5, Pallas kernels: none -> 28.5 us  [the longest x1 13.1 us: conv(): pl.pallas_call(functools.partial(conv_kernel, rows), grid_spec=pltpu.Pref...]
    all_gather x1 -> x0, blocking collectives: 23.2 us -> none  [local(): piece_sums = lax.all_gather(local_sum[None], 'tm', axis=0, tiled=True)]
    dot_general x7 -> x0, matrix products: 14.8 us -> none  [the longest x1 4.17 us: local(): jnp.dot(raster, out_weight, preferred_element_type=jnp.float32)]
    reshape x5 -> x0, local copies, waits for them, and re-layouts: 14.5 us -> none  [the longest x1 10.3 us: local(): regrouped = mapped.reshape(1, tile_count, row_tokens * 4 * channels)]
    all_to_all x1 -> x0, local copies, waits for them, and re-layouts: 14.5 us -> none  [local(): lax.all_to_all(regrouped, 'tm', split_axis=1, concat_axis=0, tiled=True)]
  transfers between devices with their start and end apart: 4 -> 8, of which waited for: 3 -> 5; matrix products, arithmetic and copies ran while one was open for 4% -> 3% of each run, Pallas kernels for 0% -> 9%
where the time goes in v1:
time: 108 us; the launch traced here: 107 us
  waiting for transfers between devices  47.8 us (44%)
  Pallas kernels  28.5 us (26%)
  starting transfers between devices  17.5 us (16%)
  local copies, waits for them, and re-layouts  12.4 us (11%)
    ppermute x6, waiting for transfers between devices, swap(): return lax.ppermute(x, 'tm', pairs)  39.8 us
    pallas_call x1, Pallas kernels, conv(): pl.pallas_call(functools.partial(conv_kernel, rows), grid_spec=pltpu.Pref...  13.1 us
    unnamed x36, local copies, waits for them, and re-layouts  11.3 us
    all_to_all x1, waiting for transfers between devices, local(): stat = lax.all_to_all(stat, 'tm', split_axis=0, concat_axis=0, tiled=True)  7.92 us
    all_to_all x1, starting transfers between devices, local(): lax.all_to_all(raster.reshape(tiles, rows, width), 'tm', split_axis=0, co...  7.39 us
    pallas_call x1, Pallas kernels, near(): pl.pallas_call(functools.partial(near_kernel, order, rows), grid_spec=plt...  6.67 us
    ppermute x6, starting transfers between devices, swap(): return lax.ppermute(x, 'tm', pairs)  6.19 us
    pallas_call x1, Pallas kernels, norm(): pl.pallas_call(functools.partial(norm_kernel, rows, channels // NORM_GROU...  4.51 us
  transfers between devices with their start and end apart: 8, of which 5 were waited for; matrix products, arithmetic and copies ran while one was open for 3% of the time, Pallas kernels for 9%

profile of v1, /device:TPU:0, one launch (start us, length us, event | category | flops | bytes accessed | tf_op | source)
XLA Modules:
  0.0 107.3 jit_solution(13223558447727922420)
XLA Ops:
  0.0 1.2 %copy-done.4 = bf16[1024,512]{1,0:T(8,128)(2,1)S(1)} copy-done((bf16[1024,512]{1,0:T(8,128)(2,1)S(1)}, bf16[1024,512]{1,0:T(8,128)(2,1)}, u32[]{:S(2)}) %copy-start.4) | copy-done | bytes 1048600
  1.9 1.4 %shard_map.91 = bf16[1024,512]{1,0:T(8,128)(2,1)S(1)} custom-call(s32[1,1024]{1,0:T(1,128)S(1)} %bitcast.14, bf16[1024,512]{1,0:T(8,128)(2,1)S(1)} %copy-done.4), custom_call_target="tpu_custom_call" | custom-call | flops 1073741824 | bytes 2097152 | tf_op jit(solution)/shard_map/pallas_call | solution.py:47
  3.4 1.0 copy-done.3
  4.3 7.4 %all-to-all-start = ((bf16[16,64,512]{2,1,0:T(8,128)(2,1)}), bf16[16,64,512]{2,1,0:T(8,128)(2,1)S(1)}, u32[]{:S(2)}, u32[]{:S(2)}) async-start(bf16[16,64,512]{2,1,0:T(8,128)(2,1)} %bitcast.10), calls=%async_computation | async-start | bytes 2097152 | tf_op jit(solution)/shard_map/all_to_all | solution.py:476
  11.7 1.2 %copy-done.5 = bf16[1024,512]{1,0:T(8,128)(2,1)S(1)} copy-done((bf16[1024,512]{1,0:T(8,128)(2,1)S(1)}, bf16[1024,512]{1,0:T(8,128)(2,1)}, u32[]{:S(2)}) %copy-start.5) | copy-done | bytes 1048600
  13.0 2.8 %shard_map.92 = bf16[1,48,512]{2,1,0:T(8,128)(2,1)S(1)} custom-call(bf16[1024,512]{1,0:T(8,128)(2,1)S(1)} %copy-done.5, bf16[512,1536]{1,0:T(8,128)(2,1)S(1)} %copy-done, bf16[512,1536]{1,0:T(8,128)(2,1)S(1)} %copy-done), custom_call_target="tpu_custom_call" | custom-call | flops 1073741824 | bytes 4194304 | tf_op jit(solution)/shard_map/pallas_call | solution.py:110
  15.8 2.9 %collective-permute-start.1 = (bf16[1,48,512]{2,1,0:T(8,128)(2,1)S(1)}, bf16[1,48,512]{2,1,0:T(8,128)(2,1)S(1)}, u32[]{:S(2)}, u32[]{:S(2)}) collective-permute-start(bf16[1,48,512]{2,1,0:T(8,128)(2,1)S(1)} %shard_map.92), channel_id=1, source_target_pairs={{0,8},{1,9},{2,10},{3,11},{4,12},{5,13},{6,14},{7,15},{8,0},{9,1},... | collective-permute-start | bytes 147464 | tf_op jit(solution)/shard_map/ppermute | solution.py:473
  18.7 21.7 %collective-permute-done.1 = bf16[1,48,512]{2,1,0:T(8,128)(2,1)S(1)} collective-permute-done((bf16[1,48,512]{2,1,0:T(8,128)(2,1)S(1)}, bf16[1,48,512]{2,1,0:T(8,128)(2,1)S(1)}, u32[]{:S(2)}, u32[]{:S(2)}) %collective-permute-start.1) | collective-permute-done | bytes 49184 | tf_op jit(solution)/shard_map/ppermute | solution.py:473
  40.6 4.5 %collective-permute-done.2 = bf16[2,48,512]{2,1,0:T(8,128)(2,1)S(1)} collective-permute-done((bf16[2,48,512]{2,1,0:T(8,128)(2,1)S(1)}, bf16[2,48,512]{2,1,0:T(8,128)(2,1)S(1)}, u32[]{:S(2)}, u32[]{:S(2)}) %collective-permute-start.2) | collective-permute-done | bytes 98336 | tf_op jit(solution)/shard_map/ppermute | solution.py:473
  45.1 1.5 %collective-permute-start.3 = (bf16[4,48,512]{2,1,0:T(8,128)(2,1)S(1)}, bf16[4,48,512]{2,1,0:T(8,128)(2,1)S(1)}, u32[]{:S(2)}, u32[]{:S(2)}) collective-permute-start(bf16[4,48,512]{2,1,0:T(8,128)(2,1)S(1)} %pad_maximum_fusion.1), channel_id=1, source_target_pairs={{0,2},{1,3},{2,0},{3,1},{4,6},{5,7},{6,4},{7,5},{8,10},{9,11},{10,... | collective-permute-start | bytes 589832 | tf_op jit(solution)/shard_map/ppermute | solution.py:473
  46.7 1.6 %collective-permute-start = (bf16[1024,512]{1,0:T(8,128)(2,1)S(1)}, bf16[1024,512]{1,0:T(8,128)(2,1)}, u32[]{:S(2)}, u32[]{:S(2)}) collective-permute-start(bf16[1024,512]{1,0:T(8,128)(2,1)S(1)} %bitcast.8), channel_id=1, source_target_pairs={{1,2},{3,4},{5,6},{7,8},{9,10},{11,12},{13,14},{2,1},{4,3},{6,5},{... | collective-permute-start | bytes 3145736 | tf_op jit(solution)/shard_map/ppermute | solution.py:473
  48.3 13.4 %collective-permute-done.3 = bf16[4,48,512]{2,1,0:T(8,128)(2,1)S(1)} collective-permute-done((bf16[4,48,512]{2,1,0:T(8,128)(2,1)S(1)}, bf16[4,48,512]{2,1,0:T(8,128)(2,1)S(1)}, u32[]{:S(2)}, u32[]{:S(2)}) %collective-permute-start.3) | collective-permute-done | bytes 196640 | tf_op jit(solution)/shard_map/ppermute | solution.py:473
  61.7 0.8 pad_maximum_fusion
  62.5 0.9 constant_dynamic-update-slice_fusion.2
  63.4 0.9 constant_dynamic-update-slice_fusion.1
  64.6 1.0 constant_dynamic-update-slice_fusion.buf_ref
  65.6 1.2 %copy-done.10 = bf16[512,1024]{1,0:T(8,128)(2,1)S(1)} copy-done((bf16[512,1024]{1,0:T(8,128)(2,1)S(1)}, bf16[512,1024]{1,0:T(8,128)(2,1)}, u32[]{:S(2)}) %copy-start.10) | copy-done | bytes 1048600
  66.8 6.7 %shard_map.93 = (bf16[1024,1024]{1,0:T(8,128)(2,1)S(1)}, bf16[1024,512]{1,0:T(8,128)(2,1)S(1)}, bf16[16,32,512]{2,1,0:T(8,128)(2,1)S(1)}, f32[16,8,512]{2,1,0:T(8,128)S(1)}) custom-call(s32[1]{0:T(128)} %bitcast.pos_ref, s32[16]{0:T(128)S(1)} %copy-done.13, s32[16]{0:T(128)S(1)} %copy-done.8, ...), custom_call_target="tpu_custom_call" | custom-call | flops 3221225472 | bytes 8388608 | tf_op jit(solution)/shard_map/pallas_call | solution.py:221
  73.6 13.1 %shard_map.94 = (f32[2,2,1024,256]{3,2,1,0:T(8,128)S(1)}, f32[16,8,256]{2,1,0:T(8,128)}) custom-call(s32[1]{0:T(128)} %bitcast.pos_ref, s32[16]{0:T(128)S(1)} %copy-done.8, bf16[1024,512]{1,0:T(8,128)(2,1)} %collective-permute-done.outer_ref, bf16[16,32,512]{2,1,0:T(8,128)(2,1)S(1)} %get-tuple-element.11.state_ref, ...), custom_call_target="tpu_custom_call" | custom-call | flops 5368709120 | bytes 7864320 | tf_op jit(solution)/shard_map/pallas_call | solution.py:343
  86.7 1.9 %copy-done.1 = f32[2,2,1024,256]{3,2,1,0:T(8,128)} copy-done((f32[2,2,1024,256]{3,2,1,0:T(8,128)}, f32[2,2,1024,256]{3,2,1,0:T(8,128)S(1)}, u32[]{:S(2)}) %copy-start.1) | copy-done | bytes 4194328
  88.7 3.9 %all-to-all-start.1 = ((f32[16,8,256]{2,1,0:T(8,128)}), f32[16,8,256]{2,1,0:T(8,128)S(1)}, u32[]{:S(2)}, u32[]{:S(2)}) async-start(f32[16,8,256]{2,1,0:T(8,128)} %get-tuple-element.15), calls=%async_computation.1 | async-start | bytes 262144 | tf_op jit(solution)/shard_map/all_to_all | solution.py:497
  92.6 7.9 %all-to-all-done.1.stat_ref = f32[16,8,256]{2,1,0:T(8,128)S(1)} async-done(((f32[16,8,256]{2,1,0:T(8,128)}), f32[16,8,256]{2,1,0:T(8,128)S(1)}, u32[]{:S(2)}, u32[]{:S(2)}) %all-to-all-start.1) | async-done | bytes 131104 | tf_op jit(solution)/shard_map/all_to_all | solution.py:497
  100.6 2.2 %copy-done.2 = f32[2,2,1024,256]{3,2,1,0:T(8,128)S(1)} copy-done((f32[2,2,1024,256]{3,2,1,0:T(8,128)S(1)}, f32[2,2,1024,256]{3,2,1,0:T(8,128)}, u32[]{:S(2)}) %copy-start.2) | copy-done | bytes 4194328
  102.8 4.5 %shard_map.95 = bf16[16,2,128,256]{3,2,1,0:T(8,128)(2,1)} custom-call(s32[1]{0:T(128)} %bitcast.pos_ref, s32[16]{0:T(128)S(1)} %copy-done.8, f32[16,8,256]{2,1,0:T(8,128)S(1)} %all-to-all-done.1.stat_ref, f32[16,256]{1,0:T(8,128)S(1)} %broadcast_in_dim.2.count_ref, f32[1,256]{1,0:T(1,128)S(1)} %bitcast.11, f32[1,256]{1,0:T(1,128)S(1)} %bitcast.12, ...), custom_call_target="tpu_custom_call" | custom-call | flops 8388608 | bytes 6291456 | tf_op jit(solution)/shard_map/pallas_call | solution.py:428
  (39 shorter events, 1.2 us)
Async XLA Ops:
  0.0 1.2 %copy-start.4 = (bf16[1024,512]{1,0:T(8,128)(2,1)S(1)}, bf16[1024,512]{1,0:T(8,128)(2,1)}, u32[]{:S(2)}) copy-start(bf16[1024,512]{1,0:T(8,128)(2,1)} %tok_ref.3) | copy-start | bytes 3145732
  1.2 0.7 copy-start.12
  1.9 9.8 %copy-start = (bf16[512,1536]{1,0:T(8,128)(2,1)S(1)}, bf16[512,1536]{1,0:T(8,128)(2,1)}, u32[]{:S(2)}) copy-start(bf16[512,1536]{1,0:T(8,128)(2,1)} %wq_ref.3) | copy-start | bytes 4718596
  3.4 1.0 copy-start.3
  4.3 36.1 %all-to-all-start = ((bf16[16,64,512]{2,1,0:T(8,128)(2,1)}), bf16[16,64,512]{2,1,0:T(8,128)(2,1)S(1)}, u32[]{:S(2)}, u32[]{:S(2)}) async-start(bf16[16,64,512]{2,1,0:T(8,128)(2,1)} %bitcast.10), calls=%async_computation | async-start | bytes 2097152 | tf_op jit(solution)/shard_map/all_to_all | solution.py:476
  11.7 1.2 %copy-start.5 = (bf16[1024,512]{1,0:T(8,128)(2,1)S(1)}, bf16[1024,512]{1,0:T(8,128)(2,1)}, u32[]{:S(2)}) copy-start(bf16[1024,512]{1,0:T(8,128)(2,1)} %tok_ref.3) | copy-start | bytes 3145732
  15.7 49.9 %copy-start.8 = (s32[16]{0:T(128)S(1)}, s32[16]{0:T(128)}, u32[]{:S(2)}) copy-start(s32[16]{0:T(128)} %valid_ref.5) | copy-start | bytes 196
  15.8 49.8 %copy-start.13 = (s32[16]{0:T(128)S(1)}, s32[16]{0:T(128)}, u32[]{:S(2)}) copy-start(s32[16]{0:T(128)} %group_ref.1) | copy-start | bytes 196
  15.8 24.6 %collective-permute-start.1 = (bf16[1,48,512]{2,1,0:T(8,128)(2,1)S(1)}, bf16[1,48,512]{2,1,0:T(8,128)(2,1)S(1)}, u32[]{:S(2)}, u32[]{:S(2)}) collective-permute-start(bf16[1,48,512]{2,1,0:T(8,128)(2,1)S(1)} %shard_map.92), channel_id=1, source_target_pairs={{0,8},{1,9},{2,10},{3,11},{4,12},{5,13},{6,14},{7,15},{8,0},{9,1},... | collective-permute-start | bytes 147464 | tf_op jit(solution)/shard_map/ppermute | solution.py:473
  40.4 4.7 %collective-permute-start.2 = (bf16[2,48,512]{2,1,0:T(8,128)(2,1)S(1)}, bf16[2,48,512]{2,1,0:T(8,128)(2,1)S(1)}, u32[]{:S(2)}, u32[]{:S(2)}) collective-permute-start(bf16[2,48,512]{2,1,0:T(8,128)(2,1)S(1)} %pad_maximum_fusion.2), channel_id=1, source_target_pairs={{0,4},{1,5},{2,6},{3,7},{4,0},{5,1},{6,2},{7,3},{8,12},{9,13},{10,... | collective-permute-start | bytes 294920 | tf_op jit(solution)/shard_map/ppermute | solution.py:473
  40.5 25.1 %collective-permute-start.5 = (bf16[1024,512]{1,0:T(8,128)(2,1)S(1)}, bf16[1024,512]{1,0:T(8,128)(2,1)}, u32[]{:S(2)}, u32[]{:S(2)}) collective-permute-start(bf16[1024,512]{1,0:T(8,128)(2,1)S(1)} %bitcast.7), channel_id=1, source_target_pairs={{0,1},{1,0},{2,3},{3,2},{4,5},{5,4},{6,7},{7,6},{8,9},{9,8},{10,11... | collective-permute-start | bytes 3145736 | tf_op jit(solution)/shard_map/ppermute | solution.py:473
  45.1 17.4 %copy-start.14 = (bf16[2,48,512]{2,1,0:T(8,128)(2,1)}, bf16[2,48,512]{2,1,0:T(8,128)(2,1)S(1)}, u32[]{:S(2)}) copy-start(bf16[2,48,512]{2,1,0:T(8,128)(2,1)S(1)} %collective-permute-done.2) | copy-start | bytes 294916
  45.1 16.6 %collective-permute-start.3 = (bf16[4,48,512]{2,1,0:T(8,128)(2,1)S(1)}, bf16[4,48,512]{2,1,0:T(8,128)(2,1)S(1)}, u32[]{:S(2)}, u32[]{:S(2)}) collective-permute-start(bf16[4,48,512]{2,1,0:T(8,128)(2,1)S(1)} %pad_maximum_fusion.1), channel_id=1, source_target_pairs={{0,2},{1,3},{2,0},{3,1},{4,6},{5,7},{6,4},{7,5},{8,10},{9,11},{10,... | collective-permute-start | bytes 589832 | tf_op jit(solution)/shard_map/ppermute | solution.py:473
  46.7 26.9 %collective-permute-start = (bf16[1024,512]{1,0:T(8,128)(2,1)S(1)}, bf16[1024,512]{1,0:T(8,128)(2,1)}, u32[]{:S(2)}, u32[]{:S(2)}) collective-permute-start(bf16[1024,512]{1,0:T(8,128)(2,1)S(1)} %bitcast.8), channel_id=1, source_target_pairs={{1,2},{3,4},{5,6},{7,8},{9,10},{11,12},{13,14},{2,1},{4,3},{6,5},{... | collective-permute-start | bytes 3145736 | tf_op jit(solution)/shard_map/ppermute | solution.py:473
  61.7 0.8 copy-start.15
  62.5 2.1 %collective-permute-start.4 = (bf16[8,48,512]{2,1,0:T(8,128)(2,1)}, bf16[8,48,512]{2,1,0:T(8,128)(2,1)}, u32[]{:S(2)}, u32[]{:S(2)}) collective-permute-start(bf16[8,48,512]{2,1,0:T(8,128)(2,1)} %pad_maximum_fusion), channel_id=1, source_target_pairs={{0,1},{1,0},{2,3},{3,2},{4,5},{5,4},{6,7},{7,6},{8,9},{9,8},{10,11... | collective-permute-start | bytes 1179656 | tf_op jit(solution)/shard_map/ppermute | solution.py:473
  65.6 1.2 %copy-start.10 = (bf16[512,1024]{1,0:T(8,128)(2,1)S(1)}, bf16[512,1024]{1,0:T(8,128)(2,1)}, u32[]{:S(2)}) copy-start(bf16[512,1024]{1,0:T(8,128)(2,1)} %wo_ref.3) | copy-start | bytes 3145732
  66.8 6.7 %copy-start.9 = (bf16[3,3,256,256]{3,2,1,0:T(8,128)(2,1)S(1)}, bf16[3,3,256,256]{3,2,1,0:T(8,128)(2,1)}, u32[]{:S(2)}) copy-start(bf16[3,3,256,256]{3,2,1,0:T(8,128)(2,1)} %param.12) | copy-start | bytes 3538948
  66.8 6.7 %copy-start.11 = (bf16[512,1024]{1,0:T(8,128)(2,1)S(1)}, bf16[512,1024]{1,0:T(8,128)(2,1)}, u32[]{:S(2)}) copy-start(bf16[512,1024]{1,0:T(8,128)(2,1)} %wo_ref.3) | copy-start | bytes 3145732
  73.6 27.0 %copy-start.6 = (f32[256]{0:T(256)S(1)}, f32[256]{0:T(256)}, u32[]{:S(2)}) copy-start(f32[256]{0:T(256)} %param.13) | copy-start | bytes 3076
  73.6 27.0 %copy-start.7 = (f32[256]{0:T(256)S(1)}, f32[256]{0:T(256)}, u32[]{:S(2)}) copy-start(f32[256]{0:T(256)} %param.14) | copy-start | bytes 3076
  86.7 1.9 %copy-start.1 = (f32[2,2,1024,256]{3,2,1,0:T(8,128)}, f32[2,2,1024,256]{3,2,1,0:T(8,128)S(1)}, u32[]{:S(2)}) copy-start(f32[2,2,1024,256]{3,2,1,0:T(8,128)S(1)} %get-tuple-element.16.conv_ref) | copy-start | bytes 12582916
  88.7 11.8 %all-to-all-start.1 = ((f32[16,8,256]{2,1,0:T(8,128)}), f32[16,8,256]{2,1,0:T(8,128)S(1)}, u32[]{:S(2)}, u32[]{:S(2)}) async-start(f32[16,8,256]{2,1,0:T(8,128)} %get-tuple-element.15), calls=%async_computation.1 | async-start | bytes 262144 | tf_op jit(solution)/shard_map/all_to_all | solution.py:497
  100.6 2.2 %copy-start.2 = (f32[2,2,1024,256]{3,2,1,0:T(8,128)S(1)}, f32[2,2,1024,256]{3,2,1,0:T(8,128)}, u32[]{:S(2)}) copy-start(f32[2,2,1024,256]{3,2,1,0:T(8,128)} %copy-done.1) | copy-start | bytes 12582916

commit v2 on v1

v2 whole, which is shorter than its diff:
```python
import functools

import jax
import jax.numpy as jnp
from jax import lax
from jax.experimental import pallas as pl
from jax.experimental.pallas import tpu as pltpu
from jax.sharding import PartitionSpec as P

HEADS = 16
NORM_GROUPS = 32
BF = jnp.bfloat16
F32 = jnp.float32
MIB = 1024 * 1024
VMEM = 60


def dot(a, b, **kw):
    return jnp.dot(a, b, preferred_element_type=F32, **kw)


def params(mib, dims=1):
    return pltpu.CompilerParams(
        vmem_limit_bytes=mib * MIB, dimension_semantics=("arbitrary",) * dims
    )


def cost(flops, nbytes, trans=0):
    return pl.CostEstimate(flops=int(flops), bytes_accessed=int(nbytes), transcendentals=int(trans))


def same_block(shape, size):
    rows = lax.broadcasted_iota(jnp.int32, shape, 0) // size
    cols = lax.broadcasted_iota(jnp.int32, shape, 1) // size
    return rows == cols


def permute_kernel(order_ref, tok_ref, out_ref, pick_ref):
    count = tok_ref.shape[0]

    @pl.when(pl.program_id(0) == 0)
    def _():
        place = lax.broadcasted_iota(jnp.int32, (count, count), 0)
        pick_ref[...] = jnp.where(place == order_ref[...], 1.0, 0.0).astype(BF)

    out_ref[...] = dot(pick_ref[...], tok_ref[...]).astype(BF)


def permute(order, tokens):
    count, width = tokens.shape
    block = 256
    return pl.pallas_call(
        permute_kernel,
        grid=(width // block,),
        in_specs=[
            pl.BlockSpec((1, count), lambda i: (0, 0)),
            pl.BlockSpec((count, block), lambda i: (0, i)),
        ],
        out_specs=pl.BlockSpec((count, block), lambda i: (0, i)),
        out_shape=jax.ShapeDtypeStruct((count, width), BF),
        scratch_shapes=[pltpu.VMEM((count, count), BF)],
        compiler_params=params(VMEM),
        cost_estimate=cost(2 * count * count * width, 4 * count * width),
    )(order.reshape(1, count), tokens)


def state_kernel(head, tok_ref, wk_ref, wv_ref, out_ref, acc_ref, sum_ref):
    step = pl.program_id(0)
    width = tok_ref.shape[1]
    block = acc_ref.shape[1]

    @pl.when(step == 0)
    def _():
        acc_ref[...] = jnp.zeros_like(acc_ref)
        sum_ref[...] = jnp.zeros_like(sum_ref)

    tok = tok_ref[...]
    keys = jnp.maximum(dot(tok, wk_ref[...]), 0.0)
    keys_b = keys.astype(BF)
    vals_b = dot(tok, wv_ref[...]).astype(BF)
    sum_ref[0:1, :] += jnp.sum(keys_b.astype(F32), axis=0, keepdims=True)
    for i in range(width // block):
        cut = slice(i * block, (i + 1) * block)
        acc_ref[i] += lax.dot_general(
            keys_b[:, cut], vals_b[:, cut], (((0,), (0,)), ((), ())), preferred_element_type=F32
        )

    @pl.when(step == pl.num_programs(0) - 1)
    def _():
        own = same_block((block, block), head)
        parts = []
        for i in range(width // block):
            full = jnp.where(own, acc_ref[i], 0.0)
            small = full[:head]
            for h in range(1, block // head):
                small = small + full[h * head : (h + 1) * head]
            parts.append(small)
        total = sum_ref[0:1, :]
        high = total.astype(BF).astype(F32)
        low = total - high
        out_ref[0] = jnp.concatenate(
            [
                jnp.concatenate(parts, axis=1),
                high,
                low,
                jnp.zeros((out_ref.shape[1] - head - 2, width), F32),
            ],
            axis=0,
        ).astype(BF)


def run_state(tokens, qkv_weight, head):
    count, width = tokens.shape
    steps, block = 4, 256
    rows = head + 16
    return pl.pallas_call(
        functools.partial(state_kernel, head),
        grid=(steps,),
        in_specs=[
            pl.BlockSpec((count // steps, width), lambda i: (i, 0)),
            pl.BlockSpec((width, width), lambda i: (0, 1)),
            pl.BlockSpec((width, width), lambda i: (0, 2)),
        ],
        out_specs=pl.BlockSpec((1, rows, width), lambda i: (0, 0, 0)),
        out_shape=jax.ShapeDtypeStruct((1, rows, width), BF),
        scratch_shapes=[
            pltpu.VMEM((width // block, block, block), F32),
            pltpu.VMEM((8, width), F32),
        ],
        compiler_params=params(VMEM),
        cost_estimate=cost(4 * count * width * width, 8 * count * width),
    )(tokens, qkv_weight, qkv_weight)


def queries(tok, wq):
    return jnp.maximum(dot(tok, wq).astype(BF).astype(F32), 0.0)


def attend(qf, state, total, own, ones):
    block = own.shape[0]
    head, width = state.shape
    qb = qf.astype(BF)
    den_in = (qf * total).astype(BF)
    outs = []
    for i in range(width // block):
        cut = slice(i * block, (i + 1) * block)
        wide = jnp.concatenate([state[:, cut]] * (block // head), axis=0)
        wide = jnp.where(own, wide, jnp.zeros_like(wide))
        numer = dot(qb[:, cut], wide)
        denom = dot(den_in[:, cut], ones) + 1.0
        outs.append(numer / denom)
    return jnp.concatenate(outs, axis=1)


def valid_rows(first, limit, frames, rows):
    frame = lax.broadcasted_iota(jnp.int32, (frames * rows, 1), 0) // rows + first
    return frame < limit


HBM = pl.BlockSpec(memory_space=pltpu.HBM)
ANY = pl.BlockSpec(memory_space=pl.ANY)
INSIDE = pl.BlockSpec(memory_space=pltpu.VMEM)


def chunk(src, dst, step, m, sem):
    at = pl.ds(pl.multiple_of(step * m, m), m)
    return pltpu.make_async_copy(src.at[at], dst.at[at], sem.at[step])


def spread_row(src, row, dst, sems):
    deep, channels = dst.shape[0] * 3 // 4, dst.shape[1] // 2
    part = src.at[pl.ds(pl.multiple_of(row * deep, deep), deep), :]
    return [
        pltpu.make_async_copy(part, dst.at[:deep, :channels], sems.at[0]),
        pltpu.make_async_copy(part, dst.at[channels:, channels:], sems.at[1]),
    ]


def clear_spread(dst):
    channels = dst.shape[1] // 2
    gap = jnp.zeros((channels, channels), BF)
    dst[3 * channels :, :channels] = gap
    dst[:channels, channels:] = gap


def store_taps(x_ref, at, line, rows):
    m, channels = line.shape[0], line.shape[1] // 2
    column = lax.broadcasted_iota(jnp.int32, (m, 1), 0) % rows
    even_px, odd_px = line[:, :channels], line[:, channels:]
    left = jnp.where(column == 0, 0.0, pltpu.roll(odd_px, 1, 0))
    right = jnp.where(column == rows - 1, 0.0, pltpu.roll(even_px, m - 1, 0))
    for b, taps in enumerate(((left, even_px, odd_px), (even_px, odd_px, right))):
        for d, tap in enumerate(taps):
            cut = slice(at + d * channels, at + (d + 1) * channels)
            x_ref[b * m : (b + 1) * m, cut] = tap.astype(BF)


def line_taps(line, rows):
    m, channels = line.shape[0], line.shape[1] // 2
    column = lax.broadcasted_iota(jnp.int32, (m, 1), 0) % rows
    even_px, odd_px = line[:, :channels], line[:, channels:]
    left = jnp.where(column == 0, 0.0, pltpu.roll(odd_px, 1, 0))
    right = jnp.where(column == rows - 1, 0.0, pltpu.roll(even_px, m - 1, 0))
    return jnp.concatenate([left.astype(BF), line.astype(BF), right.astype(BF)], axis=1)


def gather_stats(run_ref, res, live, limit, first, frames, rows):
    @pl.when(first == 0)
    def _():
        run_ref[...] = jnp.zeros_like(run_ref)

    part = jnp.sum(res, axis=0, keepdims=True)
    count = (jnp.clip(limit - first, 0, frames) * (2 * rows)).astype(F32)
    mean = part / jnp.maximum(count, 1.0)
    dev = jnp.where(live, res - mean, 0.0)
    spread = jnp.sum(dev * dev, axis=0, keepdims=True)
    had = (jnp.clip(limit, 0, first) * (2 * rows)).astype(F32)
    run_sum = run_ref[0:1, :]
    gap = mean - run_sum / jnp.maximum(had, 1.0)
    weight = had * count / jnp.maximum(had + count, 1.0)
    run_ref[1:2, :] += spread + gap * gap * weight
    run_ref[0:1, :] = run_sum + part


def near_kernel(
    rows, pos_ref, group_ref, valid_ref,
    buf0_ref, buf1_ref, own_any, inner_any, qkv_hbm, wo_hbm, taps_hbm,
    near_ref, part_ref, state_ref, total_ref, stat_ref,
    acc_ref, pend_ref, att_ref, x_ref, w2_ref, w1_ref, wq_ref, wo_ref, own_ref, inner_ref,
    own_sem, inner_sem, sems,
):
    step = pl.program_id(0)
    count, width = own_ref.shape
    m = near_ref.shape[1]
    frames = m // rows
    steps = count // m
    me = pos_ref[0]
    odd = jnp.bitwise_and(me, 1)
    head = state_ref.shape[1]
    channels = near_ref.shape[2]
    row = 3 * channels
    first_half = taps_hbm.at[pl.ds(pl.multiple_of(odd * row, row), 2 * row), :]
    second_half = taps_hbm.at[pl.ds(pl.multiple_of((1 - odd) * row, row), 2 * row), :]
    query_copy = pltpu.make_async_copy(qkv_hbm.at[:, pl.ds(0, width)], wq_ref, sems.at[0])
    late = [
        pltpu.make_async_copy(wo_hbm, wo_ref, sems.at[1]),
        pltpu.make_async_copy(first_half, w2_ref.at[:, :channels], sems.at[2]),
        pltpu.make_async_copy(second_half, w2_ref.at[:, channels:], sems.at[3]),
    ] + spread_row(taps_hbm, 2 * (1 - odd), w1_ref, sems.at[pl.ds(4, 2)])

    @pl.when(step == 0)
    def _():
        query_copy.start()
        for i in range(steps):
            chunk(own_any, own_ref, i, m, own_sem).start()
            chunk(inner_any, inner_ref, i, m, inner_sem).start()
            if i == 0:
                for copy in late:
                    copy.start()
        acc_ref[...] = jnp.zeros_like(acc_ref)
        pend_ref[...] = jnp.zeros_like(pend_ref)
        clear_spread(w1_ref)
        query_copy.wait()

    chunk(own_any, own_ref, step, m, own_sem).wait()
    chunk(inner_any, inner_ref, step, m, inner_sem).wait()
    here = pl.ds(pl.multiple_of(step * m, m), m)
    block = 256
    own = same_block((block, block), head)
    ones = jnp.where(own, 1.0, 0.0).astype(BF)
    wq = wq_ref[...]
    q_own = queries(own_ref[here, :], wq)
    q_inner = queries(inner_ref[here, :], wq)
    for i in range(frames):
        frame = step * frames + i
        rel = jnp.bitwise_xor(frame, me)
        slot = rel // 2
        other = jnp.bitwise_and(rel, 1) == 1
        piece = jnp.where(other, buf1_ref[slot].astype(F32), buf0_ref[slot].astype(F32))
        before = group_ref[jnp.maximum(frame - 1, 0)]
        fresh = jnp.where(group_ref[frame] != before, 1.0, 0.0)
        pend = pend_ref[...]
        acc = acc_ref[...] + fresh * pend
        acc_ref[...] = acc
        pend_ref[...] = (1.0 - fresh) * pend + piece
        summed = acc + piece
        state = summed[:head].astype(BF)
        total = summed[head : head + 1] + summed[head + 1 : head + 2]
        state_ref[frame] = state
        total_ref[frame] = jnp.broadcast_to(total, (8, width))
        cut = slice(i * rows, (i + 1) * rows)
        both = jnp.concatenate([q_own[cut], q_inner[cut]], axis=0)
        res = attend(both, state, total, own, ones)
        att_ref[0, cut] = res[:rows]
        att_ref[1, cut] = res[rows:]
    first = step * frames
    limit = valid_ref[me]
    keep_own = valid_rows(first, limit, frames, rows)
    keep_inner = valid_rows(first, valid_ref[jnp.bitwise_xor(me, 1)], frames, rows)

    @pl.when(step == 0)
    def _():
        for copy in late:
            copy.wait()

    half = 2 * channels
    mine = jnp.where(keep_own, dot(att_ref[0].astype(BF), wo_ref[...]), 0.0)
    w_close = wo_ref[:, pl.ds(pl.multiple_of(odd * half, half), half)]
    close = jnp.where(keep_inner, dot(att_ref[1].astype(BF), w_close), 0.0)
    store_taps(x_ref, 0, mine[:, : 2 * channels], rows)
    store_taps(x_ref, row, mine[:, 2 * channels :], rows)
    live = jnp.concatenate([keep_own, keep_own], axis=0)
    pair = dot(x_ref[...], w2_ref[...])
    more = dot(line_taps(close, rows), w1_ref[...])
    more = jnp.concatenate([more[:, :channels], more[:, channels:]], axis=0)
    res = jnp.where(live, pair[:, :channels] + more, 0.0)
    near_ref[0] = res[:m]
    near_ref[1] = res[m:]
    gather_stats(stat_ref, res, live, limit, first, frames, rows)
    part_ref[0, here] = pair[:m, channels:]
    part_ref[1, here] = pair[m:, channels:]


def near(rows, me, group_map, valid, buf0, buf1, own, inner, qkv_weight, out_weight, taps, head):
    count, width = own.shape
    frames = 4
    n = count // rows
    wide = out_weight.shape[1]
    channels = taps.shape[1]
    m = frames * rows
    deep = buf0.shape[1]
    return pl.pallas_call(
        functools.partial(near_kernel, rows),
        grid_spec=pltpu.PrefetchScalarGridSpec(
            num_scalar_prefetch=3,
            grid=(n // frames,),
            in_specs=[INSIDE, INSIDE, ANY, ANY, HBM, HBM, HBM],
            out_specs=[pl.BlockSpec((2, m, channels), lambda i, *_: (0, i, 0))] + [INSIDE] * 4,
            scratch_shapes=[
                pltpu.VMEM((deep, width), F32),
                pltpu.VMEM((deep, width), F32),
                pltpu.VMEM((2, m, width), F32),
                pltpu.VMEM((2 * m, 6 * channels), BF),
                pltpu.VMEM((6 * channels, 2 * channels), BF),
                pltpu.VMEM((4 * channels, 2 * channels), BF),
                pltpu.VMEM((width, width), BF),
                pltpu.VMEM((width, wide), BF),
                pltpu.VMEM((count, width), BF),
                pltpu.VMEM((count, width), BF),
                pltpu.SemaphoreType.DMA((n // frames,)),
                pltpu.SemaphoreType.DMA((n // frames,)),
                pltpu.SemaphoreType.DMA((6,)),
            ],
        ),
        out_shape=[
            pltpu.HBM((2, count, channels), F32),
            pltpu.VMEM((2, count, channels), F32),
            pltpu.VMEM((n, head, width), BF),
            pltpu.VMEM((n, 8, width), F32),
            pltpu.VMEM((8, channels), F32),
        ],
        compiler_params=params(24),
        cost_estimate=cost(12 * count * width * width, 16 * count * width),
    )(me, group_map, valid, buf0, buf1, own, inner, qkv_weight, out_weight, taps)


def far_kernel(
    rows, pos_ref, valid_ref,
    outer_any, state_ref, total_ref, part_ref, near_stat_ref, qkv_hbm, wo_hbm, taps_hbm,
    far_ref, stat_ref,
    wx_ref, att_ref, run_ref, wq_ref, wo_ref, outer_ref, outer_sem, sems,
):
    step = pl.program_id(0)
    count, width = outer_ref.shape
    _, m, channels = far_ref.shape
    frames = m // rows
    me = pos_ref[0]
    odd = jnp.bitwise_and(me, 1)
    head = state_ref.shape[1]
    half = 2 * channels
    half_at = pl.ds(pl.multiple_of((1 - odd) * half, half), half)
    copies = [
        pltpu.make_async_copy(qkv_hbm.at[:, pl.ds(0, width)], wq_ref, sems.at[0]),
        pltpu.make_async_copy(wo_hbm.at[:, half_at], wo_ref, sems.at[1]),
    ] + spread_row(taps_hbm, 2 * odd, wx_ref, sems.at[pl.ds(2, 2)])

    @pl.when(step == 0)
    def _():
        copies[0].start()
        for i in range(count // m):
            chunk(outer_any, outer_ref, i, m, outer_sem).start()
            if i == 0:
                for copy in copies[1:]:
                    copy.start()
        clear_spread(wx_ref)
        copies[0].wait()

    chunk(outer_any, outer_ref, step, m, outer_sem).wait()
    here = pl.ds(pl.multiple_of(step * m, m), m)
    block = 256
    own = same_block((block, block), head)
    ones = jnp.where(own, 1.0, 0.0).astype(BF)
    qf = queries(outer_ref[here, :], wq_ref[...])
    for i in range(frames):
        cut = slice(i * rows, (i + 1) * rows)
        frame = step * frames + i
        att_ref[cut] = attend(qf[cut], state_ref[frame], total_ref[frame][0:1], own, ones)
    first = step * frames
    outer_at = jnp.clip(me + 2 * odd - 1, 0, valid_ref.shape[0] - 1)
    keep = valid_rows(first, valid_ref[outer_at], frames, rows)

    @pl.when(step == 0)
    def _():
        for copy in copies[1:]:
            copy.wait()

    line = jnp.where(keep, dot(att_ref[...].astype(BF), wo_ref[...]), 0.0)
    more = dot(line_taps(line, rows), wx_ref[...])
    more = jnp.concatenate([more[:, :channels], more[:, channels:]], axis=0)
    limit = valid_ref[me]
    live = valid_rows(first, limit, frames, rows)
    live = jnp.concatenate([live, live], axis=0)
    part = jnp.concatenate([part_ref[0, here], part_ref[1, here]], axis=0)
    res = jnp.where(live, part + more, 0.0)
    far_ref[0] = res[:m]
    far_ref[1] = res[m:]
    gather_stats(run_ref, res, live, limit, first, frames, rows)

    @pl.when(step == pl.num_programs(0) - 1)
    def _():
        both = jnp.concatenate([near_stat_ref[0:2], run_ref[0:2], run_ref[4:8]], axis=0)
        stat_ref[...] = jnp.broadcast_to(both[None], stat_ref.shape)


def far(rows, me, valid, outer, state, total, part, near_stat, qkv_weight, out_weight, taps):
    count, width = outer.shape
    channels = taps.shape[1]
    frames = 4
    n = count // rows
    m = frames * rows
    return pl.pallas_call(
        functools.partial(far_kernel, rows),
        grid_spec=pltpu.PrefetchScalarGridSpec(
            num_scalar_prefetch=2,
            grid=(n // frames,),
            in_specs=[ANY, INSIDE, INSIDE, INSIDE, INSIDE, HBM, HBM, HBM],
            out_specs=[
                pl.BlockSpec((2, m, channels), lambda i, *_: (0, i, 0)),
                pl.BlockSpec((n, 8, channels), lambda i, *_: (0, 0, 0)),
            ],
            scratch_shapes=[
                pltpu.VMEM((4 * channels, 2 * channels), BF),
                pltpu.VMEM((m, width), F32),
                pltpu.VMEM((8, channels), F32),
                pltpu.VMEM((width, width), BF),
                pltpu.VMEM((width, 2 * channels), BF),
                pltpu.VMEM((count, width), BF),
                pltpu.SemaphoreType.DMA((n // frames,)),
                pltpu.SemaphoreType.DMA((4,)),
            ],
        ),
        out_shape=[
            pltpu.HBM((2, count, channels), F32),
            jax.ShapeDtypeStruct((n, 8, channels), F32),
        ],
        compiler_params=params(24),
        cost_estimate=cost(40 * count * channels * channels, 30 * count * channels),
    )(me, valid, outer, state, total, part, near_stat, qkv_weight, out_weight, taps)


def norm_kernel(
    rows, size, pos_ref, valid_ref, stat_ref, count_ref, gain_ref, bias_ref, near_hbm, far_hbm,
    out_ref, mean_ref, scale_ref, mix_ref, plane_ref, sems,
):
    step = pl.program_id(0)
    frames = out_ref.shape[0]
    m = frames * rows
    channels = out_ref.shape[3]
    steps = near_hbm.shape[1] // m

    def load(y, i):
        at = pl.ds(pl.multiple_of(i * m, m), m)
        src = (near_hbm, far_hbm)[y].at[:, at]
        return pltpu.make_async_copy(src, plane_ref.at[y, :, at], sems.at[y, i])

    me = pos_ref[0]
    odd = jnp.bitwise_and(me, 1)

    @pl.when(step == 0)
    def _():
        for i in range(steps):
            for y in range(2):
                load(y, i).start()
        stat = stat_ref[...]
        counts = count_ref[...]
        mix = jnp.where(same_block((channels, channels), size), 1.0, 0.0)
        all_count = jnp.sum(counts, axis=0, keepdims=True) * (2 * size)

        def grouped(row):
            wide = jnp.broadcast_to(row, (8, channels))
            return dot(wide, mix, precision=lax.Precision.HIGHEST)[0:1]

        sums = stat[:, 0, :] + stat[:, 2, :]
        mean = grouped(jnp.sum(sums, axis=0, keepdims=True)) / all_count
        gap0 = stat[:, 0, :] / counts - mean
        gap1 = stat[:, 2, :] / counts - mean
        spread = stat[:, 1, :] + stat[:, 3, :] + (gap0 * gap0 + gap1 * gap1) * counts
        var = grouped(jnp.sum(spread, axis=0, keepdims=True)) / all_count
        mean_ref[...] = mean
        scale_ref[...] = gain_ref[...] * lax.rsqrt(var + 1e-5)

    live = valid_rows(step * frames, valid_ref[me], frames, rows)
    mean, scale, bias = mean_ref[...], scale_ref[...], bias_ref[...]
    here = pl.ds(pl.multiple_of(step * m, m), m)
    for y in range(2):
        load(y, step).wait()
        line = 1 - odd if y == 0 else odd
        for b in range(2):
            z = (plane_ref[y, b, here] - mean) * scale + bias
            half = 0.5 * z
            z = jnp.where(live, half + half * jnp.tanh(half), 0.0)
            for c in range(channels // 128):
                mix_ref[y, c, pl.ds(b, m, 2), :] = z[:, 128 * c : 128 * (c + 1)]
        for f in range(frames):
            for c in range(channels // 128):
                out_ref[f, line, :, 128 * c : 128 * (c + 1)] = mix_ref[
                    y, c, 2 * rows * f : 2 * rows * (f + 1), :
                ].astype(BF)


def norm(rows, me, valid, stat, counts, gain, bias, near_plane, far_plane):
    count, channels = near_plane.shape[1:]
    n = valid.shape[0]
    frames = 4
    m = frames * rows
    whole = lambda *shape: pl.BlockSpec(shape, lambda i, *_: (0,) * len(shape))
    return pl.pallas_call(
        functools.partial(norm_kernel, rows, channels // NORM_GROUPS),
        grid_spec=pltpu.PrefetchScalarGridSpec(
            num_scalar_prefetch=2,
            grid=(n // frames,),
            in_specs=[
                whole(*stat.shape),
                whole(n, channels),
                whole(1, channels),
                whole(1, channels),
                HBM,
                HBM,
            ],
            out_specs=pl.BlockSpec((frames, 2, 2 * rows, channels), lambda i, *_: (i, 0, 0, 0)),
            scratch_shapes=[
                pltpu.VMEM((1, channels), F32),
                pltpu.VMEM((1, channels), F32),
                pltpu.VMEM((2, channels // 128, 2 * m, 128), F32),
                pltpu.VMEM((2, 2, count, channels), F32),
                pltpu.SemaphoreType.DMA((2, n // frames)),
            ],
        ),
        out_shape=jax.ShapeDtypeStruct((n, 2, 2 * rows, channels), BF),
        compiler_params=params(VMEM),
        cost_estimate=cost(32 * count * channels, 24 * count * channels, 4 * count * channels),
    )(me, valid, stat, counts, gain.reshape(1, channels), bias.reshape(1, channels), near_plane, far_plane)


def local(
    tokens,
    qkv_weight,
    out_weight,
    conv_weight,
    norm_gain,
    norm_bias,
    group_map,
    token_order,
    valid_frames,
):
    tiles = lax.axis_size("tm")
    rank = lax.axis_index("tm")
    count, width = tokens.shape
    rows = count // tiles
    channels = conv_weight.shape[3]
    head = width // HEADS
    me = rank.reshape(1).astype(jnp.int32)

    def swap(x, pairs):
        return lax.ppermute(x, "tm", pairs)

    qkv_weight, out_weight, taps = (
        pltpu.with_memory_space_constraint(w, pltpu.HBM)
        for w in (qkv_weight, out_weight, conv_weight.reshape(-1, channels))
    )
    raster = permute(token_order, tokens)
    tile = lax.all_to_all(
        raster.reshape(tiles, rows, width), "tm", split_axis=0, concat_axis=0, tiled=True
    ).reshape(count, width)
    buf = run_state(tokens, qkv_weight, head)

    def swap_by(x, k):
        return swap(x, [(i, i ^ k) for i in range(tiles)])

    k, gate = 2, None
    while k < tiles:
        ks = [k] if k == 2 or 2 * k >= tiles else [k, 2 * k, 3 * k]
        got = [swap_by(buf, j) for j in ks]
        gate = got[0]
        buf = jnp.concatenate([buf] + got, axis=0)
        k *= 2 if len(ks) == 1 else 4
    other = swap_by(buf, 1)
    tile, _ = lax.optimization_barrier((tile, gate))
    inner = swap_by(tile, 1)
    ends = [(i, i + 1) for i in range(1, tiles - 1, 2)]
    outer = swap(tile, ends + [(j, i) for i, j in ends])
    near_plane, part, state, total, near_stat = near(
        rows, me, group_map, valid_frames, buf, other, tile, inner, qkv_weight, out_weight, taps, head
    )
    far_plane, stat = far(
        rows, me, valid_frames, outer, state, total, part, near_stat, qkv_weight, out_weight, taps
    )
    stat = lax.all_to_all(stat, "tm", split_axis=0, concat_axis=0, tiled=True)
    counts = jnp.broadcast_to(
        (valid_frames * (2 * rows)).astype(F32)[:, None], (tiles, channels)
    )
    return norm(rows, me, valid_frames, stat, counts, norm_gain, norm_bias, near_plane, far_plane)


def solution(mesh):
    in_specs = (P(("clip", "tm"), None), P(), P(), P(), P(), P(), P("clip"), P("clip"), P("clip"))
    out_specs = P("clip", "tm", None, None)
    return jax.shard_map(local, mesh=mesh, in_specs=in_specs, out_specs=out_specs, check_vma=False)
```

time: 108 us -> 96.1 us (0.89)
  waiting for transfers between devices: 47.8 us -> 27.8 us
  Pallas kernels: 28.5 us -> 38.2 us
  local copies, waits for them, and re-layouts: 12.4 us -> 3.21 us
  starting transfers between devices: 17.5 us -> 24.6 us
    ppermute x6 -> x7, waiting for transfers between devices: 39.8 us -> 16.8 us  [swap(): return lax.ppermute(x, 'tm', pairs)]
    unnamed x36 -> x12, local copies, waits for them, and re-layouts: 11.3 us -> 2.53 us
    pallas_call x3, Pallas kernels: 21.2 us -> 27.5 us  [the longest x1 14.8 us: near(): pl.pallas_call(functools.partial(near_kernel, rows), grid_spec=pltpu.Pref...]
    ppermute x6 -> x7, starting transfers between devices: 6.19 us -> 10 us  [swap(): return lax.ppermute(x, 'tm', pairs)]
    all_to_all x1, starting transfers between devices: 3.88 us -> 7.23 us  [local(): stat = lax.all_to_all(stat, 'tm', split_axis=0, concat_axis=0, tiled=True)]
    all_to_all x1, waiting for transfers between devices: 0.01 us -> 3.01 us  [local(): lax.all_to_all(raster.reshape(tiles, rows, width), 'tm', split_axis=0, co...]
    pallas_call x1, Pallas kernels: 2.78 us -> 4.91 us  [run_state(): pl.pallas_call(functools.partial(state_kernel, head), grid=(steps,), in_s...]
    pallas_call x1, Pallas kernels: 4.51 us -> 5.79 us  [norm(): pl.pallas_call(functools.partial(norm_kernel, rows, channels // NORM_GROU...]
  transfers between devices with their start and end apart: 8 -> 9, of which waited for: 5 -> 6; matrix products, arithmetic and copies ran while one was open for 3% -> 4% of each run, Pallas kernels for 9% -> 21%
where the time goes in v2:
time: 96.1 us; the launch traced here: 95.4 us
  Pallas kernels  38.2 us (40%)
  waiting for transfers between devices  27.8 us (29%)
  starting transfers between devices  24.6 us (26%)
  local copies, waits for them, and re-layouts  3.21 us (3%)
  other arithmetic  1.47 us (2%)
    ppermute x7, waiting for transfers between devices, swap(): return lax.ppermute(x, 'tm', pairs)  16.8 us
    pallas_call x1, Pallas kernels, near(): pl.pallas_call(functools.partial(near_kernel, rows), grid_spec=pltpu.Pref...  14.8 us
    ppermute x7, starting transfers between devices, swap(): return lax.ppermute(x, 'tm', pairs)  10 us
    pallas_call x1, Pallas kernels, far(): pl.pallas_call(functools.partial(far_kernel, rows), grid_spec=pltpu.Prefe...  9.07 us
    all_to_all x1, waiting for transfers between devices, local(): stat = lax.all_to_all(stat, 'tm', split_axis=0, concat_axis=0, tiled=True)  7.92 us
    all_to_all x1, starting transfers between devices, local(): lax.all_to_all(raster.reshape(tiles, rows, width), 'tm', split_axis=0, co...  7.39 us
    all_to_all x1, starting transfers between devices, local(): stat = lax.all_to_all(stat, 'tm', split_axis=0, concat_axis=0, tiled=True)  7.23 us
    pallas_call x1, Pallas kernels, norm(): pl.pallas_call(functools.partial(norm_kernel, rows, channels // NORM_GROU...  5.79 us
  transfers between devices with their start and end apart: 9, of which 6 were waited for; matrix products, arithmetic and copies ran while one was open for 4% of the time, Pallas kernels for 21%

profile of v2, /device:TPU:0, one launch (start us, length us, event | category | flops | bytes accessed | tf_op | source)
XLA Modules:
  0.0 95.4 jit_solution(9523574183610457207)
XLA Ops:
  0.0 3.6 %shard_map.91 = bf16[1024,512]{1,0:T(8,128)(2,1)} custom-call(s32[1,1024]{1,0:T(1,128)} %bitcast.15, bf16[1024,512]{1,0:T(8,128)(2,1)} %tok_ref.3), custom_call_target="tpu_custom_call" | custom-call | flops 1073741824 | bytes 2097152 | tf_op jit(solution)/shard_map/pallas_call | solution.py:52
  3.6 7.4 %all-to-all-start = ((bf16[16,64,512]{2,1,0:T(8,128)(2,1)}), bf16[16,64,512]{2,1,0:T(8,128)(2,1)S(1)}, u32[]{:S(2)}, u32[]{:S(2)}) async-start(bf16[16,64,512]{2,1,0:T(8,128)(2,1)} %bitcast.10), calls=%async_computation | async-start | bytes 2097152 | tf_op jit(solution)/shard_map/all_to_all | solution.py:592
  11.1 4.9 %shard_map.92 = bf16[1,48,512]{2,1,0:T(8,128)(2,1)} custom-call(bf16[1024,512]{1,0:T(8,128)(2,1)} %tok_ref.3, bf16[512,1536]{1,0:T(8,128)(2,1)} %qkv_hbm.3, bf16[512,1536]{1,0:T(8,128)(2,1)} %qkv_hbm.3), custom_call_target="tpu_custom_call" | custom-call | flops 1073741824 | bytes 4194304 | tf_op jit(solution)/shard_map/pallas_call | solution.py:116
  16.0 1.9 %collective-permute-start = (bf16[1,48,512]{2,1,0:T(8,128)(2,1)}, bf16[1,48,512]{2,1,0:T(8,128)(2,1)S(1)}, u32[]{:S(2)}, u32[]{:S(2)}) collective-permute-start(bf16[1,48,512]{2,1,0:T(8,128)(2,1)} %shard_map.92), channel_id=1, source_target_pairs={{0,2},{1,3},{2,0},{3,1},{4,6},{5,7},{6,4},{7,5},{8,10},{9,11},{10,... | collective-permute-start | bytes 147464 | tf_op jit(solution)/shard_map/ppermute | solution.py:585
  17.9 3.0 %collective-permute-done = bf16[1,48,512]{2,1,0:T(8,128)(2,1)S(1)} collective-permute-done((bf16[1,48,512]{2,1,0:T(8,128)(2,1)}, bf16[1,48,512]{2,1,0:T(8,128)(2,1)S(1)}, u32[]{:S(2)}, u32[]{:S(2)}) %collective-permute-start) | collective-permute-done | bytes 49184 | tf_op jit(solution)/shard_map/ppermute | solution.py:585
  20.9 1.5 %pad_maximum_fusion = bf16[2,48,512]{2,1,0:T(8,128)(2,1)} fusion(bf16[1,48,512]{2,1,0:T(8,128)(2,1)S(1)} %collective-permute-done, bf16[1,48,512]{2,1,0:T(8,128)(2,1)} %shard_map.92), kind=kLoop, calls=%fused_computation | loop fusion | flops 49152 | bytes 196608 | tf_op jit(solution)/shard_map/concatenate | solution.py:605
  22.3 1.3 %collective-permute-start.1 = (bf16[2,48,512]{2,1,0:T(8,128)(2,1)}, bf16[2,48,512]{2,1,0:T(8,128)(2,1)}, u32[]{:S(2)}, u32[]{:S(2)}) collective-permute-start(bf16[2,48,512]{2,1,0:T(8,128)(2,1)} %pad_maximum_fusion), channel_id=1, source_target_pairs={{0,4},{1,5},{2,6},{3,7},{4,0},{5,1},{6,2},{7,3},{8,12},{9,13},{10,... | collective-permute-start | bytes 294920 | tf_op jit(solution)/shard_map/ppermute | solution.py:585
  23.7 7.7 %collective-permute-done.1 = bf16[2,48,512]{2,1,0:T(8,128)(2,1)} collective-permute-done((bf16[2,48,512]{2,1,0:T(8,128)(2,1)}, bf16[2,48,512]{2,1,0:T(8,128)(2,1)}, u32[]{:S(2)}, u32[]{:S(2)}) %collective-permute-start.1) | collective-permute-done | bytes 98336 | tf_op jit(solution)/shard_map/ppermute | solution.py:585
  31.3 3.0 %all-to-all-done = bf16[16,64,512]{2,1,0:T(8,128)(2,1)S(1)} async-done(((bf16[16,64,512]{2,1,0:T(8,128)(2,1)}), bf16[16,64,512]{2,1,0:T(8,128)(2,1)S(1)}, u32[]{:S(2)}, u32[]{:S(2)}) %all-to-all-start) | async-done | bytes 1048608 | tf_op jit(solution)/shard_map/all_to_all | solution.py:592
  34.3 0.2 collective-permute-start.6
  34.6 0.8 constant_dynamic-update-slice_fusion.4
  35.4 4.5 %collective-permute-start.3 = (bf16[2,48,512]{2,1,0:T(8,128)(2,1)}, bf16[2,48,512]{2,1,0:T(8,128)(2,1)S(1)}, u32[]{:S(2)}, u32[]{:S(2)}) collective-permute-start(bf16[2,48,512]{2,1,0:T(8,128)(2,1)} %pad_maximum_fusion), channel_id=1, source_target_pairs={{0,8},{1,9},{2,10},{3,11},{4,12},{5,13},{6,14},{7,15},{8,0},{9,1},... | collective-permute-start | bytes 294920 | tf_op jit(solution)/shard_map/ppermute | solution.py:585
  39.8 1.3 %collective-permute-start.4 = (bf16[2,48,512]{2,1,0:T(8,128)(2,1)}, bf16[2,48,512]{2,1,0:T(8,128)(2,1)S(1)}, u32[]{:S(2)}, u32[]{:S(2)}) collective-permute-start(bf16[2,48,512]{2,1,0:T(8,128)(2,1)} %pad_maximum_fusion), channel_id=1, source_target_pairs={{0,12},{1,13},{2,14},{3,15},{4,8},{5,9},{6,10},{7,11},{8,4},{9,5},... | collective-permute-start | bytes 294920 | tf_op jit(solution)/shard_map/ppermute | solution.py:585
  41.1 0.7 collective-permute-start.2
  41.8 0.8 constant_dynamic-update-slice_fusion.3
  42.6 0.9 constant_dynamic-update-slice_fusion.2
  43.5 4.4 %collective-permute-done.3 = bf16[2,48,512]{2,1,0:T(8,128)(2,1)S(1)} collective-permute-done((bf16[2,48,512]{2,1,0:T(8,128)(2,1)}, bf16[2,48,512]{2,1,0:T(8,128)(2,1)S(1)}, u32[]{:S(2)}, u32[]{:S(2)}) %collective-permute-start.3) | collective-permute-done | bytes 98336 | tf_op jit(solution)/shard_map/ppermute | solution.py:585
  48.0 1.8 %collective-permute-done.5.buf1_ref = bf16[8,48,512]{2,1,0:T(8,128)(2,1)} collective-permute-done((bf16[8,48,512]{2,1,0:T(8,128)(2,1)S(1)}, bf16[8,48,512]{2,1,0:T(8,128)(2,1)}, u32[]{:S(2)}, u32[]{:S(2)}) %collective-permute-start.5) | collective-permute-done | bytes 393248 | tf_op jit(solution)/shard_map/ppermute | solution.py:585
  49.9 14.8 %shard_map.93 = (f32[2,1024,256]{2,1,0:T(8,128)}, f32[2,1024,256]{2,1,0:T(8,128)S(1)}, bf16[16,32,512]{2,1,0:T(8,128)(2,1)S(1)}, f32[16,8,512]{2,1,0:T(8,128)S(1)}, f32[8,256]{1,0:T(8,128)S(1)}) custom-call(s32[1]{0:T(128)} %bitcast.pos_ref, s32[16]{0:T(128)S(1)} %copy-done.1, s32[16]{0:T(128)S(1)} %copy-done, ...), custom_call_target="tpu_custom_call" | custom-call | flops 3221225472 | bytes 8388608 | tf_op jit(solution)/shard_map/pallas_call | solution.py:332
  64.7 9.1 %shard_map.94 = (f32[2,1024,256]{2,1,0:T(8,128)}, f32[16,8,256]{2,1,0:T(8,128)}) custom-call(s32[1]{0:T(128)} %bitcast.pos_ref, s32[16]{0:T(128)S(1)} %copy-done, bf16[1024,512]{1,0:T(8,128)(2,1)S(1)} %collective-permute-done.2.outer_any, bf16[16,32,512]{2,1,0:T(8,128)(2,1)S(1)} %get-tuple-element.14.state_ref, ...), custom_call_target="tpu_custom_call" | custom-call | flops 2684354560 | bytes 7864320 | tf_op jit(solution)/shard_map/pallas_call | solution.py:441
  73.8 7.2 %all-to-all-start.1 = ((f32[16,8,256]{2,1,0:T(8,128)}), f32[16,8,256]{2,1,0:T(8,128)S(1)}, u32[]{:S(2)}, u32[]{:S(2)}) async-start(f32[16,8,256]{2,1,0:T(8,128)} %get-tuple-element.18), calls=%async_computation.1 | async-start | bytes 262144 | tf_op jit(solution)/shard_map/all_to_all | solution.py:618
  81.0 7.9 %all-to-all-done.1.stat_ref = f32[16,8,256]{2,1,0:T(8,128)S(1)} async-done(((f32[16,8,256]{2,1,0:T(8,128)}), f32[16,8,256]{2,1,0:T(8,128)S(1)}, u32[]{:S(2)}, u32[]{:S(2)}) %all-to-all-start.1) | async-done | bytes 131104 | tf_op jit(solution)/shard_map/all_to_all | solution.py:618
  89.0 0.7 broadcast_in_dim.2.count_ref
  89.6 5.8 %shard_map.95 = bf16[16,2,128,256]{3,2,1,0:T(8,128)(2,1)} custom-call(s32[1]{0:T(128)} %bitcast.pos_ref, s32[16]{0:T(128)} %valid_ref.5, f32[16,8,256]{2,1,0:T(8,128)} %copy-done.2, f32[16,256]{1,0:T(8,128)} %broadcast_in_dim.2.count_ref, f32[1,256]{1,0:T(1,128)} %bitcast.11, f32[1,256]{1,0:T(1,128)} %bitcast.12, ...), custom_call_target="tpu_custom_call" | custom-call | flops 8388608 | bytes 6291456 | tf_op jit(solution)/shard_map/pallas_call | solution.py:537
  (15 shorter events, 0.1 us)
Async XLA Ops:
  3.6 30.7 %all-to-all-start = ((bf16[16,64,512]{2,1,0:T(8,128)(2,1)}), bf16[16,64,512]{2,1,0:T(8,128)(2,1)S(1)}, u32[]{:S(2)}, u32[]{:S(2)}) async-start(bf16[16,64,512]{2,1,0:T(8,128)(2,1)} %bitcast.10), calls=%async_computation | async-start | bytes 2097152 | tf_op jit(solution)/shard_map/all_to_all | solution.py:592
  11.0 38.8 %copy-start = (s32[16]{0:T(128)S(1)}, s32[16]{0:T(128)}, u32[]{:S(2)}) copy-start(s32[16]{0:T(128)} %valid_ref.5) | copy-start | bytes 196
  11.0 38.8 %copy-start.1 = (s32[16]{0:T(128)S(1)}, s32[16]{0:T(128)}, u32[]{:S(2)}) copy-start(s32[16]{0:T(128)} %group_ref.1) | copy-start | bytes 196
  16.0 4.9 %collective-permute-start = (bf16[1,48,512]{2,1,0:T(8,128)(2,1)}, bf16[1,48,512]{2,1,0:T(8,128)(2,1)S(1)}, u32[]{:S(2)}, u32[]{:S(2)}) collective-permute-start(bf16[1,48,512]{2,1,0:T(8,128)(2,1)} %shard_map.92), channel_id=1, source_target_pairs={{0,2},{1,3},{2,0},{3,1},{4,6},{5,7},{6,4},{7,5},{8,10},{9,11},{10,... | collective-permute-start | bytes 147464 | tf_op jit(solution)/shard_map/ppermute | solution.py:585
  20.9 2.8 %copy-start.3 = (bf16[1,48,512]{2,1,0:T(8,128)(2,1)}, bf16[1,48,512]{2,1,0:T(8,128)(2,1)S(1)}, u32[]{:S(2)}) copy-start(bf16[1,48,512]{2,1,0:T(8,128)(2,1)S(1)} %collective-permute-done) | copy-start | bytes 147460
  22.3 9.0 %collective-permute-start.1 = (bf16[2,48,512]{2,1,0:T(8,128)(2,1)}, bf16[2,48,512]{2,1,0:T(8,128)(2,1)}, u32[]{:S(2)}, u32[]{:S(2)}) collective-permute-start(bf16[2,48,512]{2,1,0:T(8,128)(2,1)} %pad_maximum_fusion), channel_id=1, source_target_pairs={{0,4},{1,5},{2,6},{3,7},{4,0},{5,1},{6,2},{7,3},{8,12},{9,13},{10,... | collective-permute-start | bytes 294920 | tf_op jit(solution)/shard_map/ppermute | solution.py:585
  34.3 15.5 %collective-permute-start.6 = (bf16[1024,512]{1,0:T(8,128)(2,1)S(1)}, bf16[1024,512]{1,0:T(8,128)(2,1)S(1)}, u32[]{:S(2)}, u32[]{:S(2)}) collective-permute-start(bf16[1024,512]{1,0:T(8,128)(2,1)S(1)} %bitcast.7), channel_id=1, source_target_pairs={{0,1},{1,0},{2,3},{3,2},{4,5},{5,4},{6,7},{7,6},{8,9},{9,8},{10,11... | collective-permute-start | bytes 3145736 | tf_op jit(solution)/shard_map/ppermute | solution.py:585
  35.4 12.5 %collective-permute-start.3 = (bf16[2,48,512]{2,1,0:T(8,128)(2,1)}, bf16[2,48,512]{2,1,0:T(8,128)(2,1)S(1)}, u32[]{:S(2)}, u32[]{:S(2)}) collective-permute-start(bf16[2,48,512]{2,1,0:T(8,128)(2,1)} %pad_maximum_fusion), channel_id=1, source_target_pairs={{0,8},{1,9},{2,10},{3,11},{4,12},{5,13},{6,14},{7,15},{8,0},{9,1},... | collective-permute-start | bytes 294920 | tf_op jit(solution)/shard_map/ppermute | solution.py:585
  39.8 8.1 %collective-permute-start.4 = (bf16[2,48,512]{2,1,0:T(8,128)(2,1)}, bf16[2,48,512]{2,1,0:T(8,128)(2,1)S(1)}, u32[]{:S(2)}, u32[]{:S(2)}) collective-permute-start(bf16[2,48,512]{2,1,0:T(8,128)(2,1)} %pad_maximum_fusion), channel_id=1, source_target_pairs={{0,12},{1,13},{2,14},{3,15},{4,8},{5,9},{6,10},{7,11},{8,4},{9,5},... | collective-permute-start | bytes 294920 | tf_op jit(solution)/shard_map/ppermute | solution.py:585
  41.1 23.6 %collective-permute-start.2 = (bf16[1024,512]{1,0:T(8,128)(2,1)S(1)}, bf16[1024,512]{1,0:T(8,128)(2,1)S(1)}, u32[]{:S(2)}, u32[]{:S(2)}) collective-permute-start(bf16[1024,512]{1,0:T(8,128)(2,1)S(1)} %bitcast.8), channel_id=1, source_target_pairs={{1,2},{3,4},{5,6},{7,8},{9,10},{11,12},{13,14},{2,1},{4,3},{6,5},{... | collective-permute-start | bytes 3145736 | tf_op jit(solution)/shard_map/ppermute | solution.py:585
  48.0 1.9 %collective-permute-start.5 = (bf16[8,48,512]{2,1,0:T(8,128)(2,1)S(1)}, bf16[8,48,512]{2,1,0:T(8,128)(2,1)}, u32[]{:S(2)}, u32[]{:S(2)}) collective-permute-start(bf16[8,48,512]{2,1,0:T(8,128)(2,1)S(1)} %constant_dynamic-update-slice_fusion.buf0_ref), channel_id=1, source_target_pairs={{0,1},{1,0},{2,3},{3,2},{4,5},{5,4},{6,7},{7,6},{8,9},{9,8},{10,11... | collective-permute-start | bytes 1179656 | tf_op jit(solution)/shard_map/ppermute | solution.py:585
  73.8 15.2 %all-to-all-start.1 = ((f32[16,8,256]{2,1,0:T(8,128)}), f32[16,8,256]{2,1,0:T(8,128)S(1)}, u32[]{:S(2)}, u32[]{:S(2)}) async-start(f32[16,8,256]{2,1,0:T(8,128)} %get-tuple-element.18), calls=%async_computation.1 | async-start | bytes 262144 | tf_op jit(solution)/shard_map/all_to_all | solution.py:618
  89.0 0.7 copy-start.2

commit v3 on v2

--- a/solution.py
+++ b/solution.py
@@ -205,10 +205,6 @@
 
 
 def gather_stats(run_ref, res, live, limit, first, frames, rows):
-    @pl.when(first == 0)
-    def _():
-        run_ref[...] = jnp.zeros_like(run_ref)
-
     part = jnp.sum(res, axis=0, keepdims=True)
     count = (jnp.clip(limit - first, 0, frames) * (2 * rows)).astype(F32)
     mean = part / jnp.maximum(count, 1.0)
@@ -223,16 +219,16 @@
 
 
 def near_kernel(
-    rows, pos_ref, group_ref, valid_ref,
-    buf0_ref, buf1_ref, own_any, inner_any, qkv_hbm, wo_hbm, taps_hbm,
-    near_ref, part_ref, state_ref, total_ref, stat_ref,
-    acc_ref, pend_ref, att_ref, x_ref, w2_ref, w1_ref, wq_ref, wo_ref, own_ref, inner_ref,
-    own_sem, inner_sem, sems,
+    rows, parts, frames, pos_ref, group_ref, valid_ref, *refs
 ):
+    pieces, refs = refs[: 2 * parts], refs[2 * parts :]
+    own_any, inner_any, qkv_hbm, wo_hbm, taps_hbm, *refs = refs
+    near_ref, part_ref, state_ref, total_ref, stat_ref, *refs = refs
+    acc_ref, pend_ref, att_ref, x_ref, w2_ref, w1_ref, wq_ref, wo_ref, *refs = refs
+    own_ref, inner_ref, buf_ref, own_sem, inner_sem, sems, piece_sem = refs
     step = pl.program_id(0)
     count, width = own_ref.shape
-    m = near_ref.shape[1]
-    frames = m // rows
+    m = frames * rows
     steps = count // m
     me = pos_ref[0]
     odd = jnp.bitwise_and(me, 1)
@@ -248,9 +244,19 @@
         pltpu.make_async_copy(second_half, w2_ref.at[:, channels:], sems.at[3]),
     ] + spread_row(taps_hbm, 2 * (1 - odd), w1_ref, sems.at[pl.ds(4, 2)])
 
+    size = pieces[0].shape[0]
+    fetch = [
+        pltpu.make_async_copy(
+            pieces[i], buf_ref.at[i // parts, pl.ds(i % parts * size, size)], piece_sem.at[i]
+        )
+        for i in range(2 * parts)
+    ]
+
     @pl.when(step == 0)
     def _():
         query_copy.start()
+        for copy in fetch:
+            copy.start()
         for i in range(steps):
             chunk(own_any, own_ref, i, m, own_sem).start()
             chunk(inner_any, inner_ref, i, m, inner_sem).start()
@@ -260,7 +266,10 @@
         acc_ref[...] = jnp.zeros_like(acc_ref)
         pend_ref[...] = jnp.zeros_like(pend_ref)
         clear_spread(w1_ref)
+        stat_ref[...] = jnp.zeros_like(stat_ref)
         query_copy.wait()
+        for copy in fetch:
+            copy.wait()
 
     chunk(own_any, own_ref, step, m, own_sem).wait()
     chunk(inner_any, inner_ref, step, m, inner_sem).wait()
@@ -274,9 +283,7 @@
     for i in range(frames):
         frame = step * frames + i
         rel = jnp.bitwise_xor(frame, me)
-        slot = rel // 2
-        other = jnp.bitwise_and(rel, 1) == 1
-        piece = jnp.where(other, buf1_ref[slot].astype(F32), buf0_ref[slot].astype(F32))
+        piece = buf_ref[jnp.bitwise_and(rel, 1), rel // 2].astype(F32)
         before = group_ref[jnp.maximum(frame - 1, 0)]
         fresh = jnp.where(group_ref[frame] != before, 1.0, 0.0)
         pend = pend_ref[...]
@@ -314,28 +321,29 @@
     more = dot(line_taps(close, rows), w1_ref[...])
     more = jnp.concatenate([more[:, :channels], more[:, channels:]], axis=0)
     res = jnp.where(live, pair[:, :channels] + more, 0.0)
-    near_ref[0] = res[:m]
-    near_ref[1] = res[m:]
+    near_ref[0, here] = res[:m]
+    near_ref[1, here] = res[m:]
     gather_stats(stat_ref, res, live, limit, first, frames, rows)
     part_ref[0, here] = pair[:m, channels:]
     part_ref[1, here] = pair[m:, channels:]
 
 
-def near(rows, me, group_map, valid, buf0, buf1, own, inner, qkv_weight, out_weight, taps, head):
+def near(rows, me, group_map, valid, pieces, own, inner, qkv_weight, out_weight, taps, head):
     count, width = own.shape
-    frames = 4
+    frames = 16
     n = count // rows
     wide = out_weight.shape[1]
     channels = taps.shape[1]
     m = frames * rows
-    deep = buf0.shape[1]
+    deep = pieces[0].shape[1]
+    parts = len(pieces) // 2
     return pl.pallas_call(
-        functools.partial(near_kernel, rows),
+        functools.partial(near_kernel, rows, parts, frames),
         grid_spec=pltpu.PrefetchScalarGridSpec(
             num_scalar_prefetch=3,
             grid=(n // frames,),
-            in_specs=[INSIDE, INSIDE, ANY, ANY, HBM, HBM, HBM],
-            out_specs=[pl.BlockSpec((2, m, channels), lambda i, *_: (0, i, 0))] + [INSIDE] * 4,
+            in_specs=[ANY] * (2 * parts + 2) + [HBM] * 3,
+            out_specs=[INSIDE] * 5,
             scratch_shapes=[
                 pltpu.VMEM((deep, width), F32),
                 pltpu.VMEM((deep, width), F32),
@@ -347,32 +355,33 @@
                 pltpu.VMEM((width, wide), BF),
                 pltpu.VMEM((count, width), BF),
                 pltpu.VMEM((count, width), BF),
+                pltpu.VMEM((2, n // 2, deep, width), BF),
                 pltpu.SemaphoreType.DMA((n // frames,)),
                 pltpu.SemaphoreType.DMA((n // frames,)),
                 pltpu.SemaphoreType.DMA((6,)),
+                pltpu.SemaphoreType.DMA((2 * parts,)),
             ],
         ),
         out_shape=[
-            pltpu.HBM((2, count, channels), F32),
+            pltpu.VMEM((2, count, channels), F32),
             pltpu.VMEM((2, count, channels), F32),
             pltpu.VMEM((n, head, width), BF),
             pltpu.VMEM((n, 8, width), F32),
             pltpu.VMEM((8, channels), F32),
         ],
-        compiler_params=params(24),
-        cost_estimate=cost(12 * count * width * width, 16 * count * width),
-    )(me, group_map, valid, buf0, buf1, own, inner, qkv_weight, out_weight, taps)
+        compiler_params=params(40),
+        cost_estimate=cost(1, 1),
+    )(me, group_map, valid, *pieces, own, inner, qkv_weight, out_weight, taps)
 
 
 def far_kernel(
-    rows, pos_ref, valid_ref,
-    outer_any, state_ref, total_ref, part_ref, near_stat_ref, qkv_hbm, wo_hbm, taps_hbm,
+    rows, first, last, pos_ref, valid_ref,
+    outer_any, state_ref, total_ref, part_ref, before_ref, near_stat_ref, qkv_hbm, wo_hbm, taps_hbm,
     far_ref, stat_ref,
-    wx_ref, att_ref, run_ref, wq_ref, wo_ref, outer_ref, outer_sem, sems,
+    wx_ref, att_ref, run_ref, wq_ref, wo_ref, outer_ref, sems,
 ):
-    step = pl.program_id(0)
-    count, width = outer_ref.shape
-    _, m, channels = far_ref.shape
+    m, width = outer_ref.shape
+    channels = far_ref.shape[2]
     frames = m // rows
     me = pos_ref[0]
     odd = jnp.bitwise_and(me, 1)
@@ -381,118 +390,90 @@
     half_at = pl.ds(pl.multiple_of((1 - odd) * half, half), half)
     copies = [
         pltpu.make_async_copy(qkv_hbm.at[:, pl.ds(0, width)], wq_ref, sems.at[0]),
-        pltpu.make_async_copy(wo_hbm.at[:, half_at], wo_ref, sems.at[1]),
-    ] + spread_row(taps_hbm, 2 * odd, wx_ref, sems.at[pl.ds(2, 2)])
-
-    @pl.when(step == 0)
-    def _():
-        copies[0].start()
-        for i in range(count // m):
-            chunk(outer_any, outer_ref, i, m, outer_sem).start()
-            if i == 0:
-                for copy in copies[1:]:
-                    copy.start()
-        clear_spread(wx_ref)
-        copies[0].wait()
-
-    chunk(outer_any, outer_ref, step, m, outer_sem).wait()
-    here = pl.ds(pl.multiple_of(step * m, m), m)
+        pltpu.make_async_copy(outer_any, outer_ref, sems.at[1]),
+        pltpu.make_async_copy(wo_hbm.at[:, half_at], wo_ref, sems.at[2]),
+    ] + spread_row(taps_hbm, 2 * odd, wx_ref, sems.at[pl.ds(3, 2)])
+    for copy in copies:
+        copy.start()
+    clear_spread(wx_ref)
+    run_ref[...] = before_ref[...]
     block = 256
     own = same_block((block, block), head)
     ones = jnp.where(own, 1.0, 0.0).astype(BF)
-    qf = queries(outer_ref[here, :], wq_ref[...])
+    copies[0].wait()
+    copies[1].wait()
+    qf = queries(outer_ref[...], wq_ref[...])
     for i in range(frames):
         cut = slice(i * rows, (i + 1) * rows)
-        frame = step * frames + i
+        frame = first + i
         att_ref[cut] = attend(qf[cut], state_ref[frame], total_ref[frame][0:1], own, ones)
-    first = step * frames
     outer_at = jnp.clip(me + 2 * odd - 1, 0, valid_ref.shape[0] - 1)
     keep = valid_rows(first, valid_ref[outer_at], frames, rows)
-
-    @pl.when(step == 0)
-    def _():
-        for copy in copies[1:]:
-            copy.wait()
-
+    for copy in copies[2:]:
+        copy.wait()
     line = jnp.where(keep, dot(att_ref[...].astype(BF), wo_ref[...]), 0.0)
     more = dot(line_taps(line, rows), wx_ref[...])
     more = jnp.concatenate([more[:, :channels], more[:, channels:]], axis=0)
     limit = valid_ref[me]
     live = valid_rows(first, limit, frames, rows)
     live = jnp.concatenate([live, live], axis=0)
+    here = pl.ds(first * rows, m)
     part = jnp.concatenate([part_ref[0, here], part_ref[1, here]], axis=0)
     res = jnp.where(live, part + more, 0.0)
     far_ref[0] = res[:m]
     far_ref[1] = res[m:]
     gather_stats(run_ref, res, live, limit, first, frames, rows)
-
-    @pl.when(step == pl.num_programs(0) - 1)
-    def _():
+    if last:
         both = jnp.concatenate([near_stat_ref[0:2], run_ref[0:2], run_ref[4:8]], axis=0)
         stat_ref[...] = jnp.broadcast_to(both[None], stat_ref.shape)
-
-
-def far(rows, me, valid, outer, state, total, part, near_stat, qkv_weight, out_weight, taps):
-    count, width = outer.shape
+    else:
+        stat_ref[...] = run_ref[...]
+
+
+def far(rows, first, me, valid, outer, state, total, part, before, near_stat, qkv_weight, out_weight, taps):
+    m, width = outer.shape
     channels = taps.shape[1]
-    frames = 4
-    n = count // rows
-    m = frames * rows
+    n = state.shape[0]
+    last = first + m // rows == n
+    smem = pl.BlockSpec(memory_space=pltpu.SMEM)
+    stat = jax.ShapeDtypeStruct((n, 8, channels), F32) if last else pltpu.VMEM((8, channels), F32)
     return pl.pallas_call(
-        functools.partial(far_kernel, rows),
-        grid_spec=pltpu.PrefetchScalarGridSpec(
-            num_scalar_prefetch=2,
-            grid=(n // frames,),
-            in_specs=[ANY, INSIDE, INSIDE, INSIDE, INSIDE, HBM, HBM, HBM],
-            out_specs=[
-                pl.BlockSpec((2, m, channels), lambda i, *_: (0, i, 0)),
-                pl.BlockSpec((n, 8, channels), lambda i, *_: (0, 0, 0)),
-            ],
-            scratch_shapes=[
-                pltpu.VMEM((4 * channels, 2 * channels), BF),
-                pltpu.VMEM((m, width), F32),
-                pltpu.VMEM((8, channels), F32),
-                pltpu.VMEM((width, width), BF),
-                pltpu.VMEM((width, 2 * channels), BF),
-                pltpu.VMEM((count, width), BF),
-                pltpu.SemaphoreType.DMA((n // frames,)),
-                pltpu.SemaphoreType.DMA((4,)),
-            ],
-        ),
-        out_shape=[
-            pltpu.HBM((2, count, channels), F32),
-            jax.ShapeDtypeStruct((n, 8, channels), F32),
+        functools.partial(far_kernel, rows, first, last),
+        in_specs=[smem, smem, ANY] + [INSIDE] * 5 + [HBM] * 3,
+        out_specs=[INSIDE, INSIDE],
+        scratch_shapes=[
+            pltpu.VMEM((4 * channels, 2 * channels), BF),
+            pltpu.VMEM((m, width), F32),
+            pltpu.VMEM((8, channels), F32),
+            pltpu.VMEM((width, width), BF),
+            pltpu.VMEM((width, 2 * channels), BF),
+            pltpu.VMEM((m, width), BF),
+            pltpu.SemaphoreType.DMA((5,)),
         ],
-        compiler_params=params(24),
-        cost_estimate=cost(40 * count * channels * channels, 30 * count * channels),
-    )(me, valid, outer, state, total, part, near_stat, qkv_weight, out_weight, taps)
+        out_shape=[pltpu.VMEM((2, m, channels), F32), stat],
+        compiler_params=pltpu.CompilerParams(vmem_limit_bytes=32 * MIB),
+        cost_estimate=cost(1, 1),
+    )(me, valid, outer, state, total, part, before, near_stat, qkv_weight, out_weight, taps)
 
 
 def norm_kernel(
-    rows, size, pos_ref, valid_ref, stat_ref, count_ref, gain_ref, bias_ref, near_hbm, far_hbm,
-    out_ref, mean_ref, scale_ref, mix_ref, plane_ref, sems,
+    rows, size, pos_ref, valid_ref, stat_ref, gain_ref, bias_ref, near_ref, far0_ref, far1_ref,
+    out_ref, mul_ref, add_ref, mix_ref,
 ):
     step = pl.program_id(0)
     frames = out_ref.shape[0]
     m = frames * rows
     channels = out_ref.shape[3]
-    steps = near_hbm.shape[1] // m
-
-    def load(y, i):
-        at = pl.ds(pl.multiple_of(i * m, m), m)
-        src = (near_hbm, far_hbm)[y].at[:, at]
-        return pltpu.make_async_copy(src, plane_ref.at[y, :, at], sems.at[y, i])
-
     me = pos_ref[0]
     odd = jnp.bitwise_and(me, 1)
 
     @pl.when(step == 0)
     def _():
-        for i in range(steps):
-            for y in range(2):
-                load(y, i).start()
         stat = stat_ref[...]
-        counts = count_ref[...]
+        tile = lax.broadcasted_iota(jnp.int32, (stat.shape[0], channels), 0)
+        counts = jnp.zeros(tile.shape, F32)
+        for i in range(stat.shape[0]):
+            counts = jnp.where(tile == i, (valid_ref[i] * (2 * rows)).astype(F32), counts)
         mix = jnp.where(same_block((channels, channels), size), 1.0, 0.0)
         all_count = jnp.sum(counts, axis=0, keepdims=True) * (2 * size)
 
@@ -506,18 +487,23 @@
         gap1 = stat[:, 2, :] / counts - mean
         spread = stat[:, 1, :] + stat[:, 3, :] + (gap0 * gap0 + gap1 * gap1) * counts
         var = grouped(jnp.sum(spread, axis=0, keepdims=True)) / all_count
-        mean_ref[...] = mean
-        scale_ref[...] = gain_ref[...] * lax.rsqrt(var + 1e-5)
+        scale = gain_ref[...] * lax.rsqrt(var + 1e-5)
+        mul_ref[...] = 0.5 * scale
+        add_ref[...] = 0.5 * (bias_ref[...] - mean * scale)
 
     live = valid_rows(step * frames, valid_ref[me], frames, rows)
-    mean, scale, bias = mean_ref[...], scale_ref[...], bias_ref[...]
+    mul, add = mul_ref[...], add_ref[...]
     here = pl.ds(pl.multiple_of(step * m, m), m)
+    cut = far0_ref.shape[1]
+    there = pl.ds(pl.multiple_of(step * m % cut, m), m)
+    late = step * m >= cut
     for y in range(2):
-        load(y, step).wait()
         line = 1 - odd if y == 0 else odd
         for b in range(2):
-            z = (plane_ref[y, b, here] - mean) * scale + bias
-            half = 0.5 * z
+            if y == 0:
+                half = near_ref[b, here] * mul + add
+            else:
+                half = jnp.where(late, far1_ref[b, there], far0_ref[b, there]) * mul + add
             z = jnp.where(live, half + half * jnp.tanh(half), 0.0)
             for c in range(channels // 128):
                 mix_ref[y, c, pl.ds(b, m, 2), :] = z[:, 128 * c : 128 * (c + 1)]
@@ -528,7 +514,7 @@
                 ].astype(BF)
 
 
-def norm(rows, me, valid, stat, counts, gain, bias, near_plane, far_plane):
+def norm(rows, me, valid, stat, gain, bias, near_plane, *far_planes):
     count, channels = near_plane.shape[1:]
     n = valid.shape[0]
     frames = 4
@@ -541,25 +527,23 @@
             grid=(n // frames,),
             in_specs=[
                 whole(*stat.shape),
-                whole(n, channels),
                 whole(1, channels),
                 whole(1, channels),
-                HBM,
-                HBM,
+                INSIDE,
+                INSIDE,
+                INSIDE,
             ],
             out_specs=pl.BlockSpec((frames, 2, 2 * rows, channels), lambda i, *_: (i, 0, 0, 0)),
             scratch_shapes=[
                 pltpu.VMEM((1, channels), F32),
                 pltpu.VMEM((1, channels), F32),
                 pltpu.VMEM((2, channels // 128, 2 * m, 128), F32),
-                pltpu.VMEM((2, 2, count, channels), F32),
-                pltpu.SemaphoreType.DMA((2, n // frames)),
             ],
         ),
         out_shape=jax.ShapeDtypeStruct((n, 2, 2 * rows, channels), BF),
-        compiler_params=params(VMEM),
+        compiler_params=params(24),
         cost_estimate=cost(32 * count * channels, 24 * count * channels, 4 * count * channels),
-    )(me, valid, stat, counts, gain.reshape(1, channels), bias.reshape(1, channels), near_plane, far_plane)
+    )(me, valid, stat, gain.reshape(1, channels), bias.reshape(1, channels), near_plane, *far_planes)
 
 
 def local(
@@ -604,22 +588,25 @@
         gate = got[0]
         buf = jnp.concatenate([buf] + got, axis=0)
         k *= 2 if len(ks) == 1 else 4
-    other = swap_by(buf, 1)
+    pieces = [buf, swap_by(buf, 1)]
     tile, _ = lax.optimization_barrier((tile, gate))
     inner = swap_by(tile, 1)
     ends = [(i, i + 1) for i in range(1, tiles - 1, 2)]
-    outer = swap(tile, ends + [(j, i) for i, j in ends])
+    ends = ends + [(j, i) for i, j in ends]
+    cut = count // 2
+    outer = [swap(tile[:cut], ends), swap(tile[cut:], ends)]
     near_plane, part, state, total, near_stat = near(
-        rows, me, group_map, valid_frames, buf, other, tile, inner, qkv_weight, out_weight, taps, head
+        rows, me, group_map, valid_frames, pieces, tile, inner, qkv_weight, out_weight, taps, head
     )
-    far_plane, stat = far(
-        rows, me, valid_frames, outer, state, total, part, near_stat, qkv_weight, out_weight, taps
-    )
+    stat, planes = jnp.zeros((8, channels), F32), []
+    for i, piece in enumerate(outer):
+        plane, stat = far(
+            rows, i * tiles // 2, me, valid_frames, piece, state, total, part, stat, near_stat,
+            qkv_weight, out_weight, taps,
+        )
+        planes.append(plane)
     stat = lax.all_to_all(stat, "tm", split_axis=0, concat_axis=0, tiled=True)
-    counts = jnp.broadcast_to(
-        (valid_frames * (2 * rows)).astype(F32)[:, None], (tiles, channels)
-    )
-    return norm(rows, me, valid_frames, stat, counts, norm_gain, norm_bias, near_plane, far_plane)
+    return norm(rows, me, valid_frames, stat, norm_gain, norm_bias, near_plane, *planes)
 
 
 def solution(mesh):

time: 96.1 us -> 90.4 us (0.941)
  blocking collectives: 0 us -> 16.3 us
  waiting for transfers between devices: 27.8 us -> 18.4 us
  starting transfers between devices: 24.6 us -> 17.4 us
  Pallas kernels: 38.2 us -> 32.5 us
    all_to_all x0 -> x1, blocking collectives: none -> 16.3 us  [local(): stat = lax.all_to_all(stat, 'tm', split_axis=0, concat_axis=0, tiled=True)]
    all_to_all x1 -> x0, waiting for transfers between devices: 7.92 us -> none  [local(): stat = lax.all_to_all(stat, 'tm', split_axis=0, concat_axis=0, tiled=True)]
    all_to_all x1 -> x0, starting transfers between devices: 7.23 us -> none  [local(): stat = lax.all_to_all(stat, 'tm', split_axis=0, concat_axis=0, tiled=True)]
    pallas_call x2 -> x3, Pallas kernels: 23.9 us -> 19.9 us  [the longest x1 11.4 us: near(): pl.pallas_call(functools.partial(near_kernel, rows, parts, frames), grid_...]
    pallas_call x1, Pallas kernels: 5.79 us -> 4.01 us  [norm(): pl.pallas_call(functools.partial(norm_kernel, rows, channels // NORM_GROU...]
    ppermute x7 -> x8, waiting for transfers between devices: 16.8 us -> 15.6 us  [swap(): return lax.ppermute(x, 'tm', pairs)]
    slice x0 -> x1, local copies, waits for them, and re-layouts: none -> 1.03 us  [local(): outer = [swap(tile[:cut], ends), swap(tile[cut:], ends)]]
    ppermute x7 -> x8, starting transfers between devices: 10 us -> 10 us  [swap(): return lax.ppermute(x, 'tm', pairs)]
  transfers between devices with their start and end apart: 9 -> 9, of which waited for: 6 -> 5; matrix products, arithmetic and copies ran while one was open for 4% -> 6% of each run, Pallas kernels for 21% -> 23%
where the time goes in v3:
time: 90.4 us; the launch traced here: 89.9 us
  Pallas kernels  32.5 us (36%)
  waiting for transfers between devices  18.4 us (20%)
  starting transfers between devices  17.4 us (19%)
  blocking collectives  16.3 us (18%)
  local copies, waits for them, and re-layouts  3.67 us (4%)
  other arithmetic  1.44 us (2%)
    all_to_all x1, blocking collectives, local(): stat = lax.all_to_all(stat, 'tm', split_axis=0, concat_axis=0, tiled=True)  16.3 us
    ppermute x8, waiting for transfers between devices, swap(): return lax.ppermute(x, 'tm', pairs)  15.6 us
    pallas_call x1, Pallas kernels, near(): pl.pallas_call(functools.partial(near_kernel, rows, parts, frames), grid_...  11.4 us
    ppermute x8, starting transfers between devices, swap(): return lax.ppermute(x, 'tm', pairs)  10 us
    pallas_call x2, Pallas kernels, far(): pl.pallas_call(functools.partial(far_kernel, rows, first, last), in_specs...  8.54 us
    all_to_all x1, starting transfers between devices, local(): lax.all_to_all(raster.reshape(tiles, rows, width), 'tm', split_axis=0, co...  7.39 us
    pallas_call x1, Pallas kernels, run_state(): pl.pallas_call(functools.partial(state_kernel, head), grid=(steps,), in_s...  4.92 us
    pallas_call x1, Pallas kernels, norm(): pl.pallas_call(functools.partial(norm_kernel, rows, channels // NORM_GROU...  4.01 us
  transfers between devices with their start and end apart: 9, of which 5 were waited for; matrix products, arithmetic and copies ran while one was open for 6% of the time, Pallas kernels for 23%

profile of v3, /device:TPU:0, one launch (start us, length us, event | category | flops | bytes accessed | tf_op | source)
XLA Modules:
  0.0 89.9 jit_solution(16956735502877777214)
XLA Ops:
  0.0 3.6 %shard_map.91 = bf16[1024,512]{1,0:T(8,128)(2,1)} custom-call(s32[1,1024]{1,0:T(1,128)} %bitcast.16, bf16[1024,512]{1,0:T(8,128)(2,1)} %tok_ref.3), custom_call_target="tpu_custom_call" | custom-call | flops 1073741824 | bytes 2097152 | tf_op jit(solution)/shard_map/pallas_call | solution.py:52
  3.6 7.4 %all-to-all-start = ((bf16[16,64,512]{2,1,0:T(8,128)(2,1)}), bf16[16,64,512]{2,1,0:T(8,128)(2,1)S(1)}, u32[]{:S(2)}, u32[]{:S(2)}) async-start(bf16[16,64,512]{2,1,0:T(8,128)(2,1)} %bitcast.15), calls=%async_computation | async-start | bytes 2097152 | tf_op jit(solution)/shard_map/all_to_all | solution.py:576
  11.0 4.9 %shard_map.92 = bf16[1,48,512]{2,1,0:T(8,128)(2,1)} custom-call(bf16[1024,512]{1,0:T(8,128)(2,1)} %tok_ref.3, bf16[512,1536]{1,0:T(8,128)(2,1)} %qkv_hbm.3, bf16[512,1536]{1,0:T(8,128)(2,1)} %qkv_hbm.3), custom_call_target="tpu_custom_call" | custom-call | flops 1073741824 | bytes 4194304 | tf_op jit(solution)/shard_map/pallas_call | solution.py:116
  16.0 1.9 %collective-permute-start = (bf16[1,48,512]{2,1,0:T(8,128)(2,1)}, bf16[1,48,512]{2,1,0:T(8,128)(2,1)S(1)}, u32[]{:S(2)}, u32[]{:S(2)}) collective-permute-start(bf16[1,48,512]{2,1,0:T(8,128)(2,1)} %shard_map.92), channel_id=1, source_target_pairs={{0,2},{1,3},{2,0},{3,1},{4,6},{5,7},{6,4},{7,5},{8,10},{9,11},{10,... | collective-permute-start | bytes 147464 | tf_op jit(solution)/shard_map/ppermute | solution.py:569
  17.9 3.0 %collective-permute-done = bf16[1,48,512]{2,1,0:T(8,128)(2,1)S(1)} collective-permute-done((bf16[1,48,512]{2,1,0:T(8,128)(2,1)}, bf16[1,48,512]{2,1,0:T(8,128)(2,1)S(1)}, u32[]{:S(2)}, u32[]{:S(2)}) %collective-permute-start) | collective-permute-done | bytes 49184 | tf_op jit(solution)/shard_map/ppermute | solution.py:569
  20.9 1.4 %pad_maximum_fusion = bf16[2,48,512]{2,1,0:T(8,128)(2,1)} fusion(bf16[1,48,512]{2,1,0:T(8,128)(2,1)S(1)} %collective-permute-done, bf16[1,48,512]{2,1,0:T(8,128)(2,1)} %shard_map.92), kind=kLoop, calls=%fused_computation | loop fusion | flops 49152 | bytes 196608 | tf_op jit(solution)/shard_map/concatenate | solution.py:589
  22.3 1.3 %collective-permute-start.1 = (bf16[2,48,512]{2,1,0:T(8,128)(2,1)}, bf16[2,48,512]{2,1,0:T(8,128)(2,1)S(1)}, u32[]{:S(2)}, u32[]{:S(2)}) collective-permute-start(bf16[2,48,512]{2,1,0:T(8,128)(2,1)} %pad_maximum_fusion), channel_id=1, source_target_pairs={{0,4},{1,5},{2,6},{3,7},{4,0},{5,1},{6,2},{7,3},{8,12},{9,13},{10,... | collective-permute-start | bytes 294920 | tf_op jit(solution)/shard_map/ppermute | solution.py:569
  23.6 0.8 constant_dynamic-update-slice_fusion.4
  24.4 3.1 %collective-permute-start.3 = (bf16[2,48,512]{2,1,0:T(8,128)(2,1)}, bf16[2,48,512]{2,1,0:T(8,128)(2,1)}, u32[]{:S(2)}, u32[]{:S(2)}) collective-permute-start(bf16[2,48,512]{2,1,0:T(8,128)(2,1)} %pad_maximum_fusion), channel_id=1, source_target_pairs={{0,8},{1,9},{2,10},{3,11},{4,12},{5,13},{6,14},{7,15},{8,0},{9,1},... | collective-permute-start | bytes 294920 | tf_op jit(solution)/shard_map/ppermute | solution.py:569
  27.7 3.8 %collective-permute-done.1 = bf16[2,48,512]{2,1,0:T(8,128)(2,1)S(1)} collective-permute-done((bf16[2,48,512]{2,1,0:T(8,128)(2,1)}, bf16[2,48,512]{2,1,0:T(8,128)(2,1)S(1)}, u32[]{:S(2)}, u32[]{:S(2)}) %collective-permute-start.1) | collective-permute-done | bytes 98336 | tf_op jit(solution)/shard_map/ppermute | solution.py:569
  31.5 2.8 %all-to-all-done = bf16[16,64,512]{2,1,0:T(8,128)(2,1)S(1)} async-done(((bf16[16,64,512]{2,1,0:T(8,128)(2,1)}), bf16[16,64,512]{2,1,0:T(8,128)(2,1)S(1)}, u32[]{:S(2)}, u32[]{:S(2)}) %all-to-all-start) | async-done | bytes 1048608 | tf_op jit(solution)/shard_map/all_to_all | solution.py:576
  34.6 1.0 %fusion = (bf16[512,512]{1,0:T(8,128)(2,1)}, bf16[512,512]{1,0:T(8,128)(2,1)}) fusion(bf16[1024,512]{1,0:T(8,128)(2,1)S(1)} %bitcast.8), kind=kLoop, calls=%fused_computation.6 | loop fusion | bytes 2097152 | tf_op jit(solution)/shard_map/slice | solution.py:597
  35.6 0.7 collective-permute-start.7
  36.3 0.9 collective-permute-start.2
  37.2 7.3 %collective-permute-done.3 = bf16[2,48,512]{2,1,0:T(8,128)(2,1)} collective-permute-done((bf16[2,48,512]{2,1,0:T(8,128)(2,1)}, bf16[2,48,512]{2,1,0:T(8,128)(2,1)}, u32[]{:S(2)}, u32[]{:S(2)}) %collective-permute-start.3) | collective-permute-done | bytes 98336 | tf_op jit(solution)/shard_map/ppermute | solution.py:569
  44.5 0.9 %constant_dynamic-update-slice_fusion.1 = bf16[8,48,512]{2,1,0:T(8,128)(2,1)S(1)} fusion(bf16[8,48,512]{2,1,0:T(8,128)(2,1)S(1)} %constant_dynamic-update-slice_fusion.2, bf16[2,48,512]{2,1,0:T(8,128)(2,1)} %collective-permute-done.3), kind=kLoop, calls=%fused_computation.2 | loop fusion | bytes 196608
  45.4 0.9 %constant_dynamic-update-slice_fusion.refs_0_ = bf16[8,48,512]{2,1,0:T(8,128)(2,1)S(1)} fusion(bf16[8,48,512]{2,1,0:T(8,128)(2,1)S(1)} %constant_dynamic-update-slice_fusion.1, bf16[2,48,512]{2,1,0:T(8,128)(2,1)} %collective-permute-done.4), kind=kLoop, calls=%fused_computation.1 | loop fusion | bytes 196608 | tf_op jit(solution)/shard_map/concatenate | solution.py:589
  46.3 1.7 %collective-permute-start.5 = (bf16[8,48,512]{2,1,0:T(8,128)(2,1)S(1)}, bf16[8,48,512]{2,1,0:T(8,128)(2,1)}, u32[]{:S(2)}, u32[]{:S(2)}) collective-permute-start(bf16[8,48,512]{2,1,0:T(8,128)(2,1)S(1)} %constant_dynamic-update-slice_fusion.refs_0_), channel_id=1, source_target_pairs={{0,1},{1,0},{2,3},{3,2},{4,5},{5,4},{6,7},{7,6},{8,9},{9,8},{10,11... | collective-permute-start | bytes 1179656 | tf_op jit(solution)/shard_map/ppermute | solution.py:569
  48.0 1.5 %collective-permute-done.5.refs_1_ = bf16[8,48,512]{2,1,0:T(8,128)(2,1)} collective-permute-done((bf16[8,48,512]{2,1,0:T(8,128)(2,1)S(1)}, bf16[8,48,512]{2,1,0:T(8,128)(2,1)}, u32[]{:S(2)}, u32[]{:S(2)}) %collective-permute-start.5) | collective-permute-done | bytes 393248 | tf_op jit(solution)/shard_map/ppermute | solution.py:569
  49.5 11.4 %shard_map.93 = (f32[2,1024,256]{2,1,0:T(8,128)S(1)}, f32[2,1024,256]{2,1,0:T(8,128)S(1)}, bf16[16,32,512]{2,1,0:T(8,128)(2,1)S(1)}, f32[16,8,512]{2,1,0:T(8,128)S(1)}, f32[8,256]{1,0:T(8,128)S(1)}) custom-call(s32[1]{0:T(128)} %bitcast.pos_ref, s32[16]{0:T(128)S(1)} %copy-done.3, s32[16]{0:T(128)S(1)} %copy-done, ...), custom_call_target="tpu_custom_call" | custom-call | flops 1 | bytes 1 | tf_op jit(solution)/shard_map/pallas_call | solution.py:340
  60.9 4.3 %shard_map.94 = (f32[2,512,256]{2,1,0:T(8,128)S(1)}, f32[8,256]{1,0:T(8,128)S(1)}) custom-call(s32[1]{0:T(128)} %bitcast.pos_ref, s32[16]{0:T(128)S(1)} %copy-done, bf16[512,512]{1,0:T(8,128)(2,1)S(1)} %collective-permute-done.7.outer_any, bf16[16,32,512]{2,1,0:T(8,128)(2,1)S(1)} %get-tuple-element.16.state_ref, ...), custom_call_target="tpu_custom_call" | custom-call | flops 1 | bytes 1 | tf_op jit(solution)/shard_map/pallas_call | solution.py:440
  65.2 4.3 %shard_map.95 = (f32[2,512,256]{2,1,0:T(8,128)S(1)}, f32[16,8,256]{2,1,0:T(8,128)S(1)}) custom-call(s32[1]{0:T(128)} %bitcast.pos_ref, s32[16]{0:T(128)S(1)} %copy-done, bf16[512,512]{1,0:T(8,128)(2,1)S(1)} %collective-permute-done.2.outer_any, bf16[16,32,512]{2,1,0:T(8,128)(2,1)S(1)} %get-tuple-element.16.state_ref, ...), custom_call_target="tpu_custom_call" | custom-call | flops 1 | bytes 1 | tf_op jit(solution)/shard_map/pallas_call | solution.py:440
  69.5 16.3 %all_to_all.10.stat_ref = f32[16,8,256]{2,1,0:T(8,128)S(1)} all-to-all(f32[16,8,256]{2,1,0:T(8,128)S(1)} %get-tuple-element.21), channel_id=1, replica_groups=mesh['clip'=2,'tm'=16] {'tm'}, dimensions={0} | all-to-all | bytes 262144 | tf_op jit(solution)/shard_map/all_to_all | solution.py:608
  85.8 4.0 %shard_map.96 = bf16[16,2,128,256]{3,2,1,0:T(8,128)(2,1)} custom-call(s32[1]{0:T(128)} %bitcast.pos_ref, s32[16]{0:T(128)S(1)} %copy-done, f32[16,8,256]{2,1,0:T(8,128)S(1)} %all_to_all.10.stat_ref, f32[1,256]{1,0:T(1,128)S(1)} %bitcast.10, f32[1,256]{1,0:T(1,128)S(1)} %bitcast.11, f32[2,1024,256]{2,1,0:T(8,128)S(1)} %get-tuple-element.22.near_ref, ...), custom_call_target="tpu_custom_call" | custom-call | flops 8388608 | bytes 6291456 | tf_op jit(solution)/shard_map/pallas_call | solution.py:523
  (17 shorter events, 0.4 us)
Async XLA Ops:
  3.6 30.7 %all-to-all-start = ((bf16[16,64,512]{2,1,0:T(8,128)(2,1)}), bf16[16,64,512]{2,1,0:T(8,128)(2,1)S(1)}, u32[]{:S(2)}, u32[]{:S(2)}) async-start(bf16[16,64,512]{2,1,0:T(8,128)(2,1)} %bitcast.15), calls=%async_computation | async-start | bytes 2097152 | tf_op jit(solution)/shard_map/all_to_all | solution.py:576
  15.9 33.6 %copy-start = (s32[16]{0:T(128)S(1)}, s32[16]{0:T(128)}, u32[]{:S(2)}) copy-start(s32[16]{0:T(128)} %valid_ref.7) | copy-start | bytes 196
  16.0 33.6 %copy-start.3 = (s32[16]{0:T(128)S(1)}, s32[16]{0:T(128)}, u32[]{:S(2)}) copy-start(s32[16]{0:T(128)} %group_ref.1) | copy-start | bytes 196
  16.0 4.9 %collective-permute-start = (bf16[1,48,512]{2,1,0:T(8,128)(2,1)}, bf16[1,48,512]{2,1,0:T(8,128)(2,1)S(1)}, u32[]{:S(2)}, u32[]{:S(2)}) collective-permute-start(bf16[1,48,512]{2,1,0:T(8,128)(2,1)} %shard_map.92), channel_id=1, source_target_pairs={{0,2},{1,3},{2,0},{3,1},{4,6},{5,7},{6,4},{7,5},{8,10},{9,11},{10,... | collective-permute-start | bytes 147464 | tf_op jit(solution)/shard_map/ppermute | solution.py:569
  22.3 9.2 %collective-permute-start.1 = (bf16[2,48,512]{2,1,0:T(8,128)(2,1)}, bf16[2,48,512]{2,1,0:T(8,128)(2,1)S(1)}, u32[]{:S(2)}, u32[]{:S(2)}) collective-permute-start(bf16[2,48,512]{2,1,0:T(8,128)(2,1)} %pad_maximum_fusion), channel_id=1, source_target_pairs={{0,4},{1,5},{2,6},{3,7},{4,0},{5,1},{6,2},{7,3},{8,12},{9,13},{10,... | collective-permute-start | bytes 294920 | tf_op jit(solution)/shard_map/ppermute | solution.py:569
  24.4 20.0 %collective-permute-start.3 = (bf16[2,48,512]{2,1,0:T(8,128)(2,1)}, bf16[2,48,512]{2,1,0:T(8,128)(2,1)}, u32[]{:S(2)}, u32[]{:S(2)}) collective-permute-start(bf16[2,48,512]{2,1,0:T(8,128)(2,1)} %pad_maximum_fusion), channel_id=1, source_target_pairs={{0,8},{1,9},{2,10},{3,11},{4,12},{5,13},{6,14},{7,15},{8,0},{9,1},... | collective-permute-start | bytes 294920 | tf_op jit(solution)/shard_map/ppermute | solution.py:569
  27.6 17.8 %collective-permute-start.4 = (bf16[2,48,512]{2,1,0:T(8,128)(2,1)}, bf16[2,48,512]{2,1,0:T(8,128)(2,1)}, u32[]{:S(2)}, u32[]{:S(2)}) collective-permute-start(bf16[2,48,512]{2,1,0:T(8,128)(2,1)} %pad_maximum_fusion), channel_id=1, source_target_pairs={{0,12},{1,13},{2,14},{3,15},{4,8},{5,9},{6,10},{7,11},{8,4},{9,5},... | collective-permute-start | bytes 294920 | tf_op jit(solution)/shard_map/ppermute | solution.py:569
  34.3 15.2 %collective-permute-start.6 = (bf16[1024,512]{1,0:T(8,128)(2,1)S(1)}, bf16[1024,512]{1,0:T(8,128)(2,1)S(1)}, u32[]{:S(2)}, u32[]{:S(2)}) collective-permute-start(bf16[1024,512]{1,0:T(8,128)(2,1)S(1)} %bitcast.7), channel_id=1, source_target_pairs={{0,1},{1,0},{2,3},{3,2},{4,5},{5,4},{6,7},{7,6},{8,9},{9,8},{10,11... | collective-permute-start | bytes 3145736 | tf_op jit(solution)/shard_map/ppermute | solution.py:569
  35.6 25.3 %collective-permute-start.7 = (bf16[512,512]{1,0:T(8,128)(2,1)}, bf16[512,512]{1,0:T(8,128)(2,1)S(1)}, u32[]{:S(2)}, u32[]{:S(2)}) collective-permute-start(bf16[512,512]{1,0:T(8,128)(2,1)} %get-tuple-element.25), channel_id=1, source_target_pairs={{1,2},{3,4},{5,6},{7,8},{9,10},{11,12},{13,14},{2,1},{4,3},{6,5},{... | collective-permute-start | bytes 1572872 | tf_op jit(solution)/shard_map/ppermute | solution.py:569
  36.3 28.9 %collective-permute-start.2 = (bf16[512,512]{1,0:T(8,128)(2,1)}, bf16[512,512]{1,0:T(8,128)(2,1)S(1)}, u32[]{:S(2)}, u32[]{:S(2)}) collective-permute-start(bf16[512,512]{1,0:T(8,128)(2,1)} %get-tuple-element.26), channel_id=1, source_target_pairs={{1,2},{3,4},{5,6},{7,8},{9,10},{11,12},{13,14},{2,1},{4,3},{6,5},{... | collective-permute-start | bytes 1572872 | tf_op jit(solution)/shard_map/ppermute | solution.py:569
  46.3 3.2 %collective-permute-start.5 = (bf16[8,48,512]{2,1,0:T(8,128)(2,1)S(1)}, bf16[8,48,512]{2,1,0:T(8,128)(2,1)}, u32[]{:S(2)}, u32[]{:S(2)}) collective-permute-start(bf16[8,48,512]{2,1,0:T(8,128)(2,1)S(1)} %constant_dynamic-update-slice_fusion.refs_0_), channel_id=1, source_target_pairs={{0,1},{1,0},{2,3},{3,2},{4,5},{5,4},{6,7},{7,6},{8,9},{9,8},{10,11... | collective-permute-start | bytes 1179656 | tf_op jit(solution)/shard_map/ppermute | solution.py:569
  65.2 20.6 %copy-start.1 = (f32[256]{0:T(256)S(1)}, f32[256]{0:T(256)}, u32[]{:S(2)}) copy-start(f32[256]{0:T(256)} %param.13) | copy-start | bytes 3076
  65.2 20.6 %copy-start.2 = (f32[256]{0:T(256)S(1)}, f32[256]{0:T(256)}, u32[]{:S(2)}) copy-start(f32[256]{0:T(256)} %param.14) | copy-start | bytes 3076

commit v4 on v3

--- a/solution.py
+++ b/solution.py
@@ -13,6 +13,9 @@
 F32 = jnp.float32
 MIB = 1024 * 1024
 VMEM = 60
+HBM = pl.BlockSpec(memory_space=pltpu.HBM)
+ANY = pl.BlockSpec(memory_space=pl.ANY)
+INSIDE = pl.BlockSpec(memory_space=pltpu.VMEM)
 
 
 def dot(a, b, **kw):
@@ -35,37 +38,89 @@
     return rows == cols
 
 
-def permute_kernel(order_ref, tok_ref, out_ref, pick_ref):
-    count = tok_ref.shape[0]
-
-    @pl.when(pl.program_id(0) == 0)
-    def _():
-        place = lax.broadcasted_iota(jnp.int32, (count, count), 0)
-        pick_ref[...] = jnp.where(place == order_ref[...], 1.0, 0.0).astype(BF)
-
-    out_ref[...] = dot(pick_ref[...], tok_ref[...]).astype(BF)
+def permute_kernel(order_any, tok_any, out_any, order_ref, tok_ref, pick_ref, out_ref, sems):
+    count, width = tok_ref.shape
+    parts = sems.shape[0] - 2
+    rows = count // parts
+    loads = [
+        pltpu.make_async_copy(order_any, order_ref, sems.at[0]),
+        pltpu.make_async_copy(tok_any, tok_ref, sems.at[1]),
+    ]
+    for copy in loads:
+        copy.start()
+    loads[0].wait()
+    place = lax.broadcasted_iota(jnp.int32, (count, count), 0)
+    pick_ref[...] = jnp.where(place == order_ref[...], 1.0, 0.0).astype(BF)
+    loads[1].wait()
+    stores = []
+    for i in range(parts):
+        cut = pl.ds(i * rows, rows)
+        out_ref[cut] = dot(pick_ref[cut], tok_ref[...]).astype(BF)
+        stores.append(pltpu.make_async_copy(out_ref.at[cut], out_any.at[cut], sems.at[2 + i]))
+        stores[-1].start()
+    for copy in stores:
+        copy.wait()
 
 
 def permute(order, tokens):
     count, width = tokens.shape
-    block = 256
+    parts = 4
     return pl.pallas_call(
         permute_kernel,
-        grid=(width // block,),
-        in_specs=[
-            pl.BlockSpec((1, count), lambda i: (0, 0)),
-            pl.BlockSpec((count, block), lambda i: (0, i)),
+        in_specs=[HBM, HBM],
+        out_specs=HBM,
+        out_shape=pltpu.HBM((count, width), BF),
+        scratch_shapes=[
+            pltpu.VMEM((1, count), jnp.int32),
+            pltpu.VMEM((count, width), BF),
+            pltpu.VMEM((count, count), BF),
+            pltpu.VMEM((count, width), BF),
+            pltpu.SemaphoreType.DMA((2 + parts,)),
         ],
-        out_specs=pl.BlockSpec((count, block), lambda i: (0, i)),
-        out_shape=jax.ShapeDtypeStruct((count, width), BF),
-        scratch_shapes=[pltpu.VMEM((count, count), BF)],
-        compiler_params=params(VMEM),
+        compiler_params=pltpu.CompilerParams(vmem_limit_bytes=60 * MIB),
         cost_estimate=cost(2 * count * count * width, 4 * count * width),
     )(order.reshape(1, count), tokens)
 
 
-def state_kernel(head, tok_ref, wk_ref, wv_ref, out_ref, acc_ref, sum_ref):
+def chunk(src, dst, step, m, sem):
+    at = pl.ds(pl.multiple_of(step * m, m), m)
+    return pltpu.make_async_copy(src.at[at], dst.at[at], sem.at[step])
+
+
+def spread_row(src, row, dst, sems):
+    deep, channels = dst.shape[0] * 3 // 4, dst.shape[1] // 2
+    part = src.at[pl.ds(pl.multiple_of(row * deep, deep), deep), :]
+    return [
+        pltpu.make_async_copy(part, dst.at[:deep, :channels], sems.at[0]),
+        pltpu.make_async_copy(part, dst.at[channels:, channels:], sems.at[1]),
+    ]
+
+
+def clear_spread(dst):
+    channels = dst.shape[1] // 2
+    gap = jnp.zeros((channels, channels), BF)
+    dst[3 * channels :, :channels] = gap
+    dst[:channels, channels:] = gap
+
+
+def state_kernel(
+    head, pos_ref, tok_ref, wk_ref, wv_ref, qkv_hbm, wo_hbm, taps_hbm,
+    out_ref, wq_ref, wo_ref, w2_ref, wx_ref,
+    acc_ref, sum_ref, sems,
+):
     step = pl.program_id(0)
+    odd = jnp.bitwise_and(pos_ref[0], 1)
+    channels = taps_hbm.shape[1]
+    row = 3 * channels
+    first_half = taps_hbm.at[pl.ds(pl.multiple_of(odd * row, row), 2 * row), :]
+    second_half = taps_hbm.at[pl.ds(pl.multiple_of((1 - odd) * row, row), 2 * row), :]
+    staged = [
+        pltpu.make_async_copy(qkv_hbm.at[:, pl.ds(0, wq_ref.shape[1])], wq_ref, sems.at[0]),
+        pltpu.make_async_copy(wo_hbm, wo_ref, sems.at[1]),
+        pltpu.make_async_copy(first_half, w2_ref.at[:, :channels], sems.at[2]),
+        pltpu.make_async_copy(second_half, w2_ref.at[:, channels:], sems.at[3]),
+    ]
+    staged += spread_row(taps_hbm, 2 * odd, wx_ref, sems.at[pl.ds(4, 2)])
     width = tok_ref.shape[1]
     block = acc_ref.shape[1]
 
@@ -73,6 +128,9 @@
     def _():
         acc_ref[...] = jnp.zeros_like(acc_ref)
         sum_ref[...] = jnp.zeros_like(sum_ref)
+        for copy in staged:
+            copy.start()
+        clear_spread(wx_ref)
 
     tok = tok_ref[...]
     keys = jnp.maximum(dot(tok, wk_ref[...]), 0.0)
@@ -95,41 +153,63 @@
             for h in range(1, block // head):
                 small = small + full[h * head : (h + 1) * head]
             parts.append(small)
+        state = jnp.concatenate(parts, axis=1)
         total = sum_ref[0:1, :]
         high = total.astype(BF).astype(F32)
         low = total - high
-        out_ref[0] = jnp.concatenate(
-            [
-                jnp.concatenate(parts, axis=1),
-                high,
-                low,
-                jnp.zeros((out_ref.shape[1] - head - 2, width), F32),
-            ],
-            axis=0,
-        ).astype(BF)
-
-
-def run_state(tokens, qkv_weight, head):
+        lines = [row[:, 128 * i : 128 * (i + 1)] for row in (high, low) for i in range(width // 128)]
+        rows = out_ref.shape[1]
+        lines.append(jnp.zeros((rows - len(lines), 128), F32))
+        cuts = [state[i : i + rows] for i in range(0, head, rows)]
+        for copy in staged:
+            copy.wait()
+        out_ref[0] = jnp.concatenate(cuts + [jnp.concatenate(lines, axis=0)], axis=1).astype(BF)
+
+
+def unpack(packed, head, width):
+    rows = packed.shape[0]
+    cuts = head // rows
+    state = jnp.concatenate([packed[:, i * width : (i + 1) * width] for i in range(cuts)], axis=0)
+    tail = packed[:, cuts * width :]
+    lines = width // 128
+    both = tail[:lines] + tail[lines : 2 * lines]
+    return state, jnp.concatenate([both[i : i + 1] for i in range(lines)], axis=1)
+
+
+def run_state(me, tokens, qkv_weight, out_weight, taps, head):
     count, width = tokens.shape
     steps, block = 4, 256
-    rows = head + 16
+    rows = 16
+    packed = head // rows * width + 128
+    channels = taps.shape[1]
     return pl.pallas_call(
         functools.partial(state_kernel, head),
         grid=(steps,),
         in_specs=[
+            pl.BlockSpec(memory_space=pltpu.SMEM),
             pl.BlockSpec((count // steps, width), lambda i: (i, 0)),
             pl.BlockSpec((width, width), lambda i: (0, 1)),
             pl.BlockSpec((width, width), lambda i: (0, 2)),
+            HBM,
+            HBM,
+            HBM,
         ],
-        out_specs=pl.BlockSpec((1, rows, width), lambda i: (0, 0, 0)),
-        out_shape=jax.ShapeDtypeStruct((1, rows, width), BF),
+        out_specs=[pl.BlockSpec((1, rows, packed), lambda i: (0, 0, 0))] + [INSIDE] * 4,
+        out_shape=[
+            jax.ShapeDtypeStruct((1, rows, packed), BF),
+            pltpu.VMEM((width, width), BF),
+            pltpu.VMEM(out_weight.shape, BF),
+            pltpu.VMEM((6 * channels, 2 * channels), BF),
+            pltpu.VMEM((4 * channels, 2 * channels), BF),
+        ],
         scratch_shapes=[
             pltpu.VMEM((width // block, block, block), F32),
             pltpu.VMEM((8, width), F32),
+            pltpu.SemaphoreType.DMA((6,)),
         ],
-        compiler_params=params(VMEM),
+        compiler_params=params(16),
         cost_estimate=cost(4 * count * width * width, 8 * count * width),
-    )(tokens, qkv_weight, qkv_weight)
+    )(me, tokens, qkv_weight, qkv_weight, qkv_weight, out_weight, taps)
 
 
 def queries(tok, wq):
@@ -157,32 +237,6 @@
     return frame < limit
 
 
-HBM = pl.BlockSpec(memory_space=pltpu.HBM)
-ANY = pl.BlockSpec(memory_space=pl.ANY)
-INSIDE = pl.BlockSpec(memory_space=pltpu.VMEM)
-
-
-def chunk(src, dst, step, m, sem):
-    at = pl.ds(pl.multiple_of(step * m, m), m)
-    return pltpu.make_async_copy(src.at[at], dst.at[at], sem.at[step])
-
-
-def spread_row(src, row, dst, sems):
-    deep, channels = dst.shape[0] * 3 // 4, dst.shape[1] // 2
-    part = src.at[pl.ds(pl.multiple_of(row * deep, deep), deep), :]
-    return [
-        pltpu.make_async_copy(part, dst.at[:deep, :channels], sems.at[0]),
-        pltpu.make_async_copy(part, dst.at[channels:, channels:], sems.at[1]),
-    ]
-
-
-def clear_spread(dst):
-    channels = dst.shape[1] // 2
-    gap = jnp.zeros((channels, channels), BF)
-    dst[3 * channels :, :channels] = gap
-    dst[:channels, channels:] = gap
-
-
 def store_taps(x_ref, at, line, rows):
     m, channels = line.shape[0], line.shape[1] // 2
     column = lax.broadcasted_iota(jnp.int32, (m, 1), 0) % rows
@@ -222,10 +276,11 @@
     rows, parts, frames, pos_ref, group_ref, valid_ref, *refs
 ):
     pieces, refs = refs[: 2 * parts], refs[2 * parts :]
-    own_any, inner_any, qkv_hbm, wo_hbm, taps_hbm, *refs = refs
+    own_any, inner_any, wq_ref, wo_ref, w2_ref, taps_hbm, *refs = refs
     near_ref, part_ref, state_ref, total_ref, stat_ref, *refs = refs
-    acc_ref, pend_ref, att_ref, x_ref, w2_ref, w1_ref, wq_ref, wo_ref, *refs = refs
-    own_ref, inner_ref, buf_ref, own_sem, inner_sem, sems, piece_sem = refs
+    acc_ref, pend_ref, att_ref, x_ref, w1_ref, own_ref, inner_ref, buf_ref, *refs = refs
+    own_sem, inner_sem, piece_sem, sems = refs
+    late = spread_row(taps_hbm, 2 - 2 * jnp.bitwise_and(pos_ref[0], 1), w1_ref, sems)
     step = pl.program_id(0)
     count, width = own_ref.shape
     m = frames * rows
@@ -234,16 +289,6 @@
     odd = jnp.bitwise_and(me, 1)
     head = state_ref.shape[1]
     channels = near_ref.shape[2]
-    row = 3 * channels
-    first_half = taps_hbm.at[pl.ds(pl.multiple_of(odd * row, row), 2 * row), :]
-    second_half = taps_hbm.at[pl.ds(pl.multiple_of((1 - odd) * row, row), 2 * row), :]
-    query_copy = pltpu.make_async_copy(qkv_hbm.at[:, pl.ds(0, width)], wq_ref, sems.at[0])
-    late = [
-        pltpu.make_async_copy(wo_hbm, wo_ref, sems.at[1]),
-        pltpu.make_async_copy(first_half, w2_ref.at[:, :channels], sems.at[2]),
-        pltpu.make_async_copy(second_half, w2_ref.at[:, channels:], sems.at[3]),
-    ] + spread_row(taps_hbm, 2 * (1 - odd), w1_ref, sems.at[pl.ds(4, 2)])
-
     size = pieces[0].shape[0]
     fetch = [
         pltpu.make_async_copy(
@@ -254,20 +299,17 @@
 
     @pl.when(step == 0)
     def _():
-        query_copy.start()
         for copy in fetch:
             copy.start()
         for i in range(steps):
             chunk(own_any, own_ref, i, m, own_sem).start()
             chunk(inner_any, inner_ref, i, m, inner_sem).start()
-            if i == 0:
-                for copy in late:
-                    copy.start()
+        for copy in late:
+            copy.start()
+        clear_spread(w1_ref)
         acc_ref[...] = jnp.zeros_like(acc_ref)
         pend_ref[...] = jnp.zeros_like(pend_ref)
-        clear_spread(w1_ref)
         stat_ref[...] = jnp.zeros_like(stat_ref)
-        query_copy.wait()
         for copy in fetch:
             copy.wait()
 
@@ -291,8 +333,8 @@
         acc_ref[...] = acc
         pend_ref[...] = (1.0 - fresh) * pend + piece
         summed = acc + piece
-        state = summed[:head].astype(BF)
-        total = summed[head : head + 1] + summed[head + 1 : head + 2]
+        state, total = unpack(summed, head, width)
+        state = state.astype(BF)
         state_ref[frame] = state
         total_ref[frame] = jnp.broadcast_to(total, (8, width))
         cut = slice(i * rows, (i + 1) * rows)
@@ -310,7 +352,7 @@
         for copy in late:
             copy.wait()
 
-    half = 2 * channels
+    half, row = 2 * channels, 3 * channels
     mine = jnp.where(keep_own, dot(att_ref[0].astype(BF), wo_ref[...]), 0.0)
     w_close = wo_ref[:, pl.ds(pl.multiple_of(odd * half, half), half)]
     close = jnp.where(keep_inner, dot(att_ref[1].astype(BF), w_close), 0.0)
@@ -328,38 +370,33 @@
     part_ref[1, here] = pair[m:, channels:]
 
 
-def near(rows, me, group_map, valid, pieces, own, inner, qkv_weight, out_weight, taps, head):
+def near(rows, me, group_map, valid, pieces, own, inner, weights, channels, head):
     count, width = own.shape
     frames = 16
     n = count // rows
-    wide = out_weight.shape[1]
-    channels = taps.shape[1]
     m = frames * rows
-    deep = pieces[0].shape[1]
+    deep, packed = pieces[0].shape[1:]
     parts = len(pieces) // 2
     return pl.pallas_call(
         functools.partial(near_kernel, rows, parts, frames),
         grid_spec=pltpu.PrefetchScalarGridSpec(
             num_scalar_prefetch=3,
             grid=(n // frames,),
-            in_specs=[ANY] * (2 * parts + 2) + [HBM] * 3,
+            in_specs=[ANY] * (2 * parts + 2) + [INSIDE] * 3 + [HBM],
             out_specs=[INSIDE] * 5,
             scratch_shapes=[
-                pltpu.VMEM((deep, width), F32),
-                pltpu.VMEM((deep, width), F32),
+                pltpu.VMEM((deep, packed), F32),
+                pltpu.VMEM((deep, packed), F32),
                 pltpu.VMEM((2, m, width), F32),
                 pltpu.VMEM((2 * m, 6 * channels), BF),
-                pltpu.VMEM((6 * channels, 2 * channels), BF),
                 pltpu.VMEM((4 * channels, 2 * channels), BF),
-                pltpu.VMEM((width, width), BF),
-                pltpu.VMEM((width, wide), BF),
                 pltpu.VMEM((count, width), BF),
                 pltpu.VMEM((count, width), BF),
-                pltpu.VMEM((2, n // 2, deep, width), BF),
+                pltpu.VMEM((2, n // 2, deep, packed), BF),
                 pltpu.SemaphoreType.DMA((n // frames,)),
                 pltpu.SemaphoreType.DMA((n // frames,)),
-                pltpu.SemaphoreType.DMA((6,)),
                 pltpu.SemaphoreType.DMA((2 * parts,)),
+                pltpu.SemaphoreType.DMA((2,)),
             ],
         ),
         out_shape=[
@@ -369,16 +406,16 @@
             pltpu.VMEM((n, 8, width), F32),
             pltpu.VMEM((8, channels), F32),
         ],
-        compiler_params=params(40),
+        compiler_params=params(32),
         cost_estimate=cost(1, 1),
-    )(me, group_map, valid, *pieces, own, inner, qkv_weight, out_weight, taps)
+    )(me, group_map, valid, *pieces, own, inner, *weights)
 
 
 def far_kernel(
     rows, first, last, pos_ref, valid_ref,
-    outer_any, state_ref, total_ref, part_ref, before_ref, near_stat_ref, qkv_hbm, wo_hbm, taps_hbm,
+    outer_any, state_ref, total_ref, part_ref, before_ref, near_stat_ref, wq_ref, wo_ref, wx_ref,
     far_ref, stat_ref,
-    wx_ref, att_ref, run_ref, wq_ref, wo_ref, outer_ref, sems,
+    att_ref, run_ref, outer_ref, sem,
 ):
     m, width = outer_ref.shape
     channels = far_ref.shape[2]
@@ -388,20 +425,13 @@
     head = state_ref.shape[1]
     half = 2 * channels
     half_at = pl.ds(pl.multiple_of((1 - odd) * half, half), half)
-    copies = [
-        pltpu.make_async_copy(qkv_hbm.at[:, pl.ds(0, width)], wq_ref, sems.at[0]),
-        pltpu.make_async_copy(outer_any, outer_ref, sems.at[1]),
-        pltpu.make_async_copy(wo_hbm.at[:, half_at], wo_ref, sems.at[2]),
-    ] + spread_row(taps_hbm, 2 * odd, wx_ref, sems.at[pl.ds(3, 2)])
-    for copy in copies:
-        copy.start()
-    clear_spread(wx_ref)
+    copy = pltpu.make_async_copy(outer_any, outer_ref, sem)
+    copy.start()
     run_ref[...] = before_ref[...]
     block = 256
     own = same_block((block, block), head)
     ones = jnp.where(own, 1.0, 0.0).astype(BF)
-    copies[0].wait()
-    copies[1].wait()
+    copy.wait()
     qf = queries(outer_ref[...], wq_ref[...])
     for i in range(frames):
         cut = slice(i * rows, (i + 1) * rows)
@@ -409,9 +439,7 @@
         att_ref[cut] = attend(qf[cut], state_ref[frame], total_ref[frame][0:1], own, ones)
     outer_at = jnp.clip(me + 2 * odd - 1, 0, valid_ref.shape[0] - 1)
     keep = valid_rows(first, valid_ref[outer_at], frames, rows)
-    for copy in copies[2:]:
-        copy.wait()
-    line = jnp.where(keep, dot(att_ref[...].astype(BF), wo_ref[...]), 0.0)
+    line = jnp.where(keep, dot(att_ref[...].astype(BF), wo_ref[:, half_at]), 0.0)
     more = dot(line_taps(line, rows), wx_ref[...])
     more = jnp.concatenate([more[:, :channels], more[:, channels:]], axis=0)
     limit = valid_ref[me]
@@ -430,30 +458,27 @@
         stat_ref[...] = run_ref[...]
 
 
-def far(rows, first, me, valid, outer, state, total, part, before, near_stat, qkv_weight, out_weight, taps):
+def far(rows, first, me, valid, outer, state, total, part, before, near_stat, weights):
     m, width = outer.shape
-    channels = taps.shape[1]
+    channels = part.shape[2]
     n = state.shape[0]
     last = first + m // rows == n
     smem = pl.BlockSpec(memory_space=pltpu.SMEM)
     stat = jax.ShapeDtypeStruct((n, 8, channels), F32) if last else pltpu.VMEM((8, channels), F32)
     return pl.pallas_call(
         functools.partial(far_kernel, rows, first, last),
-        in_specs=[smem, smem, ANY] + [INSIDE] * 5 + [HBM] * 3,
+        in_specs=[smem, smem, ANY] + [INSIDE] * 8,
         out_specs=[INSIDE, INSIDE],
         scratch_shapes=[
-            pltpu.VMEM((4 * channels, 2 * channels), BF),
             pltpu.VMEM((m, width), F32),
             pltpu.VMEM((8, channels), F32),
-            pltpu.VMEM((width, width), BF),
-            pltpu.VMEM((width, 2 * channels), BF),
             pltpu.VMEM((m, width), BF),
-            pltpu.SemaphoreType.DMA((5,)),
+            pltpu.SemaphoreType.DMA,
         ],
         out_shape=[pltpu.VMEM((2, m, channels), F32), stat],
-        compiler_params=pltpu.CompilerParams(vmem_limit_bytes=32 * MIB),
+        compiler_params=pltpu.CompilerParams(vmem_limit_bytes=16 * MIB),
         cost_estimate=cost(1, 1),
-    )(me, valid, outer, state, total, part, before, near_stat, qkv_weight, out_weight, taps)
+    )(me, valid, outer, state, total, part, before, near_stat, *weights)
 
 
 def norm_kernel(
@@ -576,7 +601,7 @@
     tile = lax.all_to_all(
         raster.reshape(tiles, rows, width), "tm", split_axis=0, concat_axis=0, tiled=True
     ).reshape(count, width)
-    buf = run_state(tokens, qkv_weight, head)
+    buf, wq, wo, w2, wx = run_state(me, tokens, qkv_weight, out_weight, taps, head)
 
     def swap_by(x, k):
         return swap(x, [(i, i ^ k) for i in range(tiles)])
@@ -596,13 +621,14 @@
     cut = count // 2
     outer = [swap(tile[:cut], ends), swap(tile[cut:], ends)]
     near_plane, part, state, total, near_stat = near(
-        rows, me, group_map, valid_frames, pieces, tile, inner, qkv_weight, out_weight, taps, head
+        rows, me, group_map, valid_frames, pieces, tile, inner, (wq, wo, w2, taps),
+        channels, head,
     )
     stat, planes = jnp.zeros((8, channels), F32), []
     for i, piece in enumerate(outer):
         plane, stat = far(
             rows, i * tiles // 2, me, valid_frames, piece, state, total, part, stat, near_stat,
-            qkv_weight, out_weight, taps,
+            (wq, wo, wx),
         )
         planes.append(plane)
     stat = lax.all_to_all(stat, "tm", split_axis=0, concat_axis=0, tiled=True)

time: 90.4 us -> 86.8 us (0.960)
  Pallas kernels: 32.5 us -> 28.2 us
  blocking collectives: 16.3 us -> 20.4 us
  waiting for transfers between devices: 18.4 us -> 16 us
  other arithmetic: 1.44 us -> 0 us
    all_to_all x1, blocking collectives: 16.3 us -> 20.4 us  [local(): stat = lax.all_to_all(stat, 'tm', split_axis=0, concat_axis=0, tiled=True)]
    ppermute x8, waiting for transfers between devices: 15.6 us -> 12.5 us  [swap(): return lax.ppermute(x, 'tm', pairs)]
    pallas_call x2, Pallas kernels: 8.54 us -> 6.51 us  [far(): pl.pallas_call(functools.partial(far_kernel, rows, first, last), in_specs...]
    unnamed x12 -> x22, local copies, waits for them, and re-layouts: 1.73 us -> 3.39 us
    concatenate x1 -> x0, other arithmetic: 1.44 us -> none  [local(): buf = jnp.concatenate([buf] + got, axis=0)]
    slice x1, local copies, waits for them, and re-layouts: 1.03 us -> 0.07 us  [local(): outer = [swap(tile[:cut], ends), swap(tile[cut:], ends)]]
    pallas_call x1, Pallas kernels: 4.92 us -> 3.98 us  [run_state(): pl.pallas_call(functools.partial(state_kernel, head), grid=(steps,), in_s...]
    pallas_call x1, Pallas kernels: 11.4 us -> 10.5 us  [near(): pl.pallas_call(functools.partial(near_kernel, rows, parts, frames), grid_...]
  transfers between devices with their start and end apart: 9 -> 9, of which waited for: 5 -> 5; matrix products, arithmetic and copies ran while one was open for 6% -> 0% of each run, Pallas kernels for 23% -> 20%
where the time goes in v4:
time: 86.8 us; the launch traced here: 86.4 us
  Pallas kernels  28.2 us (32%)
  blocking collectives  20.4 us (24%)
  starting transfers between devices  18.1 us (21%)
  waiting for transfers between devices  16 us (18%)
  local copies, waits for them, and re-layouts  3.48 us (4%)
    all_to_all x1, blocking collectives, local(): stat = lax.all_to_all(stat, 'tm', split_axis=0, concat_axis=0, tiled=True)  20.4 us
    ppermute x8, waiting for transfers between devices, swap(): return lax.ppermute(x, 'tm', pairs)  12.5 us
    ppermute x8, starting transfers between devices, swap(): return lax.ppermute(x, 'tm', pairs)  10.7 us
    pallas_call x1, Pallas kernels, near(): pl.pallas_call(functools.partial(near_kernel, rows, parts, frames), grid_...  10.5 us
    all_to_all x1, starting transfers between devices, local(): lax.all_to_all(raster.reshape(tiles, rows, width), 'tm', split_axis=0, co...  7.4 us
    pallas_call x2, Pallas kernels, far(): pl.pallas_call(functools.partial(far_kernel, rows, first, last), in_specs...  6.51 us
    pallas_call x1, Pallas kernels, norm(): pl.pallas_call(functools.partial(norm_kernel, rows, channels // NORM_GROU...  4.01 us
    pallas_call x1, Pallas kernels, run_state(): pl.pallas_call(functools.partial(state_kernel, head), grid=(steps,), in_s...  3.98 us
  transfers between devices with their start and end apart: 9, of which 5 were waited for; matrix products, arithmetic and copies ran while one was open for 0% of the time, Pallas kernels for 20%

profile of v4, /device:TPU:0, one launch (start us, length us, event | category | flops | bytes accessed | tf_op | source)
XLA Modules:
  0.0 86.4 jit_solution(18232905824785266388)
XLA Ops:
  0.0 3.3 %shard_map.91 = bf16[1024,512]{1,0:T(8,128)(2,1)} custom-call(s32[1,1024]{1,0:T(1,128)} %bitcast.15, bf16[1024,512]{1,0:T(8,128)(2,1)} %tok_ref.1), custom_call_target="tpu_custom_call" | custom-call | flops 1073741824 | bytes 2097152 | tf_op jit(solution)/shard_map/pallas_call | solution.py:68
  3.3 7.4 %all-to-all-start = ((bf16[16,64,512]{2,1,0:T(8,128)(2,1)}), bf16[16,64,512]{2,1,0:T(8,128)(2,1)S(1)}, u32[]{:S(2)}, u32[]{:S(2)}) async-start(bf16[16,64,512]{2,1,0:T(8,128)(2,1)} %bitcast.14), calls=%async_computation | async-start | bytes 2097152 | tf_op jit(solution)/shard_map/all_to_all | solution.py:601
  10.7 1.2 %copy-done.4 = bf16[1024,512]{1,0:T(8,128)(2,1)S(1)} copy-done((bf16[1024,512]{1,0:T(8,128)(2,1)S(1)}, bf16[1024,512]{1,0:T(8,128)(2,1)}, u32[]{:S(2)}) %copy-start.4) | copy-done | bytes 1048600
  11.9 4.0 %shard_map.92 = (bf16[1,16,1152]{2,1,0:T(8,128)(2,1)S(1)}, bf16[512,512]{1,0:T(8,128)(2,1)S(1)}, bf16[512,1024]{1,0:T(8,128)(2,1)S(1)}, bf16[1536,512]{1,0:T(8,128)(2,1)S(1)}, bf16[1024,512]{1,0:T(8,128)(2,1)S(1)}) custom-call(s32[1]{0:T(128)} %bitcast.pos_ref, bf16[1024,512]{1,0:T(8,128)(2,1)S(1)} %copy-done.4, bf16[512,1536]{1,0:T(8,128)(2,1)} %qkv_hbm.1, ...), custom_call_target="tpu_custom_call" | custom-call | flops 1073741824 | bytes 4194304 | tf_op jit(solution)/shard_map/pallas_call | solution.py:185
  15.9 1.0 %copy-done = bf16[1024,512]{1,0:T(8,128)(2,1)} copy-done((bf16[1024,512]{1,0:T(8,128)(2,1)}, bf16[1024,512]{1,0:T(8,128)(2,1)S(1)}, u32[]{:S(2)}) %copy-start) | copy-done | bytes 1048600
  16.9 1.1 %copy-done.2 = bf16[1536,512]{1,0:T(8,128)(2,1)} copy-done((bf16[1536,512]{1,0:T(8,128)(2,1)}, bf16[1536,512]{1,0:T(8,128)(2,1)S(1)}, u32[]{:S(2)}) %copy-start.2) | copy-done | bytes 1572888
  18.0 1.9 %collective-permute-start = (bf16[1,16,1152]{2,1,0:T(8,128)(2,1)S(1)}, bf16[1,16,1152]{2,1,0:T(8,128)(2,1)S(1)}, u32[]{:S(2)}, u32[]{:S(2)}) collective-permute-start(bf16[1,16,1152]{2,1,0:T(8,128)(2,1)S(1)} %get-tuple-element.20), channel_id=1, source_target_pairs={{0,2},{1,3},{2,0},{3,1},{4,6},{5,7},{6,4},{7,5},{8,10},{9,11},{10,... | collective-permute-start | bytes 110600 | tf_op jit(solution)/shard_map/ppermute | solution.py:594
  19.9 2.4 %collective-permute-done = bf16[1,16,1152]{2,1,0:T(8,128)(2,1)S(1)} collective-permute-done((bf16[1,16,1152]{2,1,0:T(8,128)(2,1)S(1)}, bf16[1,16,1152]{2,1,0:T(8,128)(2,1)S(1)}, u32[]{:S(2)}, u32[]{:S(2)}) %collective-permute-start) | collective-permute-done | bytes 36896 | tf_op jit(solution)/shard_map/ppermute | solution.py:594
  22.3 3.2 %collective-permute-start.1 = (bf16[2,16,1152]{2,1,0:T(8,128)(2,1)S(1)}, bf16[2,16,1152]{2,1,0:T(8,128)(2,1)S(1)}, u32[]{:S(2)}, u32[]{:S(2)}) collective-permute-start(bf16[2,16,1152]{2,1,0:T(8,128)(2,1)S(1)} %get-tuple-element.38), channel_id=1, source_target_pairs={{0,4},{1,5},{2,6},{3,7},{4,0},{5,1},{6,2},{7,3},{8,12},{9,13},{10,... | collective-permute-start | bytes 221192 | tf_op jit(solution)/shard_map/ppermute | solution.py:594
  25.5 1.4 %collective-permute-start.3 = (bf16[2,16,1152]{2,1,0:T(8,128)(2,1)S(1)}, bf16[2,16,1152]{2,1,0:T(8,128)(2,1)S(1)}, u32[]{:S(2)}, u32[]{:S(2)}) collective-permute-start(bf16[2,16,1152]{2,1,0:T(8,128)(2,1)S(1)} %get-tuple-element.38), channel_id=1, source_target_pairs={{0,8},{1,9},{2,10},{3,11},{4,12},{5,13},{6,14},{7,15},{8,0},{9,1},... | collective-permute-start | bytes 221192 | tf_op jit(solution)/shard_map/ppermute | solution.py:594
  26.9 1.1 %collective-permute-start.4 = (bf16[2,16,1152]{2,1,0:T(8,128)(2,1)S(1)}, bf16[2,16,1152]{2,1,0:T(8,128)(2,1)S(1)}, u32[]{:S(2)}, u32[]{:S(2)}) collective-permute-start(bf16[2,16,1152]{2,1,0:T(8,128)(2,1)S(1)} %get-tuple-element.38), channel_id=1, source_target_pairs={{0,12},{1,13},{2,14},{3,15},{4,8},{5,9},{6,10},{7,11},{8,4},{9,5},... | collective-permute-start | bytes 221192 | tf_op jit(solution)/shard_map/ppermute | solution.py:594
  28.0 2.6 %collective-permute-done.1 = bf16[2,16,1152]{2,1,0:T(8,128)(2,1)S(1)} collective-permute-done((bf16[2,16,1152]{2,1,0:T(8,128)(2,1)S(1)}, bf16[2,16,1152]{2,1,0:T(8,128)(2,1)S(1)}, u32[]{:S(2)}, u32[]{:S(2)}) %collective-permute-start.1) | collective-permute-done | bytes 73760 | tf_op jit(solution)/shard_map/ppermute | solution.py:594
  30.5 3.5 %all-to-all-done = bf16[16,64,512]{2,1,0:T(8,128)(2,1)S(1)} async-done(((bf16[16,64,512]{2,1,0:T(8,128)(2,1)}), bf16[16,64,512]{2,1,0:T(8,128)(2,1)S(1)}, u32[]{:S(2)}, u32[]{:S(2)}) %all-to-all-start) | async-done | bytes 1048608 | tf_op jit(solution)/shard_map/all_to_all | solution.py:601
  34.0 0.2 collective-permute-start.6
  34.3 0.8 collective-permute-start.7
  35.2 0.9 %collective-permute-start.2 = (bf16[512,512]{1,0:T(8,128)(2,1)S(1)}, bf16[512,512]{1,0:T(8,128)(2,1)S(1)}, u32[]{:S(2)}, u32[]{:S(2)}) collective-permute-start(bf16[512,512]{1,0:T(8,128)(2,1)S(1)} %get-tuple-element.36), channel_id=1, source_target_pairs={{1,2},{3,4},{5,6},{7,8},{9,10},{11,12},{13,14},{2,1},{4,3},{6,5},{... | collective-permute-start | bytes 1572872 | tf_op jit(solution)/shard_map/ppermute | solution.py:594
  36.0 6.4 %collective-permute-done.3 = bf16[2,16,1152]{2,1,0:T(8,128)(2,1)S(1)} collective-permute-done((bf16[2,16,1152]{2,1,0:T(8,128)(2,1)S(1)}, bf16[2,16,1152]{2,1,0:T(8,128)(2,1)S(1)}, u32[]{:S(2)}, u32[]{:S(2)}) %collective-permute-start.3) | collective-permute-done | bytes 73760 | tf_op jit(solution)/shard_map/ppermute | solution.py:594
  42.5 1.2 %collective-permute-start.5 = (bf16[8,16,1152]{2,1,0:T(8,128)(2,1)S(1)}, bf16[8,16,1152]{2,1,0:T(8,128)(2,1)S(1)}, u32[]{:S(2)}, u32[]{:S(2)}) collective-permute-start(bf16[8,16,1152]{2,1,0:T(8,128)(2,1)S(1)} %constant_dynamic-update-slice_fusion.2.refs_0_), channel_id=1, source_target_pairs={{0,1},{1,0},{2,3},{3,2},{4,5},{5,4},{6,7},{7,6},{8,9},{9,8},{10,11... | collective-permute-start | bytes 884744 | tf_op jit(solution)/shard_map/ppermute | solution.py:594
  43.7 1.2 %collective-permute-done.5.refs_1_ = bf16[8,16,1152]{2,1,0:T(8,128)(2,1)S(1)} collective-permute-done((bf16[8,16,1152]{2,1,0:T(8,128)(2,1)S(1)}, bf16[8,16,1152]{2,1,0:T(8,128)(2,1)S(1)}, u32[]{:S(2)}, u32[]{:S(2)}) %collective-permute-start.5) | collective-permute-done | bytes 294944 | tf_op jit(solution)/shard_map/ppermute | solution.py:594
  44.9 10.5 %shard_map.93 = (f32[2,1024,256]{2,1,0:T(8,128)S(1)}, f32[2,1024,256]{2,1,0:T(8,128)S(1)}, bf16[16,32,512]{2,1,0:T(8,128)(2,1)S(1)}, f32[16,8,512]{2,1,0:T(8,128)S(1)}, f32[8,256]{1,0:T(8,128)S(1)}) custom-call(s32[1]{0:T(128)} %bitcast.pos_ref, s32[16]{0:T(128)S(1)} %copy-done.8, s32[16]{0:T(128)S(1)} %copy-done.5, ...), custom_call_target="tpu_custom_call" | custom-call | flops 1 | bytes 1 | tf_op jit(solution)/shard_map/pallas_call | solution.py:380
  55.5 3.1 %shard_map.94 = (f32[2,512,256]{2,1,0:T(8,128)S(1)}, f32[8,256]{1,0:T(8,128)S(1)}) custom-call(s32[1]{0:T(128)} %bitcast.pos_ref, s32[16]{0:T(128)S(1)} %copy-done.5, bf16[512,512]{1,0:T(8,128)(2,1)S(1)} %collective-permute-done.7.outer_any, bf16[16,32,512]{2,1,0:T(8,128)(2,1)S(1)} %get-tuple-element.25.state_ref, ...), custom_call_target="tpu_custom_call" | custom-call | flops 1 | bytes 1 | tf_op jit(solution)/shard_map/pallas_call | solution.py:468
  58.6 3.4 %shard_map.95 = (f32[2,512,256]{2,1,0:T(8,128)S(1)}, f32[16,8,256]{2,1,0:T(8,128)S(1)}) custom-call(s32[1]{0:T(128)} %bitcast.pos_ref, s32[16]{0:T(128)S(1)} %copy-done.5, bf16[512,512]{1,0:T(8,128)(2,1)S(1)} %collective-permute-done.2.outer_any, bf16[16,32,512]{2,1,0:T(8,128)(2,1)S(1)} %get-tuple-element.25.state_ref, ...), custom_call_target="tpu_custom_call" | custom-call | flops 1 | bytes 1 | tf_op jit(solution)/shard_map/pallas_call | solution.py:468
  62.0 20.4 %all_to_all.10.stat_ref = f32[16,8,256]{2,1,0:T(8,128)S(1)} all-to-all(f32[16,8,256]{2,1,0:T(8,128)S(1)} %get-tuple-element.31), channel_id=1, replica_groups=mesh['clip'=2,'tm'=16] {'tm'}, dimensions={0} | all-to-all | bytes 262144 | tf_op jit(solution)/shard_map/all_to_all | solution.py:634
  82.4 4.0 %shard_map.96 = bf16[16,2,128,256]{3,2,1,0:T(8,128)(2,1)} custom-call(s32[1]{0:T(128)} %bitcast.pos_ref, s32[16]{0:T(128)S(1)} %copy-done.5, f32[16,8,256]{2,1,0:T(8,128)S(1)} %all_to_all.10.stat_ref, f32[1,256]{1,0:T(1,128)S(1)} %bitcast.10, f32[1,256]{1,0:T(1,128)S(1)} %bitcast.11, f32[2,1024,256]{2,1,0:T(8,128)S(1)} %get-tuple-element.32.near_ref, ...), custom_call_target="tpu_custom_call" | custom-call | flops 8388608 | bytes 6291456 | tf_op jit(solution)/shard_map/pallas_call | solution.py:548
  (26 shorter events, 0.2 us)
Async XLA Ops:
  3.3 30.7 %all-to-all-start = ((bf16[16,64,512]{2,1,0:T(8,128)(2,1)}), bf16[16,64,512]{2,1,0:T(8,128)(2,1)S(1)}, u32[]{:S(2)}, u32[]{:S(2)}) async-start(bf16[16,64,512]{2,1,0:T(8,128)(2,1)} %bitcast.14), calls=%async_computation | async-start | bytes 2097152 | tf_op jit(solution)/shard_map/all_to_all | solution.py:601
  10.7 1.2 %copy-start.4 = (bf16[1024,512]{1,0:T(8,128)(2,1)S(1)}, bf16[1024,512]{1,0:T(8,128)(2,1)}, u32[]{:S(2)}) copy-start(bf16[1024,512]{1,0:T(8,128)(2,1)} %tok_ref.1) | copy-start | bytes 3145732
  15.9 1.0 %copy-start = (bf16[1024,512]{1,0:T(8,128)(2,1)}, bf16[1024,512]{1,0:T(8,128)(2,1)S(1)}, u32[]{:S(2)}) copy-start(bf16[1024,512]{1,0:T(8,128)(2,1)S(1)} %get-tuple-element.29.wx_ref) | copy-start | bytes 3145732
  16.9 1.1 %copy-start.2 = (bf16[1536,512]{1,0:T(8,128)(2,1)}, bf16[1536,512]{1,0:T(8,128)(2,1)S(1)}, u32[]{:S(2)}) copy-start(bf16[1536,512]{1,0:T(8,128)(2,1)S(1)} %get-tuple-element.24.refs_6_) | copy-start | bytes 4718596
  18.0 26.9 %copy-start.5 = (s32[16]{0:T(128)S(1)}, s32[16]{0:T(128)}, u32[]{:S(2)}) copy-start(s32[16]{0:T(128)} %valid_ref.7) | copy-start | bytes 196
  18.0 26.9 %copy-start.8 = (s32[16]{0:T(128)S(1)}, s32[16]{0:T(128)}, u32[]{:S(2)}) copy-start(s32[16]{0:T(128)} %group_ref.1) | copy-start | bytes 196
  18.0 4.3 %collective-permute-start = (bf16[1,16,1152]{2,1,0:T(8,128)(2,1)S(1)}, bf16[1,16,1152]{2,1,0:T(8,128)(2,1)S(1)}, u32[]{:S(2)}, u32[]{:S(2)}) collective-permute-start(bf16[1,16,1152]{2,1,0:T(8,128)(2,1)S(1)} %get-tuple-element.20), channel_id=1, source_target_pairs={{0,2},{1,3},{2,0},{3,1},{4,6},{5,7},{6,4},{7,5},{8,10},{9,11},{10,... | collective-permute-start | bytes 110600 | tf_op jit(solution)/shard_map/ppermute | solution.py:594
  22.3 8.2 %collective-permute-start.1 = (bf16[2,16,1152]{2,1,0:T(8,128)(2,1)S(1)}, bf16[2,16,1152]{2,1,0:T(8,128)(2,1)S(1)}, u32[]{:S(2)}, u32[]{:S(2)}) collective-permute-start(bf16[2,16,1152]{2,1,0:T(8,128)(2,1)S(1)} %get-tuple-element.38), channel_id=1, source_target_pairs={{0,4},{1,5},{2,6},{3,7},{4,0},{5,1},{6,2},{7,3},{8,12},{9,13},{10,... | collective-permute-start | bytes 221192 | tf_op jit(solution)/shard_map/ppermute | solution.py:594
  25.5 16.9 %collective-permute-start.3 = (bf16[2,16,1152]{2,1,0:T(8,128)(2,1)S(1)}, bf16[2,16,1152]{2,1,0:T(8,128)(2,1)S(1)}, u32[]{:S(2)}, u32[]{:S(2)}) collective-permute-start(bf16[2,16,1152]{2,1,0:T(8,128)(2,1)S(1)} %get-tuple-element.38), channel_id=1, source_target_pairs={{0,8},{1,9},{2,10},{3,11},{4,12},{5,13},{6,14},{7,15},{8,0},{9,1},... | collective-permute-start | bytes 221192 | tf_op jit(solution)/shard_map/ppermute | solution.py:594
  26.9 15.6 %collective-permute-start.4 = (bf16[2,16,1152]{2,1,0:T(8,128)(2,1)S(1)}, bf16[2,16,1152]{2,1,0:T(8,128)(2,1)S(1)}, u32[]{:S(2)}, u32[]{:S(2)}) collective-permute-start(bf16[2,16,1152]{2,1,0:T(8,128)(2,1)S(1)} %get-tuple-element.38), channel_id=1, source_target_pairs={{0,12},{1,13},{2,14},{3,15},{4,8},{5,9},{6,10},{7,11},{8,4},{9,5},... | collective-permute-start | bytes 221192 | tf_op jit(solution)/shard_map/ppermute | solution.py:594
  34.0 10.9 %copy-start.3 = (bf16[1536,512]{1,0:T(8,128)(2,1)S(1)}, bf16[1536,512]{1,0:T(8,128)(2,1)}, u32[]{:S(2)}) copy-start(bf16[1536,512]{1,0:T(8,128)(2,1)} %copy-done.2) | copy-start | bytes 4718596
  34.0 10.9 %collective-permute-start.6 = (bf16[1024,512]{1,0:T(8,128)(2,1)S(1)}, bf16[1024,512]{1,0:T(8,128)(2,1)S(1)}, u32[]{:S(2)}, u32[]{:S(2)}) collective-permute-start(bf16[1024,512]{1,0:T(8,128)(2,1)S(1)} %bitcast.7), channel_id=1, source_target_pairs={{0,1},{1,0},{2,3},{3,2},{4,5},{5,4},{6,7},{7,6},{8,9},{9,8},{10,11... | collective-permute-start | bytes 3145736 | tf_op jit(solution)/shard_map/ppermute | solution.py:594
  34.3 21.1 %collective-permute-start.7 = (bf16[512,512]{1,0:T(8,128)(2,1)S(1)}, bf16[512,512]{1,0:T(8,128)(2,1)S(1)}, u32[]{:S(2)}, u32[]{:S(2)}) collective-permute-start(bf16[512,512]{1,0:T(8,128)(2,1)S(1)} %get-tuple-element.35), channel_id=1, source_target_pairs={{1,2},{3,4},{5,6},{7,8},{9,10},{11,12},{13,14},{2,1},{4,3},{6,5},{... | collective-permute-start | bytes 1572872 | tf_op jit(solution)/shard_map/ppermute | solution.py:594
  35.2 23.5 %collective-permute-start.2 = (bf16[512,512]{1,0:T(8,128)(2,1)S(1)}, bf16[512,512]{1,0:T(8,128)(2,1)S(1)}, u32[]{:S(2)}, u32[]{:S(2)}) collective-permute-start(bf16[512,512]{1,0:T(8,128)(2,1)S(1)} %get-tuple-element.36), channel_id=1, source_target_pairs={{1,2},{3,4},{5,6},{7,8},{9,10},{11,12},{13,14},{2,1},{4,3},{6,5},{... | collective-permute-start | bytes 1572872 | tf_op jit(solution)/shard_map/ppermute | solution.py:594
  42.5 2.4 %collective-permute-start.5 = (bf16[8,16,1152]{2,1,0:T(8,128)(2,1)S(1)}, bf16[8,16,1152]{2,1,0:T(8,128)(2,1)S(1)}, u32[]{:S(2)}, u32[]{:S(2)}) collective-permute-start(bf16[8,16,1152]{2,1,0:T(8,128)(2,1)S(1)} %constant_dynamic-update-slice_fusion.2.refs_0_), channel_id=1, source_target_pairs={{0,1},{1,0},{2,3},{3,2},{4,5},{5,4},{6,7},{7,6},{8,9},{9,8},{10,11... | collective-permute-start | bytes 884744 | tf_op jit(solution)/shard_map/ppermute | solution.py:594
  44.9 10.5 %copy-start.1 = (bf16[1024,512]{1,0:T(8,128)(2,1)S(1)}, bf16[1024,512]{1,0:T(8,128)(2,1)}, u32[]{:S(2)}) copy-start(bf16[1024,512]{1,0:T(8,128)(2,1)} %copy-done) | copy-start | bytes 3145732
  58.6 23.8 %copy-start.6 = (f32[256]{0:T(256)S(1)}, f32[256]{0:T(256)}, u32[]{:S(2)}) copy-start(f32[256]{0:T(256)} %param.13) | copy-start | bytes 3076
  58.6 23.8 %copy-start.7 = (f32[256]{0:T(256)S(1)}, f32[256]{0:T(256)}, u32[]{:S(2)}) copy-start(f32[256]{0:T(256)} %param.14) | copy-start | bytes 3076

commit v5 on v4

--- a/solution.py
+++ b/solution.py
@@ -482,93 +482,85 @@
 
 
 def norm_kernel(
-    rows, size, pos_ref, valid_ref, stat_ref, gain_ref, bias_ref, near_ref, far0_ref, far1_ref,
-    out_ref, mul_ref, add_ref, mix_ref,
+    rows, size, frames, pos_ref, valid_ref, stat_ref, gain_ref, bias_ref, near_ref, far0_ref, far1_ref,
+    out_hbm, mix_ref, out_ref, sems,
 ):
-    step = pl.program_id(0)
-    frames = out_ref.shape[0]
     m = frames * rows
     channels = out_ref.shape[3]
     me = pos_ref[0]
     odd = jnp.bitwise_and(me, 1)
 
-    @pl.when(step == 0)
-    def _():
-        stat = stat_ref[...]
-        tile = lax.broadcasted_iota(jnp.int32, (stat.shape[0], channels), 0)
-        counts = jnp.zeros(tile.shape, F32)
-        for i in range(stat.shape[0]):
-            counts = jnp.where(tile == i, (valid_ref[i] * (2 * rows)).astype(F32), counts)
-        mix = jnp.where(same_block((channels, channels), size), 1.0, 0.0)
-        all_count = jnp.sum(counts, axis=0, keepdims=True) * (2 * size)
-
-        def grouped(row):
-            wide = jnp.broadcast_to(row, (8, channels))
-            return dot(wide, mix, precision=lax.Precision.HIGHEST)[0:1]
-
-        sums = stat[:, 0, :] + stat[:, 2, :]
-        mean = grouped(jnp.sum(sums, axis=0, keepdims=True)) / all_count
-        gap0 = stat[:, 0, :] / counts - mean
-        gap1 = stat[:, 2, :] / counts - mean
-        spread = stat[:, 1, :] + stat[:, 3, :] + (gap0 * gap0 + gap1 * gap1) * counts
-        var = grouped(jnp.sum(spread, axis=0, keepdims=True)) / all_count
-        scale = gain_ref[...] * lax.rsqrt(var + 1e-5)
-        mul_ref[...] = 0.5 * scale
-        add_ref[...] = 0.5 * (bias_ref[...] - mean * scale)
-
-    live = valid_rows(step * frames, valid_ref[me], frames, rows)
-    mul, add = mul_ref[...], add_ref[...]
-    here = pl.ds(pl.multiple_of(step * m, m), m)
-    cut = far0_ref.shape[1]
-    there = pl.ds(pl.multiple_of(step * m % cut, m), m)
-    late = step * m >= cut
-    for y in range(2):
-        line = 1 - odd if y == 0 else odd
-        for b in range(2):
-            if y == 0:
-                half = near_ref[b, here] * mul + add
-            else:
-                half = jnp.where(late, far1_ref[b, there], far0_ref[b, there]) * mul + add
-            z = jnp.where(live, half + half * jnp.tanh(half), 0.0)
-            for c in range(channels // 128):
-                mix_ref[y, c, pl.ds(b, m, 2), :] = z[:, 128 * c : 128 * (c + 1)]
-        for f in range(frames):
-            for c in range(channels // 128):
-                out_ref[f, line, :, 128 * c : 128 * (c + 1)] = mix_ref[
-                    y, c, 2 * rows * f : 2 * rows * (f + 1), :
-                ].astype(BF)
+    stat = stat_ref[...]
+    tile = lax.broadcasted_iota(jnp.int32, (stat.shape[0], channels), 0)
+    counts = jnp.zeros(tile.shape, F32)
+    for i in range(stat.shape[0]):
+        counts = jnp.where(tile == i, (valid_ref[i] * (2 * rows)).astype(F32), counts)
+    mix = jnp.where(same_block((channels, channels), size), 1.0, 0.0)
+    all_count = jnp.sum(counts, axis=0, keepdims=True) * (2 * size)
+
+    def grouped(row):
+        wide = jnp.broadcast_to(row, (8, channels))
+        return dot(wide, mix, precision=lax.Precision.HIGHEST)[0:1]
+
+    sums = stat[:, 0, :] + stat[:, 2, :]
+    mean = grouped(jnp.sum(sums, axis=0, keepdims=True)) / all_count
+    gap0 = stat[:, 0, :] / counts - mean
+    gap1 = stat[:, 2, :] / counts - mean
+    spread = stat[:, 1, :] + stat[:, 3, :] + (gap0 * gap0 + gap1 * gap1) * counts
+    var = grouped(jnp.sum(spread, axis=0, keepdims=True)) / all_count
+    scale = gain_ref[...] * lax.rsqrt(var + 1e-5)
+    mul = 0.5 * scale
+    add = 0.5 * (bias_ref[...] - mean * scale)
+    stores = []
+    for step in range(valid_ref.shape[0] // frames):
+        live = valid_rows(step * frames, valid_ref[me], frames, rows)
+        here = pl.ds(step * m, m)
+        cut = far0_ref.shape[1]
+        there = pl.ds(step * m % cut, m)
+        late_ref = far1_ref if step * m >= cut else far0_ref
+        for y in range(2):
+            line = 1 - odd if y == 0 else odd
+            for b in range(2):
+                if y == 0:
+                    half = near_ref[b, here] * mul + add
+                else:
+                    half = late_ref[b, there] * mul + add
+                z = jnp.where(live, half + half * jnp.tanh(half), 0.0)
+                for c in range(channels // 128):
+                    mix_ref[y, c, pl.ds(b, m, 2), :] = z[:, 128 * c : 128 * (c + 1)]
+            for f in range(frames):
+                for c in range(channels // 128):
+                    out_ref[step * frames + f, line, :, 128 * c : 128 * (c + 1)] = mix_ref[
+                        y, c, 2 * rows * f : 2 * rows * (f + 1), :
+                    ].astype(BF)
+        now = pl.ds(step * frames, frames)
+        stores.append(pltpu.make_async_copy(out_ref.at[now], out_hbm.at[now], sems.at[step]))
+        stores[-1].start()
+    for copy in stores:
+        copy.wait()
 
 
 def norm(rows, me, valid, stat, gain, bias, near_plane, *far_planes):
     count, channels = near_plane.shape[1:]
     n = valid.shape[0]
-    frames = 4
+    frames = n // 4
     m = frames * rows
-    whole = lambda *shape: pl.BlockSpec(shape, lambda i, *_: (0,) * len(shape))
+    smem = pl.BlockSpec(memory_space=pltpu.SMEM)
     return pl.pallas_call(
-        functools.partial(norm_kernel, rows, channels // NORM_GROUPS),
-        grid_spec=pltpu.PrefetchScalarGridSpec(
-            num_scalar_prefetch=2,
-            grid=(n // frames,),
-            in_specs=[
-                whole(*stat.shape),
-                whole(1, channels),
-                whole(1, channels),
-                INSIDE,
-                INSIDE,
-                INSIDE,
-            ],
-            out_specs=pl.BlockSpec((frames, 2, 2 * rows, channels), lambda i, *_: (i, 0, 0, 0)),
-            scratch_shapes=[
-                pltpu.VMEM((1, channels), F32),
-                pltpu.VMEM((1, channels), F32),
-                pltpu.VMEM((2, channels // 128, 2 * m, 128), F32),
-            ],
-        ),
-        out_shape=jax.ShapeDtypeStruct((n, 2, 2 * rows, channels), BF),
-        compiler_params=params(24),
+        functools.partial(norm_kernel, rows, channels // NORM_GROUPS, frames),
+        in_specs=[smem, smem] + [INSIDE] * 6,
+        out_specs=HBM,
+        scratch_shapes=[
+            pltpu.VMEM((2, channels // 128, 2 * m, 128), F32),
+            pltpu.VMEM((n, 2, 2 * rows, channels), BF),
+            pltpu.SemaphoreType.DMA((n // frames,)),
+        ],
+        out_shape=pltpu.HBM((n, 2, 2 * rows, channels), BF),
+        compiler_params=pltpu.CompilerParams(vmem_limit_bytes=24 * MIB),
         cost_estimate=cost(32 * count * channels, 24 * count * channels, 4 * count * channels),
-    )(me, valid, stat, gain.reshape(1, channels), bias.reshape(1, channels), near_plane, *far_planes)
+    )(
+        me, valid, stat, gain.reshape(1, channels), bias.reshape(1, channels), near_plane, *far_planes
+    )
 
 
 def local(
@@ -609,7 +601,9 @@
     k, gate = 2, None
     while k < tiles:
         ks = [k] if k == 2 or 2 * k >= tiles else [k, 2 * k, 3 * k]
-        got = [swap_by(buf, j) for j in ks]
+        got = [swap_by(buf, ks[0])]
+        late, _ = lax.optimization_barrier((buf, got[0]))
+        got += [swap_by(late, j) for j in ks[1:]]
         gate = got[0]
         buf = jnp.concatenate([buf] + got, axis=0)
         k *= 2 if len(ks) == 1 else 4

time: 86.8 us -> 86.6 us (level)
  waiting for transfers between devices: 16 us -> 14.2 us
  starting transfers between devices: 18.1 us -> 19.1 us
    all_to_all x1, waiting for transfers between devices: 3.46 us -> 0.01 us  [local(): lax.all_to_all(raster.reshape(tiles, rows, width), 'tm', split_axis=0, co...]
    ppermute x8, waiting for transfers between devices: 12.5 us -> 14.2 us  [swap(): return lax.ppermute(x, 'tm', pairs)]
    ppermute x8, starting transfers between devices: 10.7 us -> 11.8 us  [swap(): return lax.ppermute(x, 'tm', pairs)]
  transfers between devices with their start and end apart: 9 -> 9, of which waited for: 5 -> 4; matrix products, arithmetic and copies ran while one was open for 0% -> 0% of each run, Pallas kernels for 20% -> 20%
where the time goes in v5:
time: 86.6 us; the launch traced here: 86.3 us
  Pallas kernels  27.9 us (32%)
  blocking collectives  21.2 us (24%)
  starting transfers between devices  19.1 us (22%)
  waiting for transfers between devices  14.2 us (16%)
  local copies, waits for them, and re-layouts  3.48 us (4%)
    all_to_all x1, blocking collectives, local(): stat = lax.all_to_all(stat, 'tm', split_axis=0, concat_axis=0, tiled=True)  21.2 us
    ppermute x8, waiting for transfers between devices, swap(): return lax.ppermute(x, 'tm', pairs)  14.2 us
    ppermute x8, starting transfers between devices, swap(): return lax.ppermute(x, 'tm', pairs)  11.8 us
    pallas_call x1, Pallas kernels, near(): pl.pallas_call(functools.partial(near_kernel, rows, parts, frames), grid_...  10.5 us
    all_to_all x1, starting transfers between devices, local(): lax.all_to_all(raster.reshape(tiles, rows, width), 'tm', split_axis=0, co...  7.4 us
    pallas_call x2, Pallas kernels, far(): pl.pallas_call(functools.partial(far_kernel, rows, first, last), in_specs...  6.51 us
    pallas_call x1, Pallas kernels, run_state(): pl.pallas_call(functools.partial(state_kernel, head), grid=(steps,), in_s...  3.98 us
    pallas_call x1, Pallas kernels, norm(): pl.pallas_call(functools.partial(norm_kernel, rows, channels // NORM_GROU...  3.66 us
  transfers between devices with their start and end apart: 9, of which 4 were waited for; matrix products, arithmetic and copies ran while one was open for 0% of the time, Pallas kernels for 20%

profile of v5, /device:TPU:0, one launch (start us, length us, event | category | flops | bytes accessed | tf_op | source)
XLA Modules:
  0.0 86.3 jit_solution(8612976618394455967)
XLA Ops:
  0.0 3.3 %shard_map.91 = bf16[1024,512]{1,0:T(8,128)(2,1)} custom-call(s32[1,1024]{1,0:T(1,128)} %bitcast.15, bf16[1024,512]{1,0:T(8,128)(2,1)} %tok_ref.1), custom_call_target="tpu_custom_call" | custom-call | flops 1073741824 | bytes 2097152 | tf_op jit(solution)/shard_map/pallas_call | solution.py:68
  3.3 7.4 %all-to-all-start = ((bf16[16,64,512]{2,1,0:T(8,128)(2,1)}), bf16[16,64,512]{2,1,0:T(8,128)(2,1)S(1)}, u32[]{:S(2)}, u32[]{:S(2)}) async-start(bf16[16,64,512]{2,1,0:T(8,128)(2,1)} %bitcast.14), calls=%async_computation | async-start | bytes 2097152 | tf_op jit(solution)/shard_map/all_to_all | solution.py:593
  10.7 1.2 %copy-done.4 = bf16[1024,512]{1,0:T(8,128)(2,1)S(1)} copy-done((bf16[1024,512]{1,0:T(8,128)(2,1)S(1)}, bf16[1024,512]{1,0:T(8,128)(2,1)}, u32[]{:S(2)}) %copy-start.4) | copy-done | bytes 1048600
  11.9 4.0 %shard_map.92 = (bf16[1,16,1152]{2,1,0:T(8,128)(2,1)S(1)}, bf16[512,512]{1,0:T(8,128)(2,1)S(1)}, bf16[512,1024]{1,0:T(8,128)(2,1)S(1)}, bf16[1536,512]{1,0:T(8,128)(2,1)S(1)}, bf16[1024,512]{1,0:T(8,128)(2,1)S(1)}) custom-call(s32[1]{0:T(128)} %bitcast.pos_ref, bf16[1024,512]{1,0:T(8,128)(2,1)S(1)} %copy-done.4, bf16[512,1536]{1,0:T(8,128)(2,1)} %qkv_hbm.1, ...), custom_call_target="tpu_custom_call" | custom-call | flops 1073741824 | bytes 4194304 | tf_op jit(solution)/shard_map/pallas_call | solution.py:185
  15.9 1.0 %copy-done = bf16[1024,512]{1,0:T(8,128)(2,1)} copy-done((bf16[1024,512]{1,0:T(8,128)(2,1)}, bf16[1024,512]{1,0:T(8,128)(2,1)S(1)}, u32[]{:S(2)}) %copy-start) | copy-done | bytes 1048600
  16.9 1.1 %copy-done.2 = bf16[1536,512]{1,0:T(8,128)(2,1)} copy-done((bf16[1536,512]{1,0:T(8,128)(2,1)}, bf16[1536,512]{1,0:T(8,128)(2,1)S(1)}, u32[]{:S(2)}) %copy-start.2) | copy-done | bytes 1572888
  18.0 1.9 %collective-permute-start = (bf16[1,16,1152]{2,1,0:T(8,128)(2,1)S(1)}, bf16[1,16,1152]{2,1,0:T(8,128)(2,1)S(1)}, u32[]{:S(2)}, u32[]{:S(2)}) collective-permute-start(bf16[1,16,1152]{2,1,0:T(8,128)(2,1)S(1)} %get-tuple-element.21), channel_id=1, source_target_pairs={{0,2},{1,3},{2,0},{3,1},{4,6},{5,7},{6,4},{7,5},{8,10},{9,11},{10,... | collective-permute-start | bytes 110600 | tf_op jit(solution)/shard_map/ppermute | solution.py:586
  19.9 2.4 %collective-permute-done = bf16[1,16,1152]{2,1,0:T(8,128)(2,1)S(1)} collective-permute-done((bf16[1,16,1152]{2,1,0:T(8,128)(2,1)S(1)}, bf16[1,16,1152]{2,1,0:T(8,128)(2,1)S(1)}, u32[]{:S(2)}, u32[]{:S(2)}) %collective-permute-start) | collective-permute-done | bytes 36896 | tf_op jit(solution)/shard_map/ppermute | solution.py:586
  22.3 3.2 %collective-permute-start.1 = (bf16[2,16,1152]{2,1,0:T(8,128)(2,1)S(1)}, bf16[2,16,1152]{2,1,0:T(8,128)(2,1)S(1)}, u32[]{:S(2)}, u32[]{:S(2)}) collective-permute-start(bf16[2,16,1152]{2,1,0:T(8,128)(2,1)S(1)} %get-tuple-element.23), channel_id=1, source_target_pairs={{0,4},{1,5},{2,6},{3,7},{4,0},{5,1},{6,2},{7,3},{8,12},{9,13},{10,... | collective-permute-start | bytes 221192 | tf_op jit(solution)/shard_map/ppermute | solution.py:586
  25.5 4.8 %collective-permute-done.1 = bf16[2,16,1152]{2,1,0:T(8,128)(2,1)S(1)} collective-permute-done((bf16[2,16,1152]{2,1,0:T(8,128)(2,1)S(1)}, bf16[2,16,1152]{2,1,0:T(8,128)(2,1)S(1)}, u32[]{:S(2)}, u32[]{:S(2)}) %collective-permute-start.1) | collective-permute-done | bytes 73760 | tf_op jit(solution)/shard_map/ppermute | solution.py:586
  30.3 4.4 %collective-permute-start.3 = (bf16[2,16,1152]{2,1,0:T(8,128)(2,1)S(1)}, bf16[2,16,1152]{2,1,0:T(8,128)(2,1)S(1)}, u32[]{:S(2)}, u32[]{:S(2)}) collective-permute-start(bf16[2,16,1152]{2,1,0:T(8,128)(2,1)S(1)} %get-tuple-element.23), channel_id=1, source_target_pairs={{0,8},{1,9},{2,10},{3,11},{4,12},{5,13},{6,14},{7,15},{8,0},{9,1},... | collective-permute-start | bytes 221192 | tf_op jit(solution)/shard_map/ppermute | solution.py:586
  34.7 0.4 collective-permute-start.4
  35.2 0.1 fusion
  35.3 0.8 collective-permute-start.7
  36.1 0.9 %collective-permute-start.2 = (bf16[512,512]{1,0:T(8,128)(2,1)S(1)}, bf16[512,512]{1,0:T(8,128)(2,1)S(1)}, u32[]{:S(2)}, u32[]{:S(2)}) collective-permute-start(bf16[512,512]{1,0:T(8,128)(2,1)S(1)} %get-tuple-element.38), channel_id=1, source_target_pairs={{1,2},{3,4},{5,6},{7,8},{9,10},{11,12},{13,14},{2,1},{4,3},{6,5},{... | collective-permute-start | bytes 1572872 | tf_op jit(solution)/shard_map/ppermute | solution.py:586
  37.0 5.4 %collective-permute-done.3 = bf16[2,16,1152]{2,1,0:T(8,128)(2,1)S(1)} collective-permute-done((bf16[2,16,1152]{2,1,0:T(8,128)(2,1)S(1)}, bf16[2,16,1152]{2,1,0:T(8,128)(2,1)S(1)}, u32[]{:S(2)}, u32[]{:S(2)}) %collective-permute-start.3) | collective-permute-done | bytes 73760 | tf_op jit(solution)/shard_map/ppermute | solution.py:586
  42.5 0.1 collective-permute-start.5
  42.6 1.6 %collective-permute-done.5.refs_1_ = bf16[8,16,1152]{2,1,0:T(8,128)(2,1)S(1)} collective-permute-done((bf16[8,16,1152]{2,1,0:T(8,128)(2,1)S(1)}, bf16[8,16,1152]{2,1,0:T(8,128)(2,1)S(1)}, u32[]{:S(2)}, u32[]{:S(2)}) %collective-permute-start.5) | collective-permute-done | bytes 294944 | tf_op jit(solution)/shard_map/ppermute | solution.py:586
  44.2 10.5 %shard_map.93 = (f32[2,1024,256]{2,1,0:T(8,128)S(1)}, f32[2,1024,256]{2,1,0:T(8,128)S(1)}, bf16[16,32,512]{2,1,0:T(8,128)(2,1)S(1)}, f32[16,8,512]{2,1,0:T(8,128)S(1)}, f32[8,256]{1,0:T(8,128)S(1)}) custom-call(s32[1]{0:T(128)} %bitcast.pos_ref, s32[16]{0:T(128)S(1)} %copy-done.8, s32[16]{0:T(128)S(1)} %copy-done.5, ...), custom_call_target="tpu_custom_call" | custom-call | flops 1 | bytes 1 | tf_op jit(solution)/shard_map/pallas_call | solution.py:380
  54.7 3.1 %shard_map.94 = (f32[2,512,256]{2,1,0:T(8,128)S(1)}, f32[8,256]{1,0:T(8,128)S(1)}) custom-call(s32[1]{0:T(128)} %bitcast.pos_ref, s32[16]{0:T(128)S(1)} %copy-done.5, bf16[512,512]{1,0:T(8,128)(2,1)S(1)} %collective-permute-done.7.outer_any, bf16[16,32,512]{2,1,0:T(8,128)(2,1)S(1)} %get-tuple-element.27.state_ref, ...), custom_call_target="tpu_custom_call" | custom-call | flops 1 | bytes 1 | tf_op jit(solution)/shard_map/pallas_call | solution.py:468
  57.8 0.0 copy-start.6
  57.9 3.4 %shard_map.95 = (f32[2,512,256]{2,1,0:T(8,128)S(1)}, f32[16,8,256]{2,1,0:T(8,128)S(1)}) custom-call(s32[1]{0:T(128)} %bitcast.pos_ref, s32[16]{0:T(128)S(1)} %copy-done.5, bf16[512,512]{1,0:T(8,128)(2,1)S(1)} %collective-permute-done.2.outer_any, bf16[16,32,512]{2,1,0:T(8,128)(2,1)S(1)} %get-tuple-element.27.state_ref, ...), custom_call_target="tpu_custom_call" | custom-call | flops 1 | bytes 1 | tf_op jit(solution)/shard_map/pallas_call | solution.py:468
  61.2 21.2 %all_to_all.10.stat_ref = f32[16,8,256]{2,1,0:T(8,128)S(1)} all-to-all(f32[16,8,256]{2,1,0:T(8,128)S(1)} %get-tuple-element.33), channel_id=1, replica_groups=mesh['clip'=2,'tm'=16] {'tm'}, dimensions={0} | all-to-all | bytes 262144 | tf_op jit(solution)/shard_map/all_to_all | solution.py:628
  82.4 3.7 %shard_map.96 = bf16[16,2,128,256]{3,2,1,0:T(8,128)(2,1)} custom-call(s32[1]{0:T(128)} %bitcast.pos_ref, s32[16]{0:T(128)S(1)} %copy-done.5, f32[16,8,256]{2,1,0:T(8,128)S(1)} %all_to_all.10.stat_ref, f32[1,256]{1,0:T(1,128)S(1)} %bitcast.10, f32[1,256]{1,0:T(1,128)S(1)} %bitcast.11, f32[2,1024,256]{2,1,0:T(8,128)S(1)} %get-tuple-element.34.near_ref, ...), custom_call_target="tpu_custom_call" | custom-call | flops 8388608 | bytes 6291456 | tf_op jit(solution)/shard_map/pallas_call | solution.py:549
  (26 shorter events, 0.1 us)
Async XLA Ops:
  3.3 31.9 %all-to-all-start = ((bf16[16,64,512]{2,1,0:T(8,128)(2,1)}), bf16[16,64,512]{2,1,0:T(8,128)(2,1)S(1)}, u32[]{:S(2)}, u32[]{:S(2)}) async-start(bf16[16,64,512]{2,1,0:T(8,128)(2,1)} %bitcast.14), calls=%async_computation | async-start | bytes 2097152 | tf_op jit(solution)/shard_map/all_to_all | solution.py:593
  10.7 1.2 %copy-start.4 = (bf16[1024,512]{1,0:T(8,128)(2,1)S(1)}, bf16[1024,512]{1,0:T(8,128)(2,1)}, u32[]{:S(2)}) copy-start(bf16[1024,512]{1,0:T(8,128)(2,1)} %tok_ref.1) | copy-start | bytes 3145732
  15.9 1.0 %copy-start = (bf16[1024,512]{1,0:T(8,128)(2,1)}, bf16[1024,512]{1,0:T(8,128)(2,1)S(1)}, u32[]{:S(2)}) copy-start(bf16[1024,512]{1,0:T(8,128)(2,1)S(1)} %get-tuple-element.31.wx_ref) | copy-start | bytes 3145732
  16.9 1.1 %copy-start.2 = (bf16[1536,512]{1,0:T(8,128)(2,1)}, bf16[1536,512]{1,0:T(8,128)(2,1)S(1)}, u32[]{:S(2)}) copy-start(bf16[1536,512]{1,0:T(8,128)(2,1)S(1)} %get-tuple-element.26.refs_6_) | copy-start | bytes 4718596
  18.0 26.1 %copy-start.5 = (s32[16]{0:T(128)S(1)}, s32[16]{0:T(128)}, u32[]{:S(2)}) copy-start(s32[16]{0:T(128)} %valid_ref.7) | copy-start | bytes 196
  18.0 26.1 %copy-start.8 = (s32[16]{0:T(128)S(1)}, s32[16]{0:T(128)}, u32[]{:S(2)}) copy-start(s32[16]{0:T(128)} %group_ref.1) | copy-start | bytes 196
  18.0 4.3 %collective-permute-start = (bf16[1,16,1152]{2,1,0:T(8,128)(2,1)S(1)}, bf16[1,16,1152]{2,1,0:T(8,128)(2,1)S(1)}, u32[]{:S(2)}, u32[]{:S(2)}) collective-permute-start(bf16[1,16,1152]{2,1,0:T(8,128)(2,1)S(1)} %get-tuple-element.21), channel_id=1, source_target_pairs={{0,2},{1,3},{2,0},{3,1},{4,6},{5,7},{6,4},{7,5},{8,10},{9,11},{10,... | collective-permute-start | bytes 110600 | tf_op jit(solution)/shard_map/ppermute | solution.py:586
  22.3 8.0 %collective-permute-start.1 = (bf16[2,16,1152]{2,1,0:T(8,128)(2,1)S(1)}, bf16[2,16,1152]{2,1,0:T(8,128)(2,1)S(1)}, u32[]{:S(2)}, u32[]{:S(2)}) collective-permute-start(bf16[2,16,1152]{2,1,0:T(8,128)(2,1)S(1)} %get-tuple-element.23), channel_id=1, source_target_pairs={{0,4},{1,5},{2,6},{3,7},{4,0},{5,1},{6,2},{7,3},{8,12},{9,13},{10,... | collective-permute-start | bytes 221192 | tf_op jit(solution)/shard_map/ppermute | solution.py:586
  30.3 12.1 %collective-permute-start.3 = (bf16[2,16,1152]{2,1,0:T(8,128)(2,1)S(1)}, bf16[2,16,1152]{2,1,0:T(8,128)(2,1)S(1)}, u32[]{:S(2)}, u32[]{:S(2)}) collective-permute-start(bf16[2,16,1152]{2,1,0:T(8,128)(2,1)S(1)} %get-tuple-element.23), channel_id=1, source_target_pairs={{0,8},{1,9},{2,10},{3,11},{4,12},{5,13},{6,14},{7,15},{8,0},{9,1},... | collective-permute-start | bytes 221192 | tf_op jit(solution)/shard_map/ppermute | solution.py:586
  34.7 7.7 %collective-permute-start.4 = (bf16[2,16,1152]{2,1,0:T(8,128)(2,1)S(1)}, bf16[2,16,1152]{2,1,0:T(8,128)(2,1)S(1)}, u32[]{:S(2)}, u32[]{:S(2)}) collective-permute-start(bf16[2,16,1152]{2,1,0:T(8,128)(2,1)S(1)} %get-tuple-element.23), channel_id=1, source_target_pairs={{0,12},{1,13},{2,14},{3,15},{4,8},{5,9},{6,10},{7,11},{8,4},{9,5},... | collective-permute-start | bytes 221192 | tf_op jit(solution)/shard_map/ppermute | solution.py:586
  35.2 9.0 %copy-start.3 = (bf16[1536,512]{1,0:T(8,128)(2,1)S(1)}, bf16[1536,512]{1,0:T(8,128)(2,1)}, u32[]{:S(2)}) copy-start(bf16[1536,512]{1,0:T(8,128)(2,1)} %copy-done.2) | copy-start | bytes 4718596
  35.2 8.9 %collective-permute-start.6 = (bf16[1024,512]{1,0:T(8,128)(2,1)S(1)}, bf16[1024,512]{1,0:T(8,128)(2,1)S(1)}, u32[]{:S(2)}, u32[]{:S(2)}) collective-permute-start(bf16[1024,512]{1,0:T(8,128)(2,1)S(1)} %bitcast.7), channel_id=1, source_target_pairs={{0,1},{1,0},{2,3},{3,2},{4,5},{5,4},{6,7},{7,6},{8,9},{9,8},{10,11... | collective-permute-start | bytes 3145736 | tf_op jit(solution)/shard_map/ppermute | solution.py:586
  35.3 19.4 %collective-permute-start.7 = (bf16[512,512]{1,0:T(8,128)(2,1)S(1)}, bf16[512,512]{1,0:T(8,128)(2,1)S(1)}, u32[]{:S(2)}, u32[]{:S(2)}) collective-permute-start(bf16[512,512]{1,0:T(8,128)(2,1)S(1)} %get-tuple-element.37), channel_id=1, source_target_pairs={{1,2},{3,4},{5,6},{7,8},{9,10},{11,12},{13,14},{2,1},{4,3},{6,5},{... | collective-permute-start | bytes 1572872 | tf_op jit(solution)/shard_map/ppermute | solution.py:586
  36.1 21.7 %collective-permute-start.2 = (bf16[512,512]{1,0:T(8,128)(2,1)S(1)}, bf16[512,512]{1,0:T(8,128)(2,1)S(1)}, u32[]{:S(2)}, u32[]{:S(2)}) collective-permute-start(bf16[512,512]{1,0:T(8,128)(2,1)S(1)} %get-tuple-element.38), channel_id=1, source_target_pairs={{1,2},{3,4},{5,6},{7,8},{9,10},{11,12},{13,14},{2,1},{4,3},{6,5},{... | collective-permute-start | bytes 1572872 | tf_op jit(solution)/shard_map/ppermute | solution.py:586
  42.5 1.6 %collective-permute-start.5 = (bf16[8,16,1152]{2,1,0:T(8,128)(2,1)S(1)}, bf16[8,16,1152]{2,1,0:T(8,128)(2,1)S(1)}, u32[]{:S(2)}, u32[]{:S(2)}) collective-permute-start(bf16[8,16,1152]{2,1,0:T(8,128)(2,1)S(1)} %constant_dynamic-update-slice_fusion.2.refs_0_), channel_id=1, source_target_pairs={{0,1},{1,0},{2,3},{3,2},{4,5},{5,4},{6,7},{7,6},{8,9},{9,8},{10,11... | collective-permute-start | bytes 884744 | tf_op jit(solution)/shard_map/ppermute | solution.py:586
  44.1 10.5 %copy-start.1 = (bf16[1024,512]{1,0:T(8,128)(2,1)S(1)}, bf16[1024,512]{1,0:T(8,128)(2,1)}, u32[]{:S(2)}) copy-start(bf16[1024,512]{1,0:T(8,128)(2,1)} %copy-done) | copy-start | bytes 3145732
  57.8 24.6 %copy-start.6 = (f32[256]{0:T(256)S(1)}, f32[256]{0:T(256)}, u32[]{:S(2)}) copy-start(f32[256]{0:T(256)} %param.13) | copy-start | bytes 3076
  57.8 24.6 %copy-start.7 = (f32[256]{0:T(256)S(1)}, f32[256]{0:T(256)}, u32[]{:S(2)}) copy-start(f32[256]{0:T(256)} %param.14) | copy-start | bytes 3076

commit v6 on v5

--- a/solution.py
+++ b/solution.py
@@ -551,7 +551,7 @@
         in_specs=[smem, smem] + [INSIDE] * 6,
         out_specs=HBM,
         scratch_shapes=[
-            pltpu.VMEM((2, channels // 128, 2 * m, 128), F32),
+            pltpu.VMEM((2, channels // 128, 2 * m + 8, 128), F32),
             pltpu.VMEM((n, 2, 2 * rows, channels), BF),
             pltpu.SemaphoreType.DMA((n // frames,)),
         ],
@@ -612,7 +612,7 @@
     inner = swap_by(tile, 1)
     ends = [(i, i + 1) for i in range(1, tiles - 1, 2)]
     ends = ends + [(j, i) for i, j in ends]
-    cut = count // 2
+    cut = count // 4 * 3
     outer = [swap(tile[:cut], ends), swap(tile[cut:], ends)]
     near_plane, part, state, total, near_stat = near(
         rows, me, group_map, valid_frames, pieces, tile, inner, (wq, wo, w2, taps),
@@ -621,7 +621,7 @@
     stat, planes = jnp.zeros((8, channels), F32), []
     for i, piece in enumerate(outer):
         plane, stat = far(
-            rows, i * tiles // 2, me, valid_frames, piece, state, total, part, stat, near_stat,
+            rows, i * cut // rows, me, valid_frames, piece, state, total, part, stat, near_stat,
             (wq, wo, wx),
         )
         planes.append(plane)

time: 86.6 us -> 86.6 us (level)
  blocking collectives: 21.2 us -> 18.6 us
  waiting for transfers between devices: 14.2 us -> 15.8 us
  starting transfers between devices: 19.1 us -> 20.1 us
    all_to_all x1, waiting for transfers between devices: 0.01 us -> 3.65 us  [local(): lax.all_to_all(raster.reshape(tiles, rows, width), 'tm', split_axis=0, co...]
    all_to_all x1, blocking collectives: 21.2 us -> 18.6 us  [local(): stat = lax.all_to_all(stat, 'tm', split_axis=0, concat_axis=0, tiled=True)]
    ppermute x8, waiting for transfers between devices: 14.2 us -> 12.1 us  [swap(): return lax.ppermute(x, 'tm', pairs)]
    ppermute x8, starting transfers between devices: 11.8 us -> 12.7 us  [swap(): return lax.ppermute(x, 'tm', pairs)]
  transfers between devices with their start and end apart: 9 -> 9, of which waited for: 4 -> 6; matrix products, arithmetic and copies ran while one was open for 0% -> 0% of each run, Pallas kernels for 20% -> 22%
where the time goes in v6:
time: 86.6 us; the launch traced here: 86.3 us
  Pallas kernels  28 us (32%)
  starting transfers between devices  20.1 us (23%)
  blocking collectives  18.6 us (21%)
  waiting for transfers between devices  15.8 us (18%)
  local copies, waits for them, and re-layouts  3.49 us (4%)
    all_to_all x1, blocking collectives, local(): stat = lax.all_to_all(stat, 'tm', split_axis=0, concat_axis=0, tiled=True)  18.6 us
    ppermute x8, starting transfers between devices, swap(): return lax.ppermute(x, 'tm', pairs)  12.7 us
    ppermute x8, waiting for transfers between devices, swap(): return lax.ppermute(x, 'tm', pairs)  12.1 us
    pallas_call x1, Pallas kernels, near(): pl.pallas_call(functools.partial(near_kernel, rows, parts, frames), grid_...  10.5 us
    all_to_all x1, starting transfers between devices, local(): lax.all_to_all(raster.reshape(tiles, rows, width), 'tm', split_axis=0, co...  7.4 us
    pallas_call x2, Pallas kernels, far(): pl.pallas_call(functools.partial(far_kernel, rows, first, last), in_specs...  6.57 us
    pallas_call x1, Pallas kernels, run_state(): pl.pallas_call(functools.partial(state_kernel, head), grid=(steps,), in_s...  3.98 us
    pallas_call x1, Pallas kernels, norm(): pl.pallas_call(functools.partial(norm_kernel, rows, channels // NORM_GROU...  3.66 us
  transfers between devices with their start and end apart: 9, of which 6 were waited for; matrix products, arithmetic and copies ran while one was open for 0% of the time, Pallas kernels for 22%

profile of v6, /device:TPU:0, one launch (start us, length us, event | category | flops | bytes accessed | tf_op | source)
XLA Modules:
  0.0 86.3 jit_solution(521976620886433149)
XLA Ops:
  0.0 3.3 %shard_map.91 = bf16[1024,512]{1,0:T(8,128)(2,1)} custom-call(s32[1,1024]{1,0:T(1,128)} %bitcast.16, bf16[1024,512]{1,0:T(8,128)(2,1)} %tok_ref.1), custom_call_target="tpu_custom_call" | custom-call | flops 1073741824 | bytes 2097152 | tf_op jit(solution)/shard_map/pallas_call | solution.py:68
  3.3 7.4 %all-to-all-start = ((bf16[16,64,512]{2,1,0:T(8,128)(2,1)}), bf16[16,64,512]{2,1,0:T(8,128)(2,1)S(1)}, u32[]{:S(2)}, u32[]{:S(2)}) async-start(bf16[16,64,512]{2,1,0:T(8,128)(2,1)} %bitcast.15), calls=%async_computation | async-start | bytes 2097152 | tf_op jit(solution)/shard_map/all_to_all | solution.py:593
  10.7 1.2 %copy-done.4 = bf16[1024,512]{1,0:T(8,128)(2,1)S(1)} copy-done((bf16[1024,512]{1,0:T(8,128)(2,1)S(1)}, bf16[1024,512]{1,0:T(8,128)(2,1)}, u32[]{:S(2)}) %copy-start.4) | copy-done | bytes 1048600
  11.9 4.0 %shard_map.92 = (bf16[1,16,1152]{2,1,0:T(8,128)(2,1)S(1)}, bf16[512,512]{1,0:T(8,128)(2,1)S(1)}, bf16[512,1024]{1,0:T(8,128)(2,1)S(1)}, bf16[1536,512]{1,0:T(8,128)(2,1)S(1)}, bf16[1024,512]{1,0:T(8,128)(2,1)S(1)}) custom-call(s32[1]{0:T(128)} %bitcast.pos_ref, bf16[1024,512]{1,0:T(8,128)(2,1)S(1)} %copy-done.4, bf16[512,1536]{1,0:T(8,128)(2,1)} %qkv_hbm.1, ...), custom_call_target="tpu_custom_call" | custom-call | flops 1073741824 | bytes 4194304 | tf_op jit(solution)/shard_map/pallas_call | solution.py:185
  15.9 1.0 %copy-done = bf16[1024,512]{1,0:T(8,128)(2,1)} copy-done((bf16[1024,512]{1,0:T(8,128)(2,1)}, bf16[1024,512]{1,0:T(8,128)(2,1)S(1)}, u32[]{:S(2)}) %copy-start) | copy-done | bytes 1048600
  16.9 1.1 %copy-done.2 = bf16[1536,512]{1,0:T(8,128)(2,1)} copy-done((bf16[1536,512]{1,0:T(8,128)(2,1)}, bf16[1536,512]{1,0:T(8,128)(2,1)S(1)}, u32[]{:S(2)}) %copy-start.2) | copy-done | bytes 1572888
  18.0 1.9 %collective-permute-start = (bf16[1,16,1152]{2,1,0:T(8,128)(2,1)S(1)}, bf16[1,16,1152]{2,1,0:T(8,128)(2,1)S(1)}, u32[]{:S(2)}, u32[]{:S(2)}) collective-permute-start(bf16[1,16,1152]{2,1,0:T(8,128)(2,1)S(1)} %get-tuple-element.21), channel_id=1, source_target_pairs={{0,2},{1,3},{2,0},{3,1},{4,6},{5,7},{6,4},{7,5},{8,10},{9,11},{10,... | collective-permute-start | bytes 110600 | tf_op jit(solution)/shard_map/ppermute | solution.py:586
  20.0 2.4 %collective-permute-done = bf16[1,16,1152]{2,1,0:T(8,128)(2,1)S(1)} collective-permute-done((bf16[1,16,1152]{2,1,0:T(8,128)(2,1)S(1)}, bf16[1,16,1152]{2,1,0:T(8,128)(2,1)S(1)}, u32[]{:S(2)}, u32[]{:S(2)}) %collective-permute-start) | collective-permute-done | bytes 36896 | tf_op jit(solution)/shard_map/ppermute | solution.py:586
  22.3 3.2 %collective-permute-start.1 = (bf16[2,16,1152]{2,1,0:T(8,128)(2,1)S(1)}, bf16[2,16,1152]{2,1,0:T(8,128)(2,1)S(1)}, u32[]{:S(2)}, u32[]{:S(2)}) collective-permute-start(bf16[2,16,1152]{2,1,0:T(8,128)(2,1)S(1)} %get-tuple-element.23), channel_id=1, source_target_pairs={{0,4},{1,5},{2,6},{3,7},{4,0},{5,1},{6,2},{7,3},{8,12},{9,13},{10,... | collective-permute-start | bytes 221192 | tf_op jit(solution)/shard_map/ppermute | solution.py:586
  25.5 4.8 %collective-permute-done.1 = bf16[2,16,1152]{2,1,0:T(8,128)(2,1)S(1)} collective-permute-done((bf16[2,16,1152]{2,1,0:T(8,128)(2,1)S(1)}, bf16[2,16,1152]{2,1,0:T(8,128)(2,1)S(1)}, u32[]{:S(2)}, u32[]{:S(2)}) %collective-permute-start.1) | collective-permute-done | bytes 73760 | tf_op jit(solution)/shard_map/ppermute | solution.py:586
  30.4 3.6 %all-to-all-done = bf16[16,64,512]{2,1,0:T(8,128)(2,1)S(1)} async-done(((bf16[16,64,512]{2,1,0:T(8,128)(2,1)}), bf16[16,64,512]{2,1,0:T(8,128)(2,1)S(1)}, u32[]{:S(2)}, u32[]{:S(2)}) %all-to-all-start) | async-done | bytes 1048608 | tf_op jit(solution)/shard_map/all_to_all | solution.py:593
  34.0 0.2 collective-permute-start.6
  34.2 4.5 %collective-permute-start.3 = (bf16[2,16,1152]{2,1,0:T(8,128)(2,1)S(1)}, bf16[2,16,1152]{2,1,0:T(8,128)(2,1)S(1)}, u32[]{:S(2)}, u32[]{:S(2)}) collective-permute-start(bf16[2,16,1152]{2,1,0:T(8,128)(2,1)S(1)} %get-tuple-element.23), channel_id=1, source_target_pairs={{0,8},{1,9},{2,10},{3,11},{4,12},{5,13},{6,14},{7,15},{8,0},{9,1},... | collective-permute-start | bytes 221192 | tf_op jit(solution)/shard_map/ppermute | solution.py:586
  38.7 1.2 %collective-permute-start.4 = (bf16[2,16,1152]{2,1,0:T(8,128)(2,1)S(1)}, bf16[2,16,1152]{2,1,0:T(8,128)(2,1)S(1)}, u32[]{:S(2)}, u32[]{:S(2)}) collective-permute-start(bf16[2,16,1152]{2,1,0:T(8,128)(2,1)S(1)} %get-tuple-element.23), channel_id=1, source_target_pairs={{0,12},{1,13},{2,14},{3,15},{4,8},{5,9},{6,10},{7,11},{8,4},{9,5},... | collective-permute-start | bytes 221192 | tf_op jit(solution)/shard_map/ppermute | solution.py:586
  40.0 0.7 collective-permute-start.7
  40.8 2.7 %collective-permute-done.3 = bf16[2,16,1152]{2,1,0:T(8,128)(2,1)S(1)} collective-permute-done((bf16[2,16,1152]{2,1,0:T(8,128)(2,1)S(1)}, bf16[2,16,1152]{2,1,0:T(8,128)(2,1)S(1)}, u32[]{:S(2)}, u32[]{:S(2)}) %collective-permute-start.3) | collective-permute-done | bytes 73760 | tf_op jit(solution)/shard_map/ppermute | solution.py:586
  43.5 1.6 %collective-permute-done.4 = bf16[2,16,1152]{2,1,0:T(8,128)(2,1)S(1)} collective-permute-done((bf16[2,16,1152]{2,1,0:T(8,128)(2,1)S(1)}, bf16[2,16,1152]{2,1,0:T(8,128)(2,1)S(1)}, u32[]{:S(2)}, u32[]{:S(2)}) %collective-permute-start.4) | collective-permute-done | bytes 73760 | tf_op jit(solution)/shard_map/ppermute | solution.py:586
  45.2 0.9 collective-permute-start.2
  46.0 0.7 collective-permute-done.5.refs_1_
  46.7 10.5 %shard_map.93 = (f32[2,1024,256]{2,1,0:T(8,128)S(1)}, f32[2,1024,256]{2,1,0:T(8,128)S(1)}, bf16[16,32,512]{2,1,0:T(8,128)(2,1)S(1)}, f32[16,8,512]{2,1,0:T(8,128)S(1)}, f32[8,256]{1,0:T(8,128)S(1)}) custom-call(s32[1]{0:T(128)} %bitcast.pos_ref, s32[16]{0:T(128)S(1)} %copy-done.8, s32[16]{0:T(128)S(1)} %copy-done.5, ...), custom_call_target="tpu_custom_call" | custom-call | flops 1 | bytes 1 | tf_op jit(solution)/shard_map/pallas_call | solution.py:380
  57.2 4.3 %shard_map.94 = (f32[2,768,256]{2,1,0:T(8,128)S(1)}, f32[8,256]{1,0:T(8,128)S(1)}) custom-call(s32[1]{0:T(128)} %bitcast.pos_ref, s32[16]{0:T(128)S(1)} %copy-done.5, bf16[768,512]{1,0:T(8,128)(2,1)S(1)} %collective-permute-done.7.outer_any, bf16[16,32,512]{2,1,0:T(8,128)(2,1)S(1)} %get-tuple-element.27.state_ref, ...), custom_call_target="tpu_custom_call" | custom-call | flops 1 | bytes 1 | tf_op jit(solution)/shard_map/pallas_call | solution.py:468
  61.5 2.3 %shard_map.95 = (f32[2,256,256]{2,1,0:T(8,128)S(1)}, f32[16,8,256]{2,1,0:T(8,128)S(1)}) custom-call(s32[1]{0:T(128)} %bitcast.pos_ref, s32[16]{0:T(128)S(1)} %copy-done.5, bf16[256,512]{1,0:T(8,128)(2,1)S(1)} %collective-permute-done.2.outer_any, bf16[16,32,512]{2,1,0:T(8,128)(2,1)S(1)} %get-tuple-element.27.state_ref, ...), custom_call_target="tpu_custom_call" | custom-call | flops 1 | bytes 1 | tf_op jit(solution)/shard_map/pallas_call | solution.py:468
  63.9 18.6 %all_to_all.10.stat_ref = f32[16,8,256]{2,1,0:T(8,128)S(1)} all-to-all(f32[16,8,256]{2,1,0:T(8,128)S(1)} %get-tuple-element.33), channel_id=1, replica_groups=mesh['clip'=2,'tm'=16] {'tm'}, dimensions={0} | all-to-all | bytes 262144 | tf_op jit(solution)/shard_map/all_to_all | solution.py:628
  82.4 3.7 %shard_map.96 = bf16[16,2,128,256]{3,2,1,0:T(8,128)(2,1)} custom-call(s32[1]{0:T(128)} %bitcast.pos_ref, s32[16]{0:T(128)S(1)} %copy-done.5, f32[16,8,256]{2,1,0:T(8,128)S(1)} %all_to_all.10.stat_ref, f32[1,256]{1,0:T(1,128)S(1)} %bitcast.11, f32[1,256]{1,0:T(1,128)S(1)} %bitcast.12, f32[2,1024,256]{2,1,0:T(8,128)S(1)} %get-tuple-element.34.near_ref, ...), custom_call_target="tpu_custom_call" | custom-call | flops 8388608 | bytes 6291456 | tf_op jit(solution)/shard_map/pallas_call | solution.py:549
  (27 shorter events, 0.2 us)
Async XLA Ops:
  3.3 30.7 %all-to-all-start = ((bf16[16,64,512]{2,1,0:T(8,128)(2,1)}), bf16[16,64,512]{2,1,0:T(8,128)(2,1)S(1)}, u32[]{:S(2)}, u32[]{:S(2)}) async-start(bf16[16,64,512]{2,1,0:T(8,128)(2,1)} %bitcast.15), calls=%async_computation | async-start | bytes 2097152 | tf_op jit(solution)/shard_map/all_to_all | solution.py:593
  10.7 1.2 %copy-start.4 = (bf16[1024,512]{1,0:T(8,128)(2,1)S(1)}, bf16[1024,512]{1,0:T(8,128)(2,1)}, u32[]{:S(2)}) copy-start(bf16[1024,512]{1,0:T(8,128)(2,1)} %tok_ref.1) | copy-start | bytes 3145732
  15.9 1.0 %copy-start = (bf16[1024,512]{1,0:T(8,128)(2,1)}, bf16[1024,512]{1,0:T(8,128)(2,1)S(1)}, u32[]{:S(2)}) copy-start(bf16[1024,512]{1,0:T(8,128)(2,1)S(1)} %get-tuple-element.31.wx_ref) | copy-start | bytes 3145732
  16.9 1.1 %copy-start.2 = (bf16[1536,512]{1,0:T(8,128)(2,1)}, bf16[1536,512]{1,0:T(8,128)(2,1)S(1)}, u32[]{:S(2)}) copy-start(bf16[1536,512]{1,0:T(8,128)(2,1)S(1)} %get-tuple-element.26.refs_6_) | copy-start | bytes 4718596
  18.0 28.7 %copy-start.5 = (s32[16]{0:T(128)S(1)}, s32[16]{0:T(128)}, u32[]{:S(2)}) copy-start(s32[16]{0:T(128)} %valid_ref.7) | copy-start | bytes 196
  18.0 28.7 %copy-start.8 = (s32[16]{0:T(128)S(1)}, s32[16]{0:T(128)}, u32[]{:S(2)}) copy-start(s32[16]{0:T(128)} %group_ref.1) | copy-start | bytes 196
  18.0 4.3 %collective-permute-start = (bf16[1,16,1152]{2,1,0:T(8,128)(2,1)S(1)}, bf16[1,16,1152]{2,1,0:T(8,128)(2,1)S(1)}, u32[]{:S(2)}, u32[]{:S(2)}) collective-permute-start(bf16[1,16,1152]{2,1,0:T(8,128)(2,1)S(1)} %get-tuple-element.21), channel_id=1, source_target_pairs={{0,2},{1,3},{2,0},{3,1},{4,6},{5,7},{6,4},{7,5},{8,10},{9,11},{10,... | collective-permute-start | bytes 110600 | tf_op jit(solution)/shard_map/ppermute | solution.py:586
  22.3 8.0 %collective-permute-start.1 = (bf16[2,16,1152]{2,1,0:T(8,128)(2,1)S(1)}, bf16[2,16,1152]{2,1,0:T(8,128)(2,1)S(1)}, u32[]{:S(2)}, u32[]{:S(2)}) collective-permute-start(bf16[2,16,1152]{2,1,0:T(8,128)(2,1)S(1)} %get-tuple-element.23), channel_id=1, source_target_pairs={{0,4},{1,5},{2,6},{3,7},{4,0},{5,1},{6,2},{7,3},{8,12},{9,13},{10,... | collective-permute-start | bytes 221192 | tf_op jit(solution)/shard_map/ppermute | solution.py:586
  34.0 12.7 %copy-start.3 = (bf16[1536,512]{1,0:T(8,128)(2,1)S(1)}, bf16[1536,512]{1,0:T(8,128)(2,1)}, u32[]{:S(2)}) copy-start(bf16[1536,512]{1,0:T(8,128)(2,1)} %copy-done.2) | copy-start | bytes 4718596
  34.0 12.7 %collective-permute-start.6 = (bf16[1024,512]{1,0:T(8,128)(2,1)S(1)}, bf16[1024,512]{1,0:T(8,128)(2,1)S(1)}, u32[]{:S(2)}, u32[]{:S(2)}) collective-permute-start(bf16[1024,512]{1,0:T(8,128)(2,1)S(1)} %bitcast.7), channel_id=1, source_target_pairs={{0,1},{1,0},{2,3},{3,2},{4,5},{5,4},{6,7},{7,6},{8,9},{9,8},{10,11... | collective-permute-start | bytes 3145736 | tf_op jit(solution)/shard_map/ppermute | solution.py:586
  34.2 9.2 %collective-permute-start.3 = (bf16[2,16,1152]{2,1,0:T(8,128)(2,1)S(1)}, bf16[2,16,1152]{2,1,0:T(8,128)(2,1)S(1)}, u32[]{:S(2)}, u32[]{:S(2)}) collective-permute-start(bf16[2,16,1152]{2,1,0:T(8,128)(2,1)S(1)} %get-tuple-element.23), channel_id=1, source_target_pairs={{0,8},{1,9},{2,10},{3,11},{4,12},{5,13},{6,14},{7,15},{8,0},{9,1},... | collective-permute-start | bytes 221192 | tf_op jit(solution)/shard_map/ppermute | solution.py:586
  38.7 6.3 %collective-permute-start.4 = (bf16[2,16,1152]{2,1,0:T(8,128)(2,1)S(1)}, bf16[2,16,1152]{2,1,0:T(8,128)(2,1)S(1)}, u32[]{:S(2)}, u32[]{:S(2)}) collective-permute-start(bf16[2,16,1152]{2,1,0:T(8,128)(2,1)S(1)} %get-tuple-element.23), channel_id=1, source_target_pairs={{0,12},{1,13},{2,14},{3,15},{4,8},{5,9},{6,10},{7,11},{8,4},{9,5},... | collective-permute-start | bytes 221192 | tf_op jit(solution)/shard_map/ppermute | solution.py:586
  40.0 17.2 %collective-permute-start.7 = (bf16[768,512]{1,0:T(8,128)(2,1)S(1)}, bf16[768,512]{1,0:T(8,128)(2,1)S(1)}, u32[]{:S(2)}, u32[]{:S(2)}) collective-permute-start(bf16[768,512]{1,0:T(8,128)(2,1)S(1)} %slice.7), channel_id=1, source_target_pairs={{1,2},{3,4},{5,6},{7,8},{9,10},{11,12},{13,14},{2,1},{4,3},{6,5},{... | collective-permute-start | bytes 2359304 | tf_op jit(solution)/shard_map/ppermute | solution.py:586
  45.0 1.6 %collective-permute-start.5 = (bf16[8,16,1152]{2,1,0:T(8,128)(2,1)S(1)}, bf16[8,16,1152]{2,1,0:T(8,128)(2,1)S(1)}, u32[]{:S(2)}, u32[]{:S(2)}) collective-permute-start(bf16[8,16,1152]{2,1,0:T(8,128)(2,1)S(1)} %constant_dynamic-update-slice_fusion.2.refs_0_), channel_id=1, source_target_pairs={{0,1},{1,0},{2,3},{3,2},{4,5},{5,4},{6,7},{7,6},{8,9},{9,8},{10,11... | collective-permute-start | bytes 884744 | tf_op jit(solution)/shard_map/ppermute | solution.py:586
  45.2 16.4 %collective-permute-start.2 = (bf16[256,512]{1,0:T(8,128)(2,1)S(1)}, bf16[256,512]{1,0:T(8,128)(2,1)S(1)}, u32[]{:S(2)}, u32[]{:S(2)}) collective-permute-start(bf16[256,512]{1,0:T(8,128)(2,1)S(1)} %slice.6), channel_id=1, source_target_pairs={{1,2},{3,4},{5,6},{7,8},{9,10},{11,12},{13,14},{2,1},{4,3},{6,5},{... | collective-permute-start | bytes 786440 | tf_op jit(solution)/shard_map/ppermute | solution.py:586
  46.7 10.5 %copy-start.1 = (bf16[1024,512]{1,0:T(8,128)(2,1)S(1)}, bf16[1024,512]{1,0:T(8,128)(2,1)}, u32[]{:S(2)}) copy-start(bf16[1024,512]{1,0:T(8,128)(2,1)} %copy-done) | copy-start | bytes 3145732
  61.5 20.9 %copy-start.6 = (f32[256]{0:T(256)S(1)}, f32[256]{0:T(256)}, u32[]{:S(2)}) copy-start(f32[256]{0:T(256)} %param.13) | copy-start | bytes 3076
  61.5 20.9 %copy-start.7 = (f32[256]{0:T(256)S(1)}, f32[256]{0:T(256)}, u32[]{:S(2)}) copy-start(f32[256]{0:T(256)} %param.14) | copy-start | bytes 3076

commit v7 on v6

--- a/solution.py
+++ b/solution.py
@@ -601,9 +601,7 @@
     k, gate = 2, None
     while k < tiles:
         ks = [k] if k == 2 or 2 * k >= tiles else [k, 2 * k, 3 * k]
-        got = [swap_by(buf, ks[0])]
-        late, _ = lax.optimization_barrier((buf, got[0]))
-        got += [swap_by(late, j) for j in ks[1:]]
+        got = [swap_by(buf, j) for j in ks]
         gate = got[0]
         buf = jnp.concatenate([buf] + got, axis=0)
         k *= 2 if len(ks) == 1 else 4

time: 86.6 us -> 86.6 us (level)
  no operation moved by 1% of the time
where the time goes in v7:
time: 86.6 us; the launch traced here: 86.3 us
  Pallas kernels  28 us (32%)
  starting transfers between devices  20.1 us (23%)
  blocking collectives  18.6 us (21%)
  waiting for transfers between devices  15.8 us (18%)
  local copies, waits for them, and re-layouts  3.49 us (4%)
    all_to_all x1, blocking collectives, local(): stat = lax.all_to_all(stat, 'tm', split_axis=0, concat_axis=0, tiled=True)  18.6 us
    ppermute x8, starting transfers between devices, swap(): return lax.ppermute(x, 'tm', pairs)  12.7 us
    ppermute x8, waiting for transfers between devices, swap(): return lax.ppermute(x, 'tm', pairs)  12.1 us
    pallas_call x1, Pallas kernels, near(): pl.pallas_call(functools.partial(near_kernel, rows, parts, frames), grid_...  10.5 us
    all_to_all x1, starting transfers between devices, local(): lax.all_to_all(raster.reshape(tiles, rows, width), 'tm', split_axis=0, co...  7.4 us
    pallas_call x2, Pallas kernels, far(): pl.pallas_call(functools.partial(far_kernel, rows, first, last), in_specs...  6.57 us
    pallas_call x1, Pallas kernels, run_state(): pl.pallas_call(functools.partial(state_kernel, head), grid=(steps,), in_s...  3.98 us
    pallas_call x1, Pallas kernels, norm(): pl.pallas_call(functools.partial(norm_kernel, rows, channels // NORM_GROU...  3.66 us
  transfers between devices with their start and end apart: 9, of which 6 were waited for; matrix products, arithmetic and copies ran while one was open for 0% of the time, Pallas kernels for 22%

profile of v7, /device:TPU:0, one launch (start us, length us, event | category | flops | bytes accessed | tf_op | source)
XLA Modules:
  0.0 86.3 jit_solution(521976620886433149)
XLA Ops:
  0.0 3.3 %shard_map.91 = bf16[1024,512]{1,0:T(8,128)(2,1)} custom-call(s32[1,1024]{1,0:T(1,128)} %bitcast.16, bf16[1024,512]{1,0:T(8,128)(2,1)} %tok_ref.1), custom_call_target="tpu_custom_call" | custom-call | flops 1073741824 | bytes 2097152 | tf_op jit(solution)/shard_map/pallas_call | solution.py:68
  3.3 7.4 %all-to-all-start = ((bf16[16,64,512]{2,1,0:T(8,128)(2,1)}), bf16[16,64,512]{2,1,0:T(8,128)(2,1)S(1)}, u32[]{:S(2)}, u32[]{:S(2)}) async-start(bf16[16,64,512]{2,1,0:T(8,128)(2,1)} %bitcast.15), calls=%async_computation | async-start | bytes 2097152 | tf_op jit(solution)/shard_map/all_to_all | solution.py:593
  10.7 1.2 %copy-done.4 = bf16[1024,512]{1,0:T(8,128)(2,1)S(1)} copy-done((bf16[1024,512]{1,0:T(8,128)(2,1)S(1)}, bf16[1024,512]{1,0:T(8,128)(2,1)}, u32[]{:S(2)}) %copy-start.4) | copy-done | bytes 1048600
  11.9 4.0 %shard_map.92 = (bf16[1,16,1152]{2,1,0:T(8,128)(2,1)S(1)}, bf16[512,512]{1,0:T(8,128)(2,1)S(1)}, bf16[512,1024]{1,0:T(8,128)(2,1)S(1)}, bf16[1536,512]{1,0:T(8,128)(2,1)S(1)}, bf16[1024,512]{1,0:T(8,128)(2,1)S(1)}) custom-call(s32[1]{0:T(128)} %bitcast.pos_ref, bf16[1024,512]{1,0:T(8,128)(2,1)S(1)} %copy-done.4, bf16[512,1536]{1,0:T(8,128)(2,1)} %qkv_hbm.1, ...), custom_call_target="tpu_custom_call" | custom-call | flops 1073741824 | bytes 4194304 | tf_op jit(solution)/shard_map/pallas_call | solution.py:185
  15.9 1.0 %copy-done = bf16[1024,512]{1,0:T(8,128)(2,1)} copy-done((bf16[1024,512]{1,0:T(8,128)(2,1)}, bf16[1024,512]{1,0:T(8,128)(2,1)S(1)}, u32[]{:S(2)}) %copy-start) | copy-done | bytes 1048600
  16.9 1.1 %copy-done.2 = bf16[1536,512]{1,0:T(8,128)(2,1)} copy-done((bf16[1536,512]{1,0:T(8,128)(2,1)}, bf16[1536,512]{1,0:T(8,128)(2,1)S(1)}, u32[]{:S(2)}) %copy-start.2) | copy-done | bytes 1572888
  18.0 1.9 %collective-permute-start = (bf16[1,16,1152]{2,1,0:T(8,128)(2,1)S(1)}, bf16[1,16,1152]{2,1,0:T(8,128)(2,1)S(1)}, u32[]{:S(2)}, u32[]{:S(2)}) collective-permute-start(bf16[1,16,1152]{2,1,0:T(8,128)(2,1)S(1)} %get-tuple-element.20), channel_id=1, source_target_pairs={{0,2},{1,3},{2,0},{3,1},{4,6},{5,7},{6,4},{7,5},{8,10},{9,11},{10,... | collective-permute-start | bytes 110600 | tf_op jit(solution)/shard_map/ppermute | solution.py:586
  20.0 2.4 %collective-permute-done = bf16[1,16,1152]{2,1,0:T(8,128)(2,1)S(1)} collective-permute-done((bf16[1,16,1152]{2,1,0:T(8,128)(2,1)S(1)}, bf16[1,16,1152]{2,1,0:T(8,128)(2,1)S(1)}, u32[]{:S(2)}, u32[]{:S(2)}) %collective-permute-start) | collective-permute-done | bytes 36896 | tf_op jit(solution)/shard_map/ppermute | solution.py:586
  22.3 3.2 %collective-permute-start.1 = (bf16[2,16,1152]{2,1,0:T(8,128)(2,1)S(1)}, bf16[2,16,1152]{2,1,0:T(8,128)(2,1)S(1)}, u32[]{:S(2)}, u32[]{:S(2)}) collective-permute-start(bf16[2,16,1152]{2,1,0:T(8,128)(2,1)S(1)} %get-tuple-element.36), channel_id=1, source_target_pairs={{0,4},{1,5},{2,6},{3,7},{4,0},{5,1},{6,2},{7,3},{8,12},{9,13},{10,... | collective-permute-start | bytes 221192 | tf_op jit(solution)/shard_map/ppermute | solution.py:586
  25.5 4.8 %collective-permute-done.1 = bf16[2,16,1152]{2,1,0:T(8,128)(2,1)S(1)} collective-permute-done((bf16[2,16,1152]{2,1,0:T(8,128)(2,1)S(1)}, bf16[2,16,1152]{2,1,0:T(8,128)(2,1)S(1)}, u32[]{:S(2)}, u32[]{:S(2)}) %collective-permute-start.1) | collective-permute-done | bytes 73760 | tf_op jit(solution)/shard_map/ppermute | solution.py:586
  30.4 3.6 %all-to-all-done = bf16[16,64,512]{2,1,0:T(8,128)(2,1)S(1)} async-done(((bf16[16,64,512]{2,1,0:T(8,128)(2,1)}), bf16[16,64,512]{2,1,0:T(8,128)(2,1)S(1)}, u32[]{:S(2)}, u32[]{:S(2)}) %all-to-all-start) | async-done | bytes 1048608 | tf_op jit(solution)/shard_map/all_to_all | solution.py:593
  34.0 0.2 collective-permute-start.6
  34.2 4.5 %collective-permute-start.3 = (bf16[2,16,1152]{2,1,0:T(8,128)(2,1)S(1)}, bf16[2,16,1152]{2,1,0:T(8,128)(2,1)S(1)}, u32[]{:S(2)}, u32[]{:S(2)}) collective-permute-start(bf16[2,16,1152]{2,1,0:T(8,128)(2,1)S(1)} %get-tuple-element.36), channel_id=1, source_target_pairs={{0,8},{1,9},{2,10},{3,11},{4,12},{5,13},{6,14},{7,15},{8,0},{9,1},... | collective-permute-start | bytes 221192 | tf_op jit(solution)/shard_map/ppermute | solution.py:586
  38.7 1.2 %collective-permute-start.4 = (bf16[2,16,1152]{2,1,0:T(8,128)(2,1)S(1)}, bf16[2,16,1152]{2,1,0:T(8,128)(2,1)S(1)}, u32[]{:S(2)}, u32[]{:S(2)}) collective-permute-start(bf16[2,16,1152]{2,1,0:T(8,128)(2,1)S(1)} %get-tuple-element.36), channel_id=1, source_target_pairs={{0,12},{1,13},{2,14},{3,15},{4,8},{5,9},{6,10},{7,11},{8,4},{9,5},... | collective-permute-start | bytes 221192 | tf_op jit(solution)/shard_map/ppermute | solution.py:586
  40.0 0.7 collective-permute-start.7
  40.8 2.7 %collective-permute-done.3 = bf16[2,16,1152]{2,1,0:T(8,128)(2,1)S(1)} collective-permute-done((bf16[2,16,1152]{2,1,0:T(8,128)(2,1)S(1)}, bf16[2,16,1152]{2,1,0:T(8,128)(2,1)S(1)}, u32[]{:S(2)}, u32[]{:S(2)}) %collective-permute-start.3) | collective-permute-done | bytes 73760 | tf_op jit(solution)/shard_map/ppermute | solution.py:586
  43.5 1.6 %collective-permute-done.4 = bf16[2,16,1152]{2,1,0:T(8,128)(2,1)S(1)} collective-permute-done((bf16[2,16,1152]{2,1,0:T(8,128)(2,1)S(1)}, bf16[2,16,1152]{2,1,0:T(8,128)(2,1)S(1)}, u32[]{:S(2)}, u32[]{:S(2)}) %collective-permute-start.4) | collective-permute-done | bytes 73760 | tf_op jit(solution)/shard_map/ppermute | solution.py:586
  45.2 0.9 collective-permute-start.2
  46.0 0.7 collective-permute-done.5.refs_1_
  46.7 10.5 %shard_map.93 = (f32[2,1024,256]{2,1,0:T(8,128)S(1)}, f32[2,1024,256]{2,1,0:T(8,128)S(1)}, bf16[16,32,512]{2,1,0:T(8,128)(2,1)S(1)}, f32[16,8,512]{2,1,0:T(8,128)S(1)}, f32[8,256]{1,0:T(8,128)S(1)}) custom-call(s32[1]{0:T(128)} %bitcast.pos_ref, s32[16]{0:T(128)S(1)} %copy-done.8, s32[16]{0:T(128)S(1)} %copy-done.5, ...), custom_call_target="tpu_custom_call" | custom-call | flops 1 | bytes 1 | tf_op jit(solution)/shard_map/pallas_call | solution.py:380
  57.2 4.3 %shard_map.94 = (f32[2,768,256]{2,1,0:T(8,128)S(1)}, f32[8,256]{1,0:T(8,128)S(1)}) custom-call(s32[1]{0:T(128)} %bitcast.pos_ref, s32[16]{0:T(128)S(1)} %copy-done.5, bf16[768,512]{1,0:T(8,128)(2,1)S(1)} %collective-permute-done.7.outer_any, bf16[16,32,512]{2,1,0:T(8,128)(2,1)S(1)} %get-tuple-element.25.state_ref, ...), custom_call_target="tpu_custom_call" | custom-call | flops 1 | bytes 1 | tf_op jit(solution)/shard_map/pallas_call | solution.py:468
  61.5 2.3 %shard_map.95 = (f32[2,256,256]{2,1,0:T(8,128)S(1)}, f32[16,8,256]{2,1,0:T(8,128)S(1)}) custom-call(s32[1]{0:T(128)} %bitcast.pos_ref, s32[16]{0:T(128)S(1)} %copy-done.5, bf16[256,512]{1,0:T(8,128)(2,1)S(1)} %collective-permute-done.2.outer_any, bf16[16,32,512]{2,1,0:T(8,128)(2,1)S(1)} %get-tuple-element.25.state_ref, ...), custom_call_target="tpu_custom_call" | custom-call | flops 1 | bytes 1 | tf_op jit(solution)/shard_map/pallas_call | solution.py:468
  63.9 18.6 %all_to_all.10.stat_ref = f32[16,8,256]{2,1,0:T(8,128)S(1)} all-to-all(f32[16,8,256]{2,1,0:T(8,128)S(1)} %get-tuple-element.31), channel_id=1, replica_groups=mesh['clip'=2,'tm'=16] {'tm'}, dimensions={0} | all-to-all | bytes 262144 | tf_op jit(solution)/shard_map/all_to_all | solution.py:626
  82.4 3.7 %shard_map.96 = bf16[16,2,128,256]{3,2,1,0:T(8,128)(2,1)} custom-call(s32[1]{0:T(128)} %bitcast.pos_ref, s32[16]{0:T(128)S(1)} %copy-done.5, f32[16,8,256]{2,1,0:T(8,128)S(1)} %all_to_all.10.stat_ref, f32[1,256]{1,0:T(1,128)S(1)} %bitcast.11, f32[1,256]{1,0:T(1,128)S(1)} %bitcast.12, f32[2,1024,256]{2,1,0:T(8,128)S(1)} %get-tuple-element.32.near_ref, ...), custom_call_target="tpu_custom_call" | custom-call | flops 8388608 | bytes 6291456 | tf_op jit(solution)/shard_map/pallas_call | solution.py:549
  (27 shorter events, 0.2 us)
Async XLA Ops:
  3.3 30.7 %all-to-all-start = ((bf16[16,64,512]{2,1,0:T(8,128)(2,1)}), bf16[16,64,512]{2,1,0:T(8,128)(2,1)S(1)}, u32[]{:S(2)}, u32[]{:S(2)}) async-start(bf16[16,64,512]{2,1,0:T(8,128)(2,1)} %bitcast.15), calls=%async_computation | async-start | bytes 2097152 | tf_op jit(solution)/shard_map/all_to_all | solution.py:593
  10.7 1.2 %copy-start.4 = (bf16[1024,512]{1,0:T(8,128)(2,1)S(1)}, bf16[1024,512]{1,0:T(8,128)(2,1)}, u32[]{:S(2)}) copy-start(bf16[1024,512]{1,0:T(8,128)(2,1)} %tok_ref.1) | copy-start | bytes 3145732
  15.9 1.0 %copy-start = (bf16[1024,512]{1,0:T(8,128)(2,1)}, bf16[1024,512]{1,0:T(8,128)(2,1)S(1)}, u32[]{:S(2)}) copy-start(bf16[1024,512]{1,0:T(8,128)(2,1)S(1)} %get-tuple-element.29.wx_ref) | copy-start | bytes 3145732
  16.9 1.1 %copy-start.2 = (bf16[1536,512]{1,0:T(8,128)(2,1)}, bf16[1536,512]{1,0:T(8,128)(2,1)S(1)}, u32[]{:S(2)}) copy-start(bf16[1536,512]{1,0:T(8,128)(2,1)S(1)} %get-tuple-element.24.refs_6_) | copy-start | bytes 4718596
  18.0 28.7 %copy-start.5 = (s32[16]{0:T(128)S(1)}, s32[16]{0:T(128)}, u32[]{:S(2)}) copy-start(s32[16]{0:T(128)} %valid_ref.7) | copy-start | bytes 196
  18.0 28.7 %copy-start.8 = (s32[16]{0:T(128)S(1)}, s32[16]{0:T(128)}, u32[]{:S(2)}) copy-start(s32[16]{0:T(128)} %group_ref.1) | copy-start | bytes 196
  18.0 4.3 %collective-permute-start = (bf16[1,16,1152]{2,1,0:T(8,128)(2,1)S(1)}, bf16[1,16,1152]{2,1,0:T(8,128)(2,1)S(1)}, u32[]{:S(2)}, u32[]{:S(2)}) collective-permute-start(bf16[1,16,1152]{2,1,0:T(8,128)(2,1)S(1)} %get-tuple-element.20), channel_id=1, source_target_pairs={{0,2},{1,3},{2,0},{3,1},{4,6},{5,7},{6,4},{7,5},{8,10},{9,11},{10,... | collective-permute-start | bytes 110600 | tf_op jit(solution)/shard_map/ppermute | solution.py:586
  22.3 8.0 %collective-permute-start.1 = (bf16[2,16,1152]{2,1,0:T(8,128)(2,1)S(1)}, bf16[2,16,1152]{2,1,0:T(8,128)(2,1)S(1)}, u32[]{:S(2)}, u32[]{:S(2)}) collective-permute-start(bf16[2,16,1152]{2,1,0:T(8,128)(2,1)S(1)} %get-tuple-element.36), channel_id=1, source_target_pairs={{0,4},{1,5},{2,6},{3,7},{4,0},{5,1},{6,2},{7,3},{8,12},{9,13},{10,... | collective-permute-start | bytes 221192 | tf_op jit(solution)/shard_map/ppermute | solution.py:586
  34.0 12.7 %copy-start.3 = (bf16[1536,512]{1,0:T(8,128)(2,1)S(1)}, bf16[1536,512]{1,0:T(8,128)(2,1)}, u32[]{:S(2)}) copy-start(bf16[1536,512]{1,0:T(8,128)(2,1)} %copy-done.2) | copy-start | bytes 4718596
  34.0 12.7 %collective-permute-start.6 = (bf16[1024,512]{1,0:T(8,128)(2,1)S(1)}, bf16[1024,512]{1,0:T(8,128)(2,1)S(1)}, u32[]{:S(2)}, u32[]{:S(2)}) collective-permute-start(bf16[1024,512]{1,0:T(8,128)(2,1)S(1)} %bitcast.7), channel_id=1, source_target_pairs={{0,1},{1,0},{2,3},{3,2},{4,5},{5,4},{6,7},{7,6},{8,9},{9,8},{10,11... | collective-permute-start | bytes 3145736 | tf_op jit(solution)/shard_map/ppermute | solution.py:586
  34.2 9.2 %collective-permute-start.3 = (bf16[2,16,1152]{2,1,0:T(8,128)(2,1)S(1)}, bf16[2,16,1152]{2,1,0:T(8,128)(2,1)S(1)}, u32[]{:S(2)}, u32[]{:S(2)}) collective-permute-start(bf16[2,16,1152]{2,1,0:T(8,128)(2,1)S(1)} %get-tuple-element.36), channel_id=1, source_target_pairs={{0,8},{1,9},{2,10},{3,11},{4,12},{5,13},{6,14},{7,15},{8,0},{9,1},... | collective-permute-start | bytes 221192 | tf_op jit(solution)/shard_map/ppermute | solution.py:586
  38.7 6.3 %collective-permute-start.4 = (bf16[2,16,1152]{2,1,0:T(8,128)(2,1)S(1)}, bf16[2,16,1152]{2,1,0:T(8,128)(2,1)S(1)}, u32[]{:S(2)}, u32[]{:S(2)}) collective-permute-start(bf16[2,16,1152]{2,1,0:T(8,128)(2,1)S(1)} %get-tuple-element.36), channel_id=1, source_target_pairs={{0,12},{1,13},{2,14},{3,15},{4,8},{5,9},{6,10},{7,11},{8,4},{9,5},... | collective-permute-start | bytes 221192 | tf_op jit(solution)/shard_map/ppermute | solution.py:586
  40.0 17.2 %collective-permute-start.7 = (bf16[768,512]{1,0:T(8,128)(2,1)S(1)}, bf16[768,512]{1,0:T(8,128)(2,1)S(1)}, u32[]{:S(2)}, u32[]{:S(2)}) collective-permute-start(bf16[768,512]{1,0:T(8,128)(2,1)S(1)} %slice.7), channel_id=1, source_target_pairs={{1,2},{3,4},{5,6},{7,8},{9,10},{11,12},{13,14},{2,1},{4,3},{6,5},{... | collective-permute-start | bytes 2359304 | tf_op jit(solution)/shard_map/ppermute | solution.py:586
  45.0 1.6 %collective-permute-start.5 = (bf16[8,16,1152]{2,1,0:T(8,128)(2,1)S(1)}, bf16[8,16,1152]{2,1,0:T(8,128)(2,1)S(1)}, u32[]{:S(2)}, u32[]{:S(2)}) collective-permute-start(bf16[8,16,1152]{2,1,0:T(8,128)(2,1)S(1)} %constant_dynamic-update-slice_fusion.2.refs_0_), channel_id=1, source_target_pairs={{0,1},{1,0},{2,3},{3,2},{4,5},{5,4},{6,7},{7,6},{8,9},{9,8},{10,11... | collective-permute-start | bytes 884744 | tf_op jit(solution)/shard_map/ppermute | solution.py:586
  45.2 16.4 %collective-permute-start.2 = (bf16[256,512]{1,0:T(8,128)(2,1)S(1)}, bf16[256,512]{1,0:T(8,128)(2,1)S(1)}, u32[]{:S(2)}, u32[]{:S(2)}) collective-permute-start(bf16[256,512]{1,0:T(8,128)(2,1)S(1)} %slice.6), channel_id=1, source_target_pairs={{1,2},{3,4},{5,6},{7,8},{9,10},{11,12},{13,14},{2,1},{4,3},{6,5},{... | collective-permute-start | bytes 786440 | tf_op jit(solution)/shard_map/ppermute | solution.py:586
  46.7 10.5 %copy-start.1 = (bf16[1024,512]{1,0:T(8,128)(2,1)S(1)}, bf16[1024,512]{1,0:T(8,128)(2,1)}, u32[]{:S(2)}) copy-start(bf16[1024,512]{1,0:T(8,128)(2,1)} %copy-done) | copy-start | bytes 3145732
  61.5 20.9 %copy-start.6 = (f32[256]{0:T(256)S(1)}, f32[256]{0:T(256)}, u32[]{:S(2)}) copy-start(f32[256]{0:T(256)} %param.13) | copy-start | bytes 3076
  61.5 20.9 %copy-start.7 = (f32[256]{0:T(256)S(1)}, f32[256]{0:T(256)}, u32[]{:S(2)}) copy-start(f32[256]{0:T(256)} %param.14) | copy-start | bytes 3076
